TPU v7x, 32 devices: a whole 2x2x4 slice. The times are simulated.
32 devices in a mesh: tm: 4 (over y, x), cells: 8 (over z, core).
Axes of the slice: x: 2, y: 2, z: 4, core: 2. Of those that a mesh axis runs over, the one named last changes fastest.
Arguments:
- footprint: float32 [4, 4, 768, 8192], P('tm', None, None, 'cells'), may hold values from -0.03125 to 0.03125
- flux: float32 [4, 8192, 2048], P('tm', 'cells'), may hold values from -6 to 6
- obs_weight: float32 [4, 768], P('tm'), may hold values from 0.2 to 5
- obs_count: int32 [4], P('tm'), may hold values from 1 to 768, 2304 in all
Outputs:
- normal_image: float32 [4, 8192, 2048], P('tm', 'cells')
Inputs may be any that keep to these rules, and one draw needn't show every extreme that they name: `obs_count`: each block has at least one valid slot; one block has all 768 slots valid.
All inputs are finite; a program needn't handle non-finite values.
Results may differ from a plain program's by a relative error of at most 0.0001.
Values sent between devices are 32-bit elements; how exact they have to be, the bound alone decides.
No kernel may reach another device: no remote copies, remote signals or barrier semaphores. Data moves between devices by JAX's collectives and lax.ppermute only.
A program may use at most 128 MiB of HBM per device.

v0:
```python
import jax
import jax.numpy as jnp
from jax import lax
from jax.sharding import PartitionSpec as P


def from_behind(value, axis, by):
    devices = lax.axis_size(axis)
    pairs = [(i, i + by) for i in range(devices) if 0 <= i + by < devices]
    return lax.ppermute(value, axis, pairs)


def on_device(footprint, flux, obs_weight, obs_count):
    highest = lax.Precision.HIGHEST
    foot_slab = footprint[0]
    own_flux = flux[0]
    lag_count = foot_slab.shape[0]
    slot_count = foot_slab.shape[1]
    earlier = [own_flux]
    for lag_step in range(1, lag_count):
        earlier.append(from_behind(own_flux, "tm", lag_step))
    valid_rows = (jnp.arange(slot_count, dtype=jnp.int32) < obs_count[0]).astype(jnp.float32)
    row_scale = valid_rows * obs_weight[0]
    partial_value = jnp.dot(
        foot_slab[0], earlier[0], precision=highest, preferred_element_type=jnp.float32
    )
    for lag_step in range(1, lag_count):
        partial_value = partial_value + jnp.dot(
            foot_slab[lag_step],
            earlier[lag_step],
            precision=highest,
            preferred_element_type=jnp.float32,
        )
    modelled = lax.psum(partial_value, "cells")
    weighted = row_scale[:, None] * modelled
    adjoint_terms = []
    for lag_step in range(lag_count):
        adjoint_terms.append(
            lax.dot_general(
                foot_slab[lag_step],
                weighted,
                (((0,), (0,)), ((), ())),
                precision=highest,
                preferred_element_type=jnp.float32,
            )
        )
    accumulator = adjoint_terms[0]
    for lag_step in range(1, lag_count):
        accumulator = accumulator + from_behind(adjoint_terms[lag_step], "tm", -lag_step)
    return accumulator[None]


def solution(mesh):
    placed = (P("tm", None, None, "cells"), P("tm", "cells", None), P("tm", None), P("tm"))
    return jax.shard_map(
        on_device, mesh=mesh, in_specs=placed, out_specs=P("tm", "cells", None), check_vma=False
    )
```

profile of v0, /device:TPU:3, one launch (start us, length us, event | category | flops | bytes accessed | tf_op | source)
XLA Modules:
  0.0 1046.5 jit_solution(17648498848262174219)
XLA Ops:
  6.5 0.0 all-reduce.2.cloned.1.call-start
  6.5 3.7 collective-permute-start.1
  10.2 1.9 collective-permute-start
  12.1 1.2 collective-permute-start.2
  13.4 24.1 %fusion.30 = f32[768,2048]{1,0:T(8,128)S(1)} fusion(f32[1,4,768,1024]{3,2,1,0:T(8,128)} %param.4, f32[1,1024,2048]{2,1,0:T(8,128)} %param.5), kind=kOutput, calls=%fused_computation.26 | convolution fusion | flops 19327352832 | bytes 17825792 | tf_op jit(solution)/shard_map/dot_general | solution.py:24
  37.5 151.6 %collective-permute-done.1 = f32[1024,2048]{1,0:T(8,128)S(1)} collective-permute-done((f32[1024,2048]{1,0:T(8,128)}, f32[1024,2048]{1,0:T(8,128)S(1)}, u32[]{:S(2)}, u32[]{:S(2)}) %collective-permute-start.1) | collective-permute-done | bytes 8388640 | tf_op jit(solution)/shard_map/ppermute | solution.py:10
  189.1 32.3 %fusion.24 = f32[768,2048]{1,0:T(8,128)S(1)} fusion(f32[1024,2048]{1,0:T(8,128)S(1)} %collective-permute-done.1, f32[1,4,768,1024]{3,2,1,0:T(8,128)} %param.4), kind=kOutput, calls=%fused_computation.20 | convolution fusion | flops 19327352832 | bytes 17825792 | tf_op jit(solution)/shard_map/dot_general | solution.py:28
  221.4 0.0 collective-permute-done
  221.4 23.9 %fusion.27 = f32[768,2048]{1,0:T(8,128)S(1)} fusion(f32[1024,2048]{1,0:T(8,128)} %collective-permute-done, f32[1,4,768,1024]{3,2,1,0:T(8,128)} %param.4), kind=kOutput, calls=%fused_computation.23 | convolution fusion | flops 19327352832 | bytes 17825792 | tf_op jit(solution)/shard_map/dot_general | solution.py:28
  245.3 0.0 copy-start.1
  245.3 0.0 collective-permute-done.2
  245.3 25.0 %add_add_fusion = f32[768,2048]{1,0:T(8,128)} fusion(f32[768,2048]{1,0:T(8,128)S(1)} %fusion.24, f32[768,2048]{1,0:T(8,128)S(1)} %fusion.30, f32[768,2048]{1,0:T(8,128)S(1)} %fusion.27, f32[1024,2048]{1,0:T(8,128)S(1)} %collective-permute-done.2, f32[1,4,768,1024]{3,2,1,0:T(8,128)} %param.4), kind=kOutput, calls=%fused_computation.4 | convolution fusion | flops 19332071424 | bytes 36700160 | tf_op jit(solution)/shard_map/dot_general | solution.py:28
  270.3 0.0 all-reduce.2.cloned.1.call-update
  271.0 0.0 copy-done.1
  271.0 317.2 %all-reduce.2.cloned.1.call-done = f32[768,2048]{1,0:T(8,128)} async-done(((f32[768,2048]{1,0:T(8,128)}), f32[768,2048]{1,0:T(8,128)}) %all-reduce.2.cloned.1.call-update) | async-done | bytes 6291472 | tf_op jit(solution)/shard_map/psum | solution.py:34
  588.2 0.0 copy-start
  588.2 25.9 %fusion.17 = f32[1024,2048]{0,1:T(8,128)} fusion(f32[768,2048]{1,0:T(8,128)} %all-reduce.2.cloned.1.call-done, f32[768]{0:T(1024)S(1)} %fusion.50, f32[1,4,768,1024]{3,2,1,0:T(8,128)} %param.4), kind=kOutput, calls=%fused_computation.15 | convolution fusion | flops 19328925696 | bytes 17828864 | tf_op jit(solution)/shard_map/dot_general | solution.py:39
  614.1 1.2 collective-permute-start.5
  615.3 0.0 copy-done
  615.3 24.3 %fusion.14 = f32[1024,2048]{0,1:T(8,128)} fusion(f32[768,2048]{1,0:T(8,128)S(1)} %copy-done, f32[768]{0:T(1024)S(1)} %fusion.50, f32[1,4,768,1024]{3,2,1,0:T(8,128)} %param.4), kind=kOutput, calls=%fused_computation.14 | convolution fusion | flops 19328925696 | bytes 17828864 | tf_op jit(solution)/shard_map/dot_general | solution.py:39
  639.6 1.3 collective-permute-start.4
  640.9 24.2 %fusion.11 = f32[1024,2048]{0,1:T(8,128)} fusion(f32[768,2048]{1,0:T(8,128)S(1)} %copy-done, f32[768]{0:T(1024)S(1)} %fusion.50, f32[1,4,768,1024]{3,2,1,0:T(8,128)} %param.4), kind=kOutput, calls=%fused_computation.13 | convolution fusion | flops 19328925696 | bytes 17828864 | tf_op jit(solution)/shard_map/dot_general | solution.py:39
  665.1 2.3 collective-permute-start.3
  667.4 0.0 collective-permute-done.5
  667.4 335.9 %collective-permute-done.4 = f32[1024,2048]{0,1:T(8,128)S(1)} collective-permute-done((f32[1024,2048]{0,1:T(8,128)}, f32[1024,2048]{0,1:T(8,128)S(1)}, u32[]{:S(2)}, u32[]{:S(2)}) %collective-permute-start.4) | collective-permute-done | bytes 8388640 | tf_op jit(solution)/shard_map/ppermute | solution.py:10
  1003.3 0.0 collective-permute-done.3
  1003.3 26.8 %fusion.2 = f32[1,1024,2048]{1,2,0:T(8,128)} fusion(f32[1024,2048]{0,1:T(8,128)S(1)} %collective-permute-done.5, f32[1024,2048]{0,1:T(8,128)S(1)} %collective-permute-done.4, f32[1024,2048]{0,1:T(8,128)S(1)} %collective-permute-done.3, f32[1,4,768,1024]{3,2,1,0:T(8,128)} %param.4, f32[768,2048]{1,0:T(8,128)} %all-reduce.2.cloned.1.call-done, f32[768]{0:T(1024)S(1)} %fusion.50), kind=kOutput, calls=%fused_computation.3 | convolution fusion | flops 19335217152 | bytes 42994688 | tf_op jit(solution)/shard_map/dot_general | solution.py:39
  1030.1 9.1 copy.5
  (2 shorter events, 0.0 us)
Async XLA Ops:
  6.5 581.7 %all-reduce.2.cloned.1.call-start = ((), (), s32[]{:S(2)}) async-start(), calls=%async_computation | async-start | bytes 12582912 | tf_op jit(solution)/shard_map/psum | solution.py:34
  6.5 182.6 %collective-permute-start.1 = (f32[1024,2048]{1,0:T(8,128)}, f32[1024,2048]{1,0:T(8,128)S(1)}, u32[]{:S(2)}, u32[]{:S(2)}) collective-permute-start(f32[1024,2048]{1,0:T(8,128)} %bitcast.48), channel_id=1, source_target_pairs={{0,16},{8,24},{1,17},{9,25},{2,18},{10,26},{3,19},{11,27},{4,20},{... | collective-permute-start | bytes 25165832 | tf_op jit(solution)/shard_map/ppermute | solution.py:10
  10.2 211.2 %collective-permute-start = (f32[1024,2048]{1,0:T(8,128)}, f32[1024,2048]{1,0:T(8,128)}, u32[]{:S(2)}, u32[]{:S(2)}) collective-permute-start(f32[1024,2048]{1,0:T(8,128)} %bitcast.49), channel_id=1, source_target_pairs={{0,8},{8,16},{16,24},{1,9},{9,17},{17,25},{2,10},{10,18},{18,26},{... | collective-permute-start | bytes 25165832 | tf_op jit(solution)/shard_map/ppermute | solution.py:10
  12.1 233.1 %collective-permute-start.2 = (f32[1024,2048]{1,0:T(8,128)}, f32[1024,2048]{1,0:T(8,128)S(1)}, u32[]{:S(2)}, u32[]{:S(2)}) collective-permute-start(f32[1024,2048]{1,0:T(8,128)} %bitcast.50), channel_id=1, source_target_pairs={{0,24},{1,25},{2,26},{3,27},{4,28},{5,29},{6,30},{7,31}} | collective-permute-start | bytes 25165832 | tf_op jit(solution)/shard_map/ppermute | solution.py:10
  245.3 25.7 %copy-start.1 = (f32[1,768]{1,0:T(1,128)S(1)}, f32[1,768]{1,0:T(1,128)}, u32[]{:S(2)}) copy-start(f32[1,768]{1,0:T(1,128)} %param.6) | copy-start | bytes 9220
  588.2 27.1 %copy-start = (f32[768,2048]{1,0:T(8,128)S(1)}, f32[768,2048]{1,0:T(8,128)}, u32[]{:S(2)}) copy-start(f32[768,2048]{1,0:T(8,128)} %all-reduce.2.cloned.1.call-done) | copy-start | bytes 18874372
  614.1 53.3 %collective-permute-start.5 = (f32[1024,2048]{0,1:T(8,128)}, f32[1024,2048]{0,1:T(8,128)S(1)}, u32[]{:S(2)}, u32[]{:S(2)}) collective-permute-start(f32[1024,2048]{0,1:T(8,128)} %fusion.17), channel_id=1, source_target_pairs={{24,0},{25,1},{26,2},{27,3},{28,4},{29,5},{30,6},{31,7}} | collective-permute-start | bytes 25165832 | tf_op jit(solution)/shard_map/ppermute | solution.py:10
  639.6 363.7 %collective-permute-start.4 = (f32[1024,2048]{0,1:T(8,128)}, f32[1024,2048]{0,1:T(8,128)S(1)}, u32[]{:S(2)}, u32[]{:S(2)}) collective-permute-start(f32[1024,2048]{0,1:T(8,128)} %fusion.14), channel_id=1, source_target_pairs={{16,0},{24,8},{17,1},{25,9},{18,2},{26,10},{19,3},{27,11},{20,4},{... | collective-permute-start | bytes 25165832 | tf_op jit(solution)/shard_map/ppermute | solution.py:10
  665.1 338.2 %collective-permute-start.3 = (f32[1024,2048]{0,1:T(8,128)}, f32[1024,2048]{0,1:T(8,128)S(1)}, u32[]{:S(2)}, u32[]{:S(2)}) collective-permute-start(f32[1024,2048]{0,1:T(8,128)} %fusion.11), channel_id=1, source_target_pairs={{8,0},{16,8},{24,16},{9,1},{17,9},{25,17},{10,2},{18,10},{26,18},{... | collective-permute-start | bytes 25165832 | tf_op jit(solution)/shard_map/ppermute | solution.py:10
Sparse Core Ops, SparseCore 0:
  270.4 317.7 all-reduce.1
where the time goes:
time: 1060 us; the launch traced here: 1050 us
  waiting for transfers between devices  805 us (76%)
  matrix products  207 us (20%)
  between operations  14.6 us (1%)
  starting transfers between devices  11.5 us (1%)
    ppermute x6, waiting for transfers between devices, from_behind(): return lax.ppermute(value, axis, pairs)  487 us
    psum x1, waiting for transfers between devices, on_device(): modelled = lax.psum(partial_value, 'cells')  317 us
    dot_general x4, matrix products, on_device(): lax.dot_general(foot_slab[lag_step], weighted, (((0,), (0,)), ((), ())),...  101 us
    dot_general x3, matrix products, on_device(): jnp.dot(foot_slab[lag_step], earlier[lag_step], precision=highest, prefer...  81.1 us
    dot_general x1, matrix products, on_device(): jnp.dot(foot_slab[0], earlier[0], precision=highest, preferred_element_ty...  24.1 us
  transfers between devices with their start and end apart: 7, of which 3 were waited for; matrix products, arithmetic and copies ran while one was open for 12% of the time, Pallas kernels for 0%

commit v1 on v0

v1 whole, which is shorter than its diff:
```python
import jax
import jax.numpy as jnp
from jax import lax
from jax.sharding import Mesh, PartitionSpec as P

CHUNKS = 2


def shifted(value, by):
    devices = lax.axis_size("tm")
    pairs = [(i, i + by) for i in range(devices) if 0 <= i + by < devices]
    return lax.ppermute(value, "tm", pairs)


def swapped(value):
    return lax.ppermute(value, "core", [(0, 1), (1, 0)])


def product(left, right):
    return jnp.dot(
        left, right, precision=lax.Precision.HIGH, preferred_element_type=jnp.float32
    )


def adjoint(left, right):
    return lax.dot_general(
        left,
        right,
        (((0,), (0,)), ((), ())),
        precision=lax.Precision.HIGH,
        preferred_element_type=jnp.float32,
    )


def on_device(footprint, flux, obs_weight, obs_count):
    foot = footprint[0]
    lags, slots, _ = foot.shape
    half = flux.shape[2] // 2
    width = half // CHUNKS
    core = lax.axis_index("core")
    valid = (jnp.arange(slots, dtype=jnp.int32) < obs_count[0]).astype(jnp.float32)
    row_scale = valid * obs_weight[0]

    foot_own = [foot[0]] + [shifted(foot[lag], -lag) for lag in range(1, lags)]
    flux_own = lax.dynamic_slice_in_dim(flux[0], core * half, half, 1)
    flux_other = swapped(lax.dynamic_slice_in_dim(flux[0], (1 - core) * half, half, 1))
    foot_other = [swapped(value) for value in foot_own]

    def forward(lag, start, size):
        return product(foot_own[lag], flux_own[:, start:start + size]) + product(
            foot_other[lag], flux_other[:, start:start + size]
        )

    early = forward(0, 0, half)
    for lag in range(1, lags - 1):
        early = early + shifted(forward(lag, 0, half), lag)

    own_parts, other_parts = [], []
    for chunk in range(CHUNKS):
        start = chunk * width
        last = shifted(forward(lags - 1, start, width), lags - 1)
        if chunk:
            last, modelled = lax.optimization_barrier((last, modelled))
        partial = early[:, start:start + width] + last
        modelled = lax.psum(partial, "z")
        scale, arrived = lax.optimization_barrier((row_scale, modelled))
        weighted = scale[:, None] * arrived
        own, other = None, None
        for lag in range(lags):
            here = weighted if lag == 0 else shifted(weighted, -lag)
            term_own, term_other = adjoint(foot_own[lag], here), adjoint(foot_other[lag], here)
            own = term_own if own is None else own + term_own
            other = term_other if other is None else other + term_other
        own_parts.append(own)
        other_parts.append(swapped(other))
    own = jnp.concatenate(own_parts, axis=1)
    other = jnp.concatenate(other_parts, axis=1)
    first = jnp.where(core == 0, own, other)
    second = jnp.where(core == 0, other, own)
    return jnp.concatenate([first, second], axis=1)[None]


def solution(mesh):
    devices = mesh.devices
    split = Mesh(devices.reshape(devices.shape[0], devices.shape[1] // 2, 2), ("tm", "z", "core"))
    cells = ("z", "core")
    placed = (P("tm", None, None, cells), P("tm", cells, None), P("tm", None), P("tm"))
    return jax.shard_map(
        on_device, mesh=split, in_specs=placed, out_specs=P("tm", cells, None), check_vma=False
    )
```

time: 1060 us -> 637 us (0.60)
  waiting for transfers between devices: 805 us -> 362 us
  matrix products: 207 us -> 171 us
  local copies, waits for them, and re-layouts: 9.13 us -> 29.3 us
  starting transfers between devices: 11.5 us -> 30.9 us
  other arithmetic: 0.02 us -> 16.5 us
    ppermute x6 -> x20, waiting for transfers between devices: 487 us -> 244 us  [the longest x13 244 us: shifted(): return lax.ppermute(value, 'tm', pairs)]
    psum x1 -> x2, waiting for transfers between devices: 317 us -> 118 us  [on_device(): modelled = lax.psum(partial, 'z')]
    dot_general x8 -> x26, matrix products: 207 us -> 171 us  [the longest x10 102 us: product(): jnp.dot(left, right, precision=lax.Precision.HIGH, preferred_element_type...]
    ppermute x6 -> x20, starting transfers between devices: 11.5 us -> 30.8 us  [the longest x13 22.7 us: shifted(): return lax.ppermute(value, 'tm', pairs)]
    squeeze x0 -> x1, local copies, waits for them, and re-layouts: none -> 10.7 us  [on_device(): foot_own = [foot[0]] + [shifted(foot[lag], -lag) for lag in range(1, lags)]]
  transfers between devices with their start and end apart: 7 -> 22, of which waited for: 3 -> 8; matrix products, arithmetic and copies ran while one was open for 12% -> 30% of each run, Pallas kernels for 0% -> 0%
where the time goes in v1:
time: 637 us; the launch traced here: 624 us
  waiting for transfers between devices  362 us (57%)
  matrix products  171 us (27%)
  starting transfers between devices  30.9 us (5%)
  local copies, waits for them, and re-layouts  29.3 us (5%)
  other arithmetic  16.5 us (3%)
  between operations  14.8 us (2%)
    ppermute x13, waiting for transfers between devices, shifted(): return lax.ppermute(value, 'tm', pairs)  244 us
    psum x2, waiting for transfers between devices, on_device(): modelled = lax.psum(partial, 'z')  118 us
    dot_general x10, matrix products, product(): jnp.dot(left, right, precision=lax.Precision.HIGH, preferred_element_type...  102 us
    dot_general x16, matrix products, adjoint(): lax.dot_general(left, right, (((0,), (0,)), ((), ())), precision=lax.Prec...  68.6 us
    ppermute x13, starting transfers between devices, shifted(): return lax.ppermute(value, 'tm', pairs)  22.7 us
  transfers between devices with their start and end apart: 22, of which 8 were waited for; matrix products, arithmetic and copies ran while one was open for 30% of the time, Pallas kernels for 0%

profile of v1, /device:TPU:3, one launch (start us, length us, event | category | flops | bytes accessed | tf_op | source)
XLA Modules:
  0.0 624.2 jit_solution(3158813942686587122)
XLA Ops:
  6.5 10.7 %slice_bitcast_fusion.3 = (f32[768,1024]{1,0:T(8,128)}, f32[768,1024]{1,0:T(8,128)}, f32[768,1024]{1,0:T(8,128)}, f32[768,1024]{1,0:T(8,128)}) fusion(f32[1,4,768,1024]{3,2,1,0:T(8,128)} %param.4), kind=kLoop, calls=%fused_computation.13 | loop fusion | bytes 25165824 | tf_op jit(solution)/shard_map/squeeze | solution.py:44
  17.2 1.9 collective-permute-start.2
  21.3 4.5 dynamic-slice_bitcast_fusion
  26.5 62.8 %collective-permute-done.2 = f32[768,1024]{1,0:T(8,128)} collective-permute-done((f32[768,1024]{1,0:T(8,128)}, f32[768,1024]{1,0:T(8,128)}, u32[]{:S(2)}, u32[]{:S(2)}) %collective-permute-start.2) | collective-permute-done | bytes 3145760 | tf_op jit(solution)/shard_map/ppermute | solution.py:12
  90.9 66.8 %collective-permute-done.5 = f32[768,1024]{1,0:T(8,128)} collective-permute-done((f32[768,1024]{1,0:T(8,128)}, f32[768,1024]{1,0:T(8,128)}, u32[]{:S(2)}, u32[]{:S(2)}) %collective-permute-start.5) | collective-permute-done | bytes 3145760 | tf_op jit(solution)/shard_map/ppermute | solution.py:12
  158.8 13.8 %fusion.20 = f32[1024,768]{1,0:T(8,128)} fusion(f32[1024,1024]{1,0:T(8,128)S(1)} %get-tuple-element.22, f32[768,1024]{1,0:T(8,128)} %collective-permute-done.2), kind=kOutput, calls=%fused_computation.40 | convolution fusion | flops 4831838208 | bytes 10485760 | tf_op jit(solution)/shard_map/dot_general | solution.py:20
  172.6 14.1 %fusion.21 = f32[1024,768]{1,0:T(8,128)} fusion(f32[1024,1024]{1,0:T(8,128)S(1)} %get-tuple-element.22, f32[768,1024]{1,0:T(8,128)} %collective-permute-done.5), kind=kOutput, calls=%fused_computation.41 | convolution fusion | flops 4831838208 | bytes 10485760 | tf_op jit(solution)/shard_map/dot_general | solution.py:20
  186.7 13.5 %add_bitcast_fusion.1 = f32[768,1024]{0,1:T(8,128)S(1)} fusion(f32[1024,768]{1,0:T(8,128)} %fusion.20, f32[1024,1024]{1,0:T(8,128)S(1)} %collective-permute-done, f32[768,1024]{1,0:T(8,128)S(1)} %collective-permute-done.3), kind=kOutput, calls=%fused_computation.11 | convolution fusion | flops 4832624640 | bytes 13631488 | tf_op jit(solution)/shard_map/dot_general | solution.py:20
  200.2 2.5 collective-permute-start.4
  202.7 13.9 %add_bitcast_fusion = f32[768,1024]{0,1:T(8,128)} fusion(f32[1024,768]{1,0:T(8,128)} %fusion.21, f32[1024,1024]{1,0:T(8,128)S(1)} %collective-permute-done, f32[768,1024]{1,0:T(8,128)S(1)} %collective-permute-done.6), kind=kOutput, calls=%fused_computation.9 | convolution fusion | flops 4832624640 | bytes 13631488 | tf_op jit(solution)/shard_map/dot_general | solution.py:20
  216.6 1.9 collective-permute-start.7
  218.5 13.8 %fusion.18 = f32[1024,768]{1,0:T(8,128)} fusion(f32[1024,1024]{1,0:T(8,128)S(1)} %get-tuple-element.22, f32[1,4,768,1024]{3,2,1,0:T(8,128)} %param.4), kind=kOutput, calls=%fused_computation.38 | convolution fusion | flops 4831838208 | bytes 10485760 | tf_op jit(solution)/shard_map/dot_general | solution.py:20
  232.3 5.5 fusion.5
  237.8 5.3 fusion.9
  243.1 5.4 add_bitcast_fusion.7
  250.3 9.9 %fusion.19 = f32[1024,768]{1,0:T(8,128)S(1)} fusion(f32[1024,1024]{1,0:T(8,128)S(1)} %collective-permute-done, f32[768,1024]{1,0:T(8,128)S(1)} %collective-permute-done.1), kind=kOutput, calls=%fused_computation.39 | convolution fusion | flops 4831838208 | bytes 10485760 | tf_op jit(solution)/shard_map/dot_general | solution.py:20
  260.3 6.8 %add_bitcast_fusion.6 = f32[768,512]{0,1:T(8,128)} fusion(f32[512,768]{1,0:T(8,128)S(1)} %fusion.5, f32[768,1024]{1,0:T(8,128)S(1)} %collective-permute-done.9, f32[1024,1024]{1,0:T(8,128)S(1)} %collective-permute-done), kind=kOutput, calls=%fused_computation.28 | convolution fusion | flops 2416312320 | bytes 8388608 | tf_op jit(solution)/shard_map/dot_general | solution.py:20
  268.9 2.8 collective-permute-done.4
  271.7 81.3 %collective-permute-done.7 = f32[768,1024]{0,1:T(8,128)S(1)} collective-permute-done((f32[768,1024]{0,1:T(8,128)}, f32[768,1024]{0,1:T(8,128)S(1)}, u32[]{:S(2)}, u32[]{:S(2)}) %collective-permute-start.7) | collective-permute-done | bytes 3145760 | tf_op jit(solution)/shard_map/ppermute | solution.py:12
  355.5 2.8 slice_add_fusion.1
  359.1 69.7 %all-reduce.3.cloned.1.call-done = f32[768,512]{0,1:T(8,128)} async-done(((f32[768,512]{0,1:T(8,128)}), f32[768,512]{0,1:T(8,128)}) %all-reduce.3.cloned.1.call-update) | async-done | bytes 1572880 | tf_op jit(solution)/shard_map/psum | solution.py:65
  428.8 3.2 slice_add_fusion
  432.0 2.7 broadcast_multiply_fusion.1
  434.7 2.2 collective-permute-start.11
  438.2 2.0 collective-permute-start.13
  440.2 6.4 %fusion.17 = f32[512,1024]{1,0:T(8,128)} fusion(f32[768,512]{0,1:T(8,128)} %broadcast_multiply_fusion.1, f32[1,4,768,1024]{3,2,1,0:T(8,128)} %param.4), kind=kOutput, calls=%fused_computation.37 | convolution fusion | flops 2415919104 | bytes 6815744 | tf_op jit(solution)/shard_map/dot_general | solution.py:26
  446.5 5.6 fusion.26
  452.1 48.2 %all-reduce.5.cloned.1.call-done = f32[768,512]{0,1:T(8,128)} async-done(((f32[768,512]{0,1:T(8,128)}), f32[768,512]{0,1:T(8,128)}) %all-reduce.5.cloned.1.call-update) | async-done | bytes 1572880 | tf_op jit(solution)/shard_map/psum | solution.py:65
  504.2 3.0 collective-permute-start.15
  507.2 4.1 fusion.27
  511.4 4.3 fusion.28
  515.7 4.2 add_bitcast_fusion.3
  520.0 2.1 collective-permute-start.18
  522.1 4.6 fusion.16
  526.7 5.5 fusion.22
  532.1 5.2 fusion.23
  537.4 2.9 fusion.29
  541.7 2.7 fusion.30
  544.4 29.2 %collective-permute-done.16 = f32[768,512]{0,1:T(8,128)S(1)} collective-permute-done((f32[768,512]{0,1:T(8,128)S(1)}, f32[768,512]{0,1:T(8,128)S(1)}, u32[]{:S(2)}, u32[]{:S(2)}) %collective-permute-start.16) | collective-permute-done | bytes 1572896 | tf_op jit(solution)/shard_map/ppermute | solution.py:12
  573.6 2.7 fusion.31
  576.3 3.0 add_bitcast_fusion.2
  579.3 2.6 collective-permute-start.19
  581.9 4.2 add_bitcast_fusion.5
  586.1 4.6 fusion.24
  590.7 4.6 fusion.25
  595.3 4.2 add_bitcast_fusion.4
  604.0 4.1 maximum_bitcast_fusion
  608.1 9.1 %copy.5 = f32[1,1024,2048]{2,1,0:T(8,128)} copy(f32[1,1024,2048]{1,2,0:T(8,128)} %maximum_bitcast_fusion) | data formatting | bytes 16777216 | tf_op jit(solution)/shard_map/broadcast_in_dim | solution.py:80
  (70 shorter events, 22.9 us)
Async XLA Ops:
  6.5 422.2 %all-reduce.3.cloned.1.call-start = ((), (), s32[]{:S(2)}) async-start(), calls=%async_computation | async-start | bytes 3145728 | tf_op jit(solution)/shard_map/psum | solution.py:65
  17.2 72.1 %collective-permute-start.2 = (f32[768,1024]{1,0:T(8,128)}, f32[768,1024]{1,0:T(8,128)}, u32[]{:S(2)}, u32[]{:S(2)}) collective-permute-start(f32[768,1024]{1,0:T(8,128)} %get-tuple-element.16), channel_id=1, source_target_pairs={{8,0},{16,8},{24,16},{9,1},{17,9},{25,17},{10,2},{18,10},{26,18},{... | collective-permute-start | bytes 9437192 | tf_op jit(solution)/shard_map/ppermute | solution.py:12
  19.1 138.6 %collective-permute-start.5 = (f32[768,1024]{1,0:T(8,128)}, f32[768,1024]{1,0:T(8,128)}, u32[]{:S(2)}, u32[]{:S(2)}) collective-permute-start(f32[768,1024]{1,0:T(8,128)} %get-tuple-element.18), channel_id=1, source_target_pairs={{16,0},{24,8},{17,1},{25,9},{18,2},{26,10},{19,3},{27,11},{20,4},{... | collective-permute-start | bytes 9437192 | tf_op jit(solution)/shard_map/ppermute | solution.py:12
  20.4 137.8 %collective-permute-start.8 = (f32[768,1024]{1,0:T(8,128)}, f32[768,1024]{1,0:T(8,128)S(1)}, u32[]{:S(2)}, u32[]{:S(2)}) collective-permute-start(f32[768,1024]{1,0:T(8,128)} %get-tuple-element.17), channel_id=1, source_target_pairs={{24,0},{25,1},{26,2},{27,3},{28,4},{29,5},{30,6},{31,7}} | collective-permute-start | bytes 9437192 | tf_op jit(solution)/shard_map/ppermute | solution.py:12
  21.3 136.9 %copy-start.13 = (f32[768,1024]{1,0:T(8,128)S(1)}, f32[768,1024]{1,0:T(8,128)}, u32[]{:S(2)}) copy-start(f32[768,1024]{1,0:T(8,128)} %get-tuple-element.15) | copy-start | bytes 9437188
  25.8 160.9 %collective-permute-start = (f32[1024,1024]{1,0:T(8,128)S(1)}, f32[1024,1024]{1,0:T(8,128)S(1)}, u32[]{:S(2)}, u32[]{:S(2)}) collective-permute-start(f32[1024,1024]{1,0:T(8,128)S(1)} %get-tuple-element.21), channel_id=1, source_target_pairs={{0,1},{1,0},{2,3},{3,2},{4,5},{5,4},{6,7},{7,6},{8,9},{9,8},{10,11... | collective-permute-start | bytes 12582920 | tf_op jit(solution)/shard_map/ppermute | solution.py:16
  89.3 97.3 %collective-permute-start.3 = (f32[768,1024]{1,0:T(8,128)}, f32[768,1024]{1,0:T(8,128)S(1)}, u32[]{:S(2)}, u32[]{:S(2)}) collective-permute-start(f32[768,1024]{1,0:T(8,128)} %collective-permute-done.2), channel_id=1, source_target_pairs={{0,1},{1,0},{2,3},{3,2},{4,5},{5,4},{6,7},{7,6},{8,9},{9,8},{10,11... | collective-permute-start | bytes 9437192 | tf_op jit(solution)/shard_map/ppermute | solution.py:16
  157.8 44.9 %collective-permute-start.6 = (f32[768,1024]{1,0:T(8,128)}, f32[768,1024]{1,0:T(8,128)S(1)}, u32[]{:S(2)}, u32[]{:S(2)}) collective-permute-start(f32[768,1024]{1,0:T(8,128)} %collective-permute-done.5), channel_id=1, source_target_pairs={{0,1},{1,0},{2,3},{3,2},{4,5},{5,4},{6,7},{7,6},{8,9},{9,8},{10,11... | collective-permute-start | bytes 9437192 | tf_op jit(solution)/shard_map/ppermute | solution.py:16
  158.2 92.1 %collective-permute-start.1 = (f32[768,1024]{1,0:T(8,128)S(1)}, f32[768,1024]{1,0:T(8,128)S(1)}, u32[]{:S(2)}, u32[]{:S(2)}) collective-permute-start(f32[768,1024]{1,0:T(8,128)S(1)} %copy-done.13), channel_id=1, source_target_pairs={{0,1},{1,0},{2,3},{3,2},{4,5},{5,4},{6,7},{7,6},{8,9},{9,8},{10,11... | collective-permute-start | bytes 9437192 | tf_op jit(solution)/shard_map/ppermute | solution.py:16
  158.3 84.8 %collective-permute-start.9 = (f32[768,1024]{1,0:T(8,128)S(1)}, f32[768,1024]{1,0:T(8,128)S(1)}, u32[]{:S(2)}, u32[]{:S(2)}) collective-permute-start(f32[768,1024]{1,0:T(8,128)S(1)} %collective-permute-done.8), channel_id=1, source_target_pairs={{0,1},{1,0},{2,3},{3,2},{4,5},{5,4},{6,7},{7,6},{8,9},{9,8},{10,11... | collective-permute-start | bytes 9437192 | tf_op jit(solution)/shard_map/ppermute | solution.py:16
  186.7 13.5 %copy-start.2 = (f32[768,1024]{1,0:T(8,128)}, f32[768,1024]{1,0:T(8,128)S(1)}, u32[]{:S(2)}) copy-start(f32[768,1024]{1,0:T(8,128)S(1)} %collective-permute-done.3) | copy-start | bytes 9437188
  200.2 71.5 %collective-permute-start.4 = (f32[768,1024]{0,1:T(8,128)S(1)}, f32[768,1024]{0,1:T(8,128)S(1)}, u32[]{:S(2)}, u32[]{:S(2)}) collective-permute-start(f32[768,1024]{0,1:T(8,128)S(1)} %add_bitcast_fusion.1), channel_id=1, source_target_pairs={{0,8},{8,16},{16,24},{1,9},{9,17},{17,25},{2,10},{10,18},{18,26},{... | collective-permute-start | bytes 9437192 | tf_op jit(solution)/shard_map/ppermute | solution.py:12
  202.7 13.9 %copy-start.4 = (f32[768,1024]{1,0:T(8,128)}, f32[768,1024]{1,0:T(8,128)S(1)}, u32[]{:S(2)}) copy-start(f32[768,1024]{1,0:T(8,128)S(1)} %collective-permute-done.6) | copy-start | bytes 9437188
  216.6 136.4 %collective-permute-start.7 = (f32[768,1024]{0,1:T(8,128)}, f32[768,1024]{0,1:T(8,128)S(1)}, u32[]{:S(2)}, u32[]{:S(2)}) collective-permute-start(f32[768,1024]{0,1:T(8,128)} %add_bitcast_fusion), channel_id=1, source_target_pairs={{0,16},{8,24},{1,17},{9,25},{2,18},{10,26},{3,19},{11,27},{4,20},{... | collective-permute-start | bytes 9437192 | tf_op jit(solution)/shard_map/ppermute | solution.py:12
  243.1 17.1 %copy-start = (f32[768,1024]{1,0:T(8,128)}, f32[768,1024]{1,0:T(8,128)S(1)}, u32[]{:S(2)}) copy-start(f32[768,1024]{1,0:T(8,128)S(1)} %collective-permute-done.9) | copy-start | bytes 9437188
  248.5 105.4 %collective-permute-start.10 = (f32[768,512]{0,1:T(8,128)S(1)}, f32[768,512]{0,1:T(8,128)}, u32[]{:S(2)}, u32[]{:S(2)}) collective-permute-start(f32[768,512]{0,1:T(8,128)S(1)} %add_bitcast_fusion.7), channel_id=1, source_target_pairs={{0,24},{1,25},{2,26},{3,27},{4,28},{5,29},{6,30},{7,31}} | collective-permute-start | bytes 4718600 | tf_op jit(solution)/shard_map/ppermute | solution.py:12
  250.3 9.9 %copy-start.6 = (f32[768,1024]{1,0:T(8,128)}, f32[768,1024]{1,0:T(8,128)S(1)}, u32[]{:S(2)}) copy-start(f32[768,1024]{1,0:T(8,128)S(1)} %collective-permute-done.1) | copy-start | bytes 9437188
  260.3 92.8 %copy-start.14 = (f32[1024,768]{1,0:T(8,128)S(1)}, f32[1024,768]{1,0:T(8,128)}, u32[]{:S(2)}) copy-start(f32[1024,768]{1,0:T(8,128)} %fusion.18) | copy-start | bytes 9437188
  267.0 92.0 %collective-permute-start.14 = (f32[768,512]{0,1:T(8,128)}, f32[768,512]{0,1:T(8,128)}, u32[]{:S(2)}, u32[]{:S(2)}) collective-permute-start(f32[768,512]{0,1:T(8,128)} %add_bitcast_fusion.6), channel_id=1, source_target_pairs={{0,24},{1,25},{2,26},{3,27},{4,28},{5,29},{6,30},{7,31}} | collective-permute-start | bytes 4718600 | tf_op jit(solution)/shard_map/ppermute | solution.py:12
  353.8 1.7 copy-start.9
  353.9 5.2 copy-start.15
  358.3 142.0 %all-reduce.5.cloned.1.call-start = ((), (), s32[]{:S(2)}) async-start(), calls=%async_computation.1 | async-start | bytes 3145728 | tf_op jit(solution)/shard_map/psum | solution.py:65
  434.7 69.5 %collective-permute-start.11 = (f32[768,512]{0,1:T(8,128)}, f32[768,512]{0,1:T(8,128)}, u32[]{:S(2)}, u32[]{:S(2)}) collective-permute-start(f32[768,512]{0,1:T(8,128)} %broadcast_multiply_fusion.1), channel_id=1, source_target_pairs={{8,0},{16,8},{24,16},{9,1},{17,9},{25,17},{10,2},{18,10},{26,18},{... | collective-permute-start | bytes 4718600 | tf_op jit(solution)/shard_map/ppermute | solution.py:12
  436.9 74.5 %collective-permute-start.12 = (f32[768,512]{0,1:T(8,128)}, f32[768,512]{0,1:T(8,128)}, u32[]{:S(2)}, u32[]{:S(2)}) collective-permute-start(f32[768,512]{0,1:T(8,128)} %broadcast_multiply_fusion.1), channel_id=1, source_target_pairs={{16,0},{24,8},{17,1},{25,9},{18,2},{26,10},{19,3},{27,11},{20,4},{... | collective-permute-start | bytes 4718600 | tf_op jit(solution)/shard_map/ppermute | solution.py:12
  438.2 8.3 %copy-start.7 = (f32[768,1024]{1,0:T(8,128)S(1)}, f32[768,1024]{1,0:T(8,128)}, u32[]{:S(2)}) copy-start(f32[768,1024]{1,0:T(8,128)} %copy-done.6) | copy-start | bytes 9437188
  438.2 77.5 %collective-permute-start.13 = (f32[768,512]{0,1:T(8,128)}, f32[768,512]{0,1:T(8,128)}, u32[]{:S(2)}, u32[]{:S(2)}) collective-permute-start(f32[768,512]{0,1:T(8,128)} %broadcast_multiply_fusion.1), channel_id=1, source_target_pairs={{24,0},{25,1},{26,2},{27,3},{28,4},{29,5},{30,6},{31,7}} | collective-permute-start | bytes 4718600 | tf_op jit(solution)/shard_map/ppermute | solution.py:12
  500.3 6.9 %copy-start.3 = (f32[768,1024]{1,0:T(8,128)S(1)}, f32[768,1024]{1,0:T(8,128)}, u32[]{:S(2)}) copy-start(f32[768,1024]{1,0:T(8,128)} %copy-done.2) | copy-start | bytes 9437188
  502.0 9.4 %copy-start.5 = (f32[768,1024]{1,0:T(8,128)S(1)}, f32[768,1024]{1,0:T(8,128)}, u32[]{:S(2)}) copy-start(f32[768,1024]{1,0:T(8,128)} %copy-done.4) | copy-start | bytes 9437188
  502.0 74.3 %collective-permute-start.17 = (f32[768,512]{0,1:T(8,128)S(1)}, f32[768,512]{0,1:T(8,128)S(1)}, u32[]{:S(2)}, u32[]{:S(2)}) collective-permute-start(f32[768,512]{0,1:T(8,128)S(1)} %broadcast_multiply_fusion), channel_id=1, source_target_pairs={{24,0},{25,1},{26,2},{27,3},{28,4},{29,5},{30,6},{31,7}} | collective-permute-start | bytes 4718600 | tf_op jit(solution)/shard_map/ppermute | solution.py:12
  502.9 70.7 %collective-permute-start.16 = (f32[768,512]{0,1:T(8,128)S(1)}, f32[768,512]{0,1:T(8,128)S(1)}, u32[]{:S(2)}, u32[]{:S(2)}) collective-permute-start(f32[768,512]{0,1:T(8,128)S(1)} %broadcast_multiply_fusion), channel_id=1, source_target_pairs={{16,0},{24,8},{17,1},{25,9},{18,2},{26,10},{19,3},{27,11},{20,4},{... | collective-permute-start | bytes 4718600 | tf_op jit(solution)/shard_map/ppermute | solution.py:12
  504.2 37.5 %collective-permute-start.15 = (f32[768,512]{0,1:T(8,128)S(1)}, f32[768,512]{0,1:T(8,128)S(1)}, u32[]{:S(2)}, u32[]{:S(2)}) collective-permute-start(f32[768,512]{0,1:T(8,128)S(1)} %broadcast_multiply_fusion), channel_id=1, source_target_pairs={{8,0},{16,8},{24,16},{9,1},{17,9},{25,17},{10,2},{18,10},{26,18},{... | collective-permute-start | bytes 4718600 | tf_op jit(solution)/shard_map/ppermute | solution.py:12
  511.4 4.3 copy-start.1
  511.4 4.3 copy-start.12
  520.0 79.5 %collective-permute-start.18 = (f32[1024,512]{0,1:T(8,128)S(1)}, f32[1024,512]{0,1:T(8,128)}, u32[]{:S(2)}, u32[]{:S(2)}) collective-permute-start(f32[1024,512]{0,1:T(8,128)S(1)} %add_bitcast_fusion.3), channel_id=1, source_target_pairs={{0,1},{1,0},{2,3},{3,2},{4,5},{5,4},{6,7},{7,6},{8,9},{9,8},{10,11... | collective-permute-start | bytes 6291464 | tf_op jit(solution)/shard_map/ppermute | solution.py:16
  532.1 5.2 copy-start.8
  576.3 5.6 copy-start.11
  579.3 21.9 %collective-permute-start.19 = (f32[1024,512]{0,1:T(8,128)S(1)}, f32[1024,512]{0,1:T(8,128)S(1)}, u32[]{:S(2)}, u32[]{:S(2)}) collective-permute-start(f32[1024,512]{0,1:T(8,128)S(1)} %add_bitcast_fusion.2), channel_id=1, source_target_pairs={{0,1},{1,0},{2,3},{3,2},{4,5},{5,4},{6,7},{7,6},{8,9},{9,8},{10,11... | collective-permute-start | bytes 6291464 | tf_op jit(solution)/shard_map/ppermute | solution.py:16
  601.2 1.6 copy-start.10
Sparse Core Ops, SparseCore 0:
  358.4 70.2 all-reduce.2
  432.1 68.1 all-reduce.4

commit v2 on v1

v2 whole, which is shorter than its diff:
```python
import functools

import jax
import jax.numpy as jnp
from jax import lax
from jax.experimental import pallas as pl
from jax.experimental.pallas import tpu as pltpu
from jax.sharding import Mesh, PartitionSpec as P

CHUNKS = 3
TILE = 256
VMEM_LIMIT = 60 * 1024 * 1024


def shifted(value, by):
    devices = lax.axis_size("tm")
    pairs = [(i, i + by) for i in range(devices) if 0 <= i + by < devices]
    return lax.ppermute(value, "tm", pairs)


def swapped(value):
    return lax.ppermute(value, "core", [(0, 1), (1, 0)])


def together(first, second):
    return lax.optimization_barrier((first, second))


def halves(value):
    high = value.astype(jnp.bfloat16)
    low = (value - high.astype(jnp.float32)).astype(jnp.bfloat16)
    return high, low


def times(left, right, dims):
    return lax.dot_general(left, right, (dims, ((), ())), preferred_element_type=jnp.float32)


def forward_kernel(count, core_ref, *refs):
    foot_own, foot_other = refs[:count], refs[count:2 * count]
    flux_own, flux_other = refs[2 * count:2 * count + 2]
    outs = refs[2 * count + 2:3 * count + 2]
    high_ref, low_ref = refs[3 * count + 2:]
    rows, cells = foot_own[0].shape[-2:]

    @pl.when(pl.program_id(0) == 0)
    def _():
        for i in range(count):
            for side, source in ((0, foot_own[i]), (1, foot_other[i])):
                high, low = halves(source[...].reshape(rows, cells))
                at = (pl.ds(i * rows, rows), pl.ds(side * cells, cells))
                high_ref[at] = high
                low_ref[at] = low

    total = None
    for side, source in ((0, flux_own), (1, flux_other)):
        high, low = halves(source[...].reshape(cells, -1))
        at = pl.ds(side * cells, cells)
        dims = ((1,), (0,))
        term = times(high_ref[:, at], high, dims)
        term = term + times(low_ref[:, at], high, dims)
        term = term + times(high_ref[:, at], low, dims)
        total = term if total is None else total + term
    for i in range(count):
        outs[i][...] = total[i * rows:(i + 1) * rows]


def forward(
    foot_own, own_specs, foot_other, other_specs, rows, flux, flux_other, cells, half, core
):
    count = len(foot_own)
    tile = min(TILE, half)
    steps = half // tile
    work = 2 * count * rows * 2 * cells * half
    outs = pl.pallas_call(
        functools.partial(forward_kernel, count),
        grid_spec=pltpu.PrefetchScalarGridSpec(
            num_scalar_prefetch=1,
            grid=(steps,),
            in_specs=[
                *own_specs,
                *other_specs,
                pl.BlockSpec((1, cells, tile), lambda j, c: (0, 0, c[0] * steps + j)),
                pl.BlockSpec((cells, tile), lambda j, c: (0, j)),
            ],
            out_specs=[pl.BlockSpec((rows, tile), lambda j, c: (0, j))] * count,
            scratch_shapes=[pltpu.VMEM((count * rows, 2 * cells), jnp.bfloat16)] * 2,
        ),
        out_shape=[jax.ShapeDtypeStruct((rows, half), jnp.float32)] * count,
        compiler_params=pltpu.CompilerParams(vmem_limit_bytes=VMEM_LIMIT),
        cost_estimate=pl.CostEstimate(
            flops=3 * work,
            bytes_accessed=4 * (count * rows * (2 * cells + half) + 2 * cells * half),
            transcendentals=0,
        ),
    )(core, *foot_own, *foot_other, flux, flux_other)
    return list(outs)


def adjoint_kernel(count, first, core_ref, *refs):
    foot, weighted = refs[:count], refs[count:2 * count]
    rest = refs[2 * count:]
    before = None if first else rest[0]
    out_ref, high_ref, low_ref = rest[-3:]
    rows, tile = foot[0].shape[-2:]

    @pl.when(pl.program_id(0) == 0)
    def _():
        for i in range(count):
            high, low = halves(weighted[i][...])
            high_ref[pl.ds(i * rows, rows), :] = high
            low_ref[pl.ds(i * rows, rows), :] = low

    slab = jnp.concatenate([foot[i][...].reshape(rows, tile) for i in range(count)], axis=0)
    high, low = halves(slab)
    dims = ((0,), (0,))
    total = times(high, high_ref[...], dims)
    total = total + times(low, high_ref[...], dims)
    total = total + times(high, low_ref[...], dims)
    if not first:
        total = total + before[...]
    out_ref[...] = total


def adjoint(foot, foot_specs, weighted, before, out_shape, at_core, core, cells):
    count = len(foot)
    rows, half = weighted[0].shape
    tile = min(TILE, cells)
    out_spec = pl.BlockSpec((tile, half), lambda j, c: (j, c[0] if at_core else 0))
    first = before is None
    return pl.pallas_call(
        functools.partial(adjoint_kernel, count, first),
        grid_spec=pltpu.PrefetchScalarGridSpec(
            num_scalar_prefetch=1,
            grid=(cells // tile,),
            in_specs=[
                *[spec(tile) for spec in foot_specs],
                *[pl.BlockSpec((rows, half), lambda j, c: (0, 0))] * count,
                *([] if first else [out_spec]),
            ],
            out_specs=out_spec,
            scratch_shapes=[pltpu.VMEM((count * rows, half), jnp.bfloat16)] * 2,
        ),
        out_shape=jax.ShapeDtypeStruct(out_shape, jnp.float32),
        input_output_aliases={} if first else {1 + 2 * count: 0},
        compiler_params=pltpu.CompilerParams(vmem_limit_bytes=VMEM_LIMIT),
        cost_estimate=pl.CostEstimate(
            flops=3 * 2 * count * rows * cells * half,
            bytes_accessed=4 * (count * rows * (cells + half) + 2 * cells * half),
            transcendentals=0,
        ),
    )(core, *foot, *weighted, *([] if first else [before]))


def combine_kernel(scale, same, *refs):
    total = same[...]
    for ref in refs[:-1]:
        total = total + ref[...]
    refs[-1][...] = scale[...] * total


def combine(scale, same, gathered, r):
    rows, half = gathered[0].shape
    tile = min(TILE, half)
    block = pl.BlockSpec((rows, tile), lambda j: (0, j))
    return pl.pallas_call(
        combine_kernel,
        grid=(half // tile,),
        in_specs=[
            pl.BlockSpec((rows, 1), lambda j: (r, 0)),
            block,
            *[block] * len(gathered),
        ],
        out_specs=block,
        out_shape=jax.ShapeDtypeStruct((rows, half), jnp.float32),
        cost_estimate=pl.CostEstimate(
            flops=(len(gathered) + 1) * rows * half,
            bytes_accessed=4 * (len(gathered) + 2) * rows * half,
            transcendentals=0,
        ),
    )(scale, same, *gathered)


def paste_kernel(core_ref, arrived, before, out_ref):
    out_ref[...] = arrived[...]


def paste(arrived, whole, core):
    cells, half = arrived.shape
    tile = min(TILE, cells)
    return pl.pallas_call(
        paste_kernel,
        grid_spec=pltpu.PrefetchScalarGridSpec(
            num_scalar_prefetch=1,
            grid=(cells // tile,),
            in_specs=[
                pl.BlockSpec((tile, half), lambda j, c: (j, 0)),
                pl.BlockSpec(memory_space=pl.ANY),
            ],
            out_specs=pl.BlockSpec((tile, half), lambda j, c: (j, 1 - c[0])),
        ),
        out_shape=jax.ShapeDtypeStruct(whole.shape, jnp.float32),
        input_output_aliases={2: 0},
        cost_estimate=pl.CostEstimate(
            flops=0, bytes_accessed=8 * cells * half, transcendentals=0
        ),
    )(core, arrived, whole)


def on_device(footprint, flux, obs_weight, obs_count):
    _, lags, slots, cells = footprint.shape
    half = flux.shape[2] // 2
    rows = slots // CHUNKS
    core_at = lax.axis_index("core")
    core = core_at.astype(jnp.int32)[None]
    valid = (jnp.arange(slots, dtype=jnp.int32) < obs_count[0]).astype(jnp.float32)
    row_scale = (valid * obs_weight[0])[:, None]
    later = range(1, lags)

    def whole(block):
        return pl.BlockSpec((rows, cells), lambda j, c: (block, 0))

    def column(block):
        return lambda tile: pl.BlockSpec((rows, tile), lambda j, c: (block, j))

    own = [[shifted(footprint[0, lag, :rows], -lag) for lag in later]]
    flux_sent = lax.dynamic_slice_in_dim(flux[0], (1 - core_at) * half, half, 1)
    if half == cells and cells % rows == 0:
        flux_other = foot_other = swapped(jnp.concatenate([flux_sent, footprint[0, 0]], axis=0))
        foot_at = cells // rows
    else:
        flux_other, foot_other = swapped(flux_sent), swapped(footprint[0, 0])
        foot_at = 0
    chunks = range(CHUNKS)
    same = forward(
        [footprint] * CHUNKS,
        [pl.BlockSpec((1, 1, rows, cells), lambda j, c, r=r: (0, 0, r, 0)) for r in chunks],
        [foot_other] * CHUNKS,
        [whole(foot_at + r) for r in chunks],
        rows, flux, flux_other, cells, half, core,
    )
    own_specs = [whole(0)] * len(later)
    other_specs = [whole(i) for i in range(len(later))]

    partial, other, weighted = [], [], []
    for r in chunks:
        if r > 0:
            pieces = []
            for lag in later:
                piece = footprint[0, lag, r * rows:(r + 1) * rows]
                if r == 1:
                    piece, same[0] = together(piece, same[0])
                else:
                    piece, gathered[lag - 1] = together(piece, gathered[lag - 1])
                pieces.append(shifted(piece, -lag))
            own.append(pieces)
            if r > 1:
                own[r][0], weighted[r - 2] = together(own[r][0], weighted[r - 2])
            gathered = [shifted(terms[lag - 1], lag) for lag in later]
            for i in range(len(later)):
                own[r][i], gathered[i] = together(own[r][i], gathered[i])
            partial.append(combine(row_scale, same[r - 1], gathered, r - 1))
            own[r][0], partial[r - 1] = together(own[r][0], partial[r - 1])
            if r > 1:
                partial[r - 1], weighted[r - 2] = together(partial[r - 1], weighted[r - 2])
            weighted.append(lax.psum(partial[r - 1], "z"))
        else:
            own[r][0], same[0] = together(own[r][0], same[0])
        other.append(swapped(jnp.concatenate(own[r], axis=0)))
        terms = forward(
            own[r], own_specs, [other[r]] * len(later), other_specs,
            rows, flux, flux_other, cells, half, core,
        )
    gathered = [shifted(terms[lag - 1], lag) for lag in later]
    partial.append(combine(row_scale, same[r], gathered, r))
    partial[r], weighted[r - 1] = together(partial[r], weighted[r - 1])
    weighted.append(lax.psum(partial[r], "z"))

    sent = []
    for r in chunks:
        if r > 0:
            for i in range(len(later)):
                weighted[r], sent[r - 1][i] = together(weighted[r], sent[r - 1][i])
        sent.append([shifted(weighted[r], -lag) for lag in later])
    mine, theirs = None, None
    for r in chunks:
        here = [weighted[r], *sent[r]]
        if r + 1 < CHUNKS:
            here[0], _ = together(here[0], weighted[r + 1])

        def own_rows(tile, r=r):
            return pl.BlockSpec((1, 1, rows, tile), lambda j, c: (0, 0, r, j))

        theirs = adjoint(
            [foot_other] + [other[r]] * len(later),
            [column(foot_at + r)] + [column(i) for i in range(len(later))],
            here, theirs, (cells, half), False, core, cells,
        )
        mine = adjoint(
            [footprint, *own[r]], [own_rows] + [column(0)] * len(later),
            here, mine, (cells, 2 * half), True, core, cells,
        )
    return paste(swapped(theirs), mine, core)[None]


def solution(mesh):
    devices = mesh.devices
    split = Mesh(devices.reshape(devices.shape[0], devices.shape[1] // 2, 2), ("tm", "z", "core"))
    cells = ("z", "core")
    placed = (P("tm", None, None, cells), P("tm", cells, None), P("tm", None), P("tm"))
    return jax.shard_map(
        on_device, mesh=split, in_specs=placed, out_specs=P("tm", cells, None), check_vma=False
    )
```

time: 637 us -> 507 us (0.80); the launches traced: 624 us -> 504 us
  matrix products: 171 us -> 0 us
  Pallas kernels: 0 us -> 152 us
  waiting for transfers between devices: 362 us -> 227 us
  starting transfers between devices: 30.9 us -> 77 us
  local copies, waits for them, and re-layouts: 29.3 us -> 20.1 us
    dot_general x26 -> x0, matrix products: 171 us -> none  [the longest x10 102 us: product(): jnp.dot(left, right, precision=lax.Precision.HIGH, preferred_element_type...]
    pallas_call x0 -> x14, Pallas kernels: none -> 152 us  [the longest x6 71.4 us: adjoint(): pl.pallas_call(functools.partial(adjoint_kernel, count, first), grid_spec...]
    ppermute x13 -> x27, waiting for transfers between devices: 244 us -> 136 us  [shifted(): return lax.ppermute(value, 'tm', pairs)]
    ppermute x13 -> x27, starting transfers between devices: 22.7 us -> 73.9 us  [shifted(): return lax.ppermute(value, 'tm', pairs)]
    psum x2 -> x3, waiting for transfers between devices: 118 us -> 78.2 us  [the longest x1 47.4 us: on_device(): weighted.append(lax.psum(partial[r], 'z'))]
    ppermute x7 -> x5, waiting for transfers between devices: 0.02 us -> 12.6 us  [swapped(): return lax.ppermute(value, 'core', [(0, 1), (1, 0)])]
    concatenate x0 -> x4, other arithmetic: none -> 12.4 us  [the longest x1 6.82 us: on_device(): jnp.concatenate([flux_sent, footprint[0, 0]], axis=0)]
    broadcast_in_dim x1 -> x0, local copies, waits for them, and re-layouts: 9.12 us -> none  [on_device(): return jnp.concatenate([first, second], axis=1)[None]]
  transfers between devices with their start and end apart: 22 -> 35, of which waited for: 8 -> 16; matrix products, arithmetic and copies ran while one was open for 30% -> 1% of each run, Pallas kernels for 0% -> 22%
where the time goes in v2:
time: 507 us; the launch traced here: 504 us
  waiting for transfers between devices  227 us (45%)
  Pallas kernels  152 us (30%)
  starting transfers between devices  77 us (15%)
  local copies, waits for them, and re-layouts  20.1 us (4%)
  between operations  14.1 us (3%)
  other arithmetic  13.1 us (3%)
    ppermute x27, waiting for transfers between devices, shifted(): return lax.ppermute(value, 'tm', pairs)  136 us
    ppermute x27, starting transfers between devices, shifted(): return lax.ppermute(value, 'tm', pairs)  73.9 us
    pallas_call x6, Pallas kernels, adjoint(): pl.pallas_call(functools.partial(adjoint_kernel, count, first), grid_spec...  71.4 us
    pallas_call x4, Pallas kernels, forward(): pl.pallas_call(functools.partial(forward_kernel, count), grid_spec=pltpu....  62.8 us
    psum x1, waiting for transfers between devices, on_device(): weighted.append(lax.psum(partial[r], 'z'))  47.4 us
    psum x2, waiting for transfers between devices, on_device(): weighted.append(lax.psum(partial[r - 1], 'z'))  30.8 us
    pallas_call x3, Pallas kernels, combine(): pl.pallas_call(combine_kernel, grid=(half // tile,), in_specs=[pl.BlockSp...  13.2 us
    ppermute x5, waiting for transfers between devices, swapped(): return lax.ppermute(value, 'core', [(0, 1), (1, 0)])  12.6 us
  transfers between devices with their start and end apart: 35, of which 16 were waited for; matrix products, arithmetic and copies ran while one was open for 1% of the time, Pallas kernels for 22%

profile of v2, /device:TPU:3, one launch (start us, length us, event | category | flops | bytes accessed | tf_op | source)
XLA Modules:
  0.0 503.5 jit_solution(10304074311076908163)
XLA Ops:
  6.5 3.9 slice_bitcast_fusion
  10.5 2.7 dynamic-slice_bitcast_fusion
  13.1 6.8 %pad_maximum_fusion = f32[1792,1024]{1,0:T(8,128)} fusion(f32[768,1024]{1,0:T(8,128)} %slice_bitcast_fusion, f32[1024,1024]{1,0:T(8,128)S(1)} %dynamic-slice_bitcast_fusion), kind=kLoop, calls=%fused_computation | loop fusion | flops 1835008 | bytes 14680064 | tf_op jit(solution)/shard_map/concatenate | solution.py:229
  20.6 3.8 slice_bitcast_fusion.9
  24.5 1.9 collective-permute-start.1
  28.4 3.8 collective-permute-done.refs_3_.refs_4_.refs_5_.refs_7_.refs_0_
  32.3 15.6 %shard_map.46 = (f32[256,1024]{1,0:T(8,128)}, f32[256,1024]{1,0:T(8,128)}, f32[256,1024]{1,0:T(8,128)}) custom-call(s32[1]{0:T(128)} %bitcast.core_ref, f32[1,4,768,1024]{3,2,1,0:T(8,128)} %refs_0_.7, f32[1,4,768,1024]{3,2,1,0:T(8,128)} %refs_0_.7, f32[1,4,768,1024]{3,2,1,0:T(8,128)} %refs_0_.7, ...), custom_call_target="tpu_custom_call" | custom-call | flops 9663676416 | bytes 17825792 | tf_op jit(solution)/shard_map/pallas_call | solution.py:75
  47.9 4.4 collective-permute-done.1.refs_0_.refs_1_
  52.3 22.8 %collective-permute-done.3.refs_1_.refs_2_ = f32[256,1024]{1,0:T(8,128)S(1)} collective-permute-done((f32[256,1024]{1,0:T(8,128)}, f32[256,1024]{1,0:T(8,128)S(1)}, u32[]{:S(2)}, u32[]{:S(2)}) %collective-permute-start.3) | collective-permute-done | bytes 1048608 | tf_op jit(solution)/shard_map/ppermute | solution.py:18
  78.0 1.8 collective-permute-start.10
  79.7 3.5 collective-permute-done.5.refs_3_.refs_4_.refs_5_.refs_1_.refs_2_
  84.9 15.7 %shard_map.47 = (f32[256,1024]{1,0:T(8,128)}, f32[256,1024]{1,0:T(8,128)}, f32[256,1024]{1,0:T(8,128)}) custom-call(s32[1]{0:T(128)} %bitcast.core_ref, f32[256,1024]{1,0:T(8,128)} %copy-done.12, f32[256,1024]{1,0:T(8,128)} %copy-done.13, f32[256,1024]{1,0:T(8,128)} %copy-done.14, f32[768,1024]{1,0:T(8,128)} %copy-done, f32[768,1024]{1,0:T(8,128)} %copy-done, ...), custom_call_target="tpu_custom_call" | custom-call | flops 9663676416 | bytes 17825792 | tf_op jit(solution)/shard_map/pallas_call | solution.py:75
  101.4 4.8 collective-permute-start.2
  106.2 1.9 collective-permute-start.6
  109.5 5.1 %collective-permute-start.9 = (f32[256,1024]{1,0:T(8,128)}, f32[256,1024]{1,0:T(8,128)}, u32[]{:S(2)}, u32[]{:S(2)}) collective-permute-start(f32[256,1024]{1,0:T(8,128)} %get-tuple-element.76), channel_id=1, source_target_pairs={{0,16},{8,24},{1,17},{9,25},{2,18},{10,26},{3,19},{11,27},{4,20},{... | collective-permute-start | bytes 3145736 | tf_op jit(solution)/shard_map/ppermute | solution.py:18
  116.2 12.6 %collective-permute-done.2.refs_0_.refs_1_ = f32[256,1024]{1,0:T(8,128)S(1)} collective-permute-done((f32[256,1024]{1,0:T(8,128)}, f32[256,1024]{1,0:T(8,128)S(1)}, u32[]{:S(2)}, u32[]{:S(2)}) %collective-permute-start.2) | collective-permute-done | bytes 1048608 | tf_op jit(solution)/shard_map/ppermute | solution.py:18
  128.8 22.3 %collective-permute-done.6.refs_0_ = f32[256,1024]{1,0:T(8,128)} collective-permute-done((f32[256,1024]{1,0:T(8,128)}, f32[256,1024]{1,0:T(8,128)}, u32[]{:S(2)}, u32[]{:S(2)}) %collective-permute-start.6) | collective-permute-done | bytes 1048608 | tf_op jit(solution)/shard_map/ppermute | solution.py:18
  151.9 4.6 shard_map.48
  156.6 3.2 pad_maximum_fusion.2
  160.3 11.3 %collective-permute-start.7 = (f32[256,1024]{1,0:T(8,128)}, f32[256,1024]{1,0:T(8,128)}, u32[]{:S(2)}, u32[]{:S(2)}) collective-permute-start(f32[256,1024]{1,0:T(8,128)} %get-tuple-element.70), channel_id=1, source_target_pairs={{8,0},{16,8},{24,16},{9,1},{17,9},{25,17},{10,2},{18,10},{26,18},{... | collective-permute-start | bytes 3145736 | tf_op jit(solution)/shard_map/ppermute | solution.py:18
  171.6 1.7 collective-permute-start.16
  175.2 15.6 %shard_map.49 = (f32[256,1024]{1,0:T(8,128)}, f32[256,1024]{1,0:T(8,128)}, f32[256,1024]{1,0:T(8,128)}) custom-call(s32[1]{0:T(128)} %bitcast.core_ref, f32[256,1024]{1,0:T(8,128)} %copy-done.6, f32[256,1024]{1,0:T(8,128)} %copy-done.7, f32[256,1024]{1,0:T(8,128)} %collective-permute-done.10.refs_2_.refs_3_, f32[768,1024]{1,0:T(8,128)} %copy-done.1, ...), custom_call_target="tpu_custom_call" | custom-call | flops 9663676416 | bytes 17825792 | tf_op jit(solution)/shard_map/pallas_call | solution.py:75
  192.9 6.4 %collective-permute-start.15 = (f32[256,1024]{1,0:T(8,128)}, f32[256,1024]{1,0:T(8,128)S(1)}, u32[]{:S(2)}, u32[]{:S(2)}) collective-permute-start(f32[256,1024]{1,0:T(8,128)} %get-tuple-element.91), channel_id=1, source_target_pairs={{0,16},{8,24},{1,17},{9,25},{2,18},{10,26},{3,19},{11,27},{4,20},{... | collective-permute-start | bytes 3145736 | tf_op jit(solution)/shard_map/ppermute | solution.py:18
  199.3 4.9 collective-permute-start.13
  204.2 24.7 %all-reduce.4.cloned.1.call-done.refs_4_ = f32[256,1024]{1,0:T(8,128)} async-done(((f32[256,1024]{1,0:T(8,128)}), f32[256,1024]{1,0:T(8,128)}) %all-reduce.4.cloned.1.call-update) | async-done | bytes 1048592 | tf_op jit(solution)/shard_map/psum | solution.py:266
  229.0 14.2 %collective-permute-done.15.refs_1_ = f32[256,1024]{1,0:T(8,128)S(1)} collective-permute-done((f32[256,1024]{1,0:T(8,128)}, f32[256,1024]{1,0:T(8,128)S(1)}, u32[]{:S(2)}, u32[]{:S(2)}) %collective-permute-start.15) | collective-permute-done | bytes 1048608 | tf_op jit(solution)/shard_map/ppermute | solution.py:18
  244.1 4.2 shard_map.50
  248.4 1.9 pad_maximum_fusion.3
  250.9 5.3 %collective-permute-done.18.refs_3_.refs_4_.refs_5_.refs_1_.refs_2_ = f32[768,1024]{1,0:T(8,128)S(1)} collective-permute-done((f32[768,1024]{1,0:T(8,128)S(1)}, f32[768,1024]{1,0:T(8,128)S(1)}, u32[]{:S(2)}, u32[]{:S(2)}) %collective-permute-start.18) | collective-permute-done | bytes 3145760 | tf_op jit(solution)/shard_map/ppermute | solution.py:22
  257.9 15.8 %shard_map.51 = (f32[256,1024]{1,0:T(8,128)}, f32[256,1024]{1,0:T(8,128)}, f32[256,1024]{1,0:T(8,128)}) custom-call(s32[1]{0:T(128)} %bitcast.core_ref, f32[256,1024]{1,0:T(8,128)} %collective-permute-done.7.refs_0_.refs_1_, f32[256,1024]{1,0:T(8,128)} %copy-done.8, f32[256,1024]{1,0:T(8,128)} %collective-permute-done.16.refs_2_.refs_3_, ...), custom_call_target="tpu_custom_call" | custom-call | flops 9663676416 | bytes 17825792 | tf_op jit(solution)/shard_map/pallas_call | solution.py:75
  273.7 9.3 %collective-permute-start.19 = (f32[256,1024]{1,0:T(8,128)}, f32[256,1024]{1,0:T(8,128)}, u32[]{:S(2)}, u32[]{:S(2)}) collective-permute-start(f32[256,1024]{1,0:T(8,128)} %get-tuple-element.100), channel_id=1, source_target_pairs={{0,8},{8,16},{16,24},{1,9},{9,17},{17,25},{2,10},{10,18},{18,26},{... | collective-permute-start | bytes 3145736 | tf_op jit(solution)/shard_map/ppermute | solution.py:18
  283.0 2.3 collective-permute-start.20
  287.0 3.4 collective-permute-start.22
  291.8 13.8 %collective-permute-done.19.refs_0_ = f32[256,1024]{1,0:T(8,128)} collective-permute-done((f32[256,1024]{1,0:T(8,128)}, f32[256,1024]{1,0:T(8,128)}, u32[]{:S(2)}, u32[]{:S(2)}) %collective-permute-start.19) | collective-permute-done | bytes 1048608 | tf_op jit(solution)/shard_map/ppermute | solution.py:18
  306.3 23.0 %collective-permute-done.20.refs_1_ = f32[256,1024]{1,0:T(8,128)} collective-permute-done((f32[256,1024]{1,0:T(8,128)}, f32[256,1024]{1,0:T(8,128)}, u32[]{:S(2)}, u32[]{:S(2)}) %collective-permute-start.20) | collective-permute-done | bytes 1048608 | tf_op jit(solution)/shard_map/ppermute | solution.py:18
  329.3 4.3 shard_map.52
  333.6 6.1 %all-reduce.6.cloned.1.call-done.refs_4_ = f32[256,1024]{1,0:T(8,128)} async-done(((f32[256,1024]{1,0:T(8,128)}), f32[256,1024]{1,0:T(8,128)}) %all-reduce.6.cloned.1.call-update) | async-done | bytes 1048592 | tf_op jit(solution)/shard_map/psum | solution.py:266
  341.7 2.2 collective-permute-start.25
  345.9 47.4 %all-reduce.8.cloned.1.call-done.refs_4_ = f32[256,1024]{1,0:T(8,128)} async-done(((f32[256,1024]{1,0:T(8,128)}), f32[256,1024]{1,0:T(8,128)}) %all-reduce.8.cloned.1.call-update) | async-done | bytes 1048592 | tf_op jit(solution)/shard_map/psum | solution.py:277
  393.3 2.2 collective-permute-start.28
  398.5 11.6 %shard_map.53.refs_8_ = f32[1024,1024]{1,0:T(8,128)} custom-call(s32[1]{0:T(128)} %bitcast.core_ref, f32[1792,1024]{1,0:T(8,128)} %collective-permute-done.refs_3_.refs_4_.refs_5_.refs_7_.refs_0_, f32[768,1024]{1,0:T(8,128)} %copy-done, f32[768,1024]{1,0:T(8,128)} %copy-done, f32[768,1024]{1,0:T(8,128)} %copy-done, ...), custom_call_target="tpu_custom_call" | custom-call | flops 6442450944 | bytes 16777216 | tf_op jit(solution)/shard_map/pallas_call | solution.py:131
  410.1 12.0 %shard_map.54.refs_8_ = f32[1024,1024]{1,0:T(8,128)} custom-call(s32[1]{0:T(128)} %bitcast.core_ref, f32[1792,1024]{1,0:T(8,128)} %collective-permute-done.refs_3_.refs_4_.refs_5_.refs_7_.refs_0_, f32[768,1024]{1,0:T(8,128)} %copy-done.1, f32[768,1024]{1,0:T(8,128)} %copy-done.1, f32[768,1024]{1,0:T(8,128)} %copy-done.1, ...), custom_call_target="tpu_custom_call", output_to_operand_aliasing={{}: (9, {})} | custom-call | flops 6442450944 | bytes 16777216 | tf_op jit(solution)/shard_map/pallas_call | solution.py:131
  422.1 21.9 %collective-permute-done.29.refs_6_ = f32[256,1024]{1,0:T(8,128)} collective-permute-done((f32[256,1024]{1,0:T(8,128)}, f32[256,1024]{1,0:T(8,128)}, u32[]{:S(2)}, u32[]{:S(2)}) %collective-permute-start.29) | collective-permute-done | bytes 1048608 | tf_op jit(solution)/shard_map/ppermute | solution.py:18
  444.0 12.0 %shard_map.55 = f32[1024,1024]{1,0:T(8,128)} custom-call(s32[1]{0:T(128)} %bitcast.core_ref, f32[1792,1024]{1,0:T(8,128)} %collective-permute-done.refs_3_.refs_4_.refs_5_.refs_7_.refs_0_, f32[768,1024]{1,0:T(8,128)} %copy-done.2, f32[768,1024]{1,0:T(8,128)} %copy-done.2, f32[768,1024]{1,0:T(8,128)} %copy-done.2, ...), custom_call_target="tpu_custom_call", output_to_operand_aliasing={{}: (9, {})} | custom-call | flops 6442450944 | bytes 16777216 | tf_op jit(solution)/shard_map/pallas_call | solution.py:131
  456.5 11.6 %shard_map.56.refs_8_ = f32[1024,2048]{1,0:T(8,128)} custom-call(s32[1]{0:T(128)} %bitcast.core_ref, f32[1,4,768,1024]{3,2,1,0:T(8,128)} %refs_0_.7, f32[256,1024]{1,0:T(8,128)} %copy-done.12, f32[256,1024]{1,0:T(8,128)} %copy-done.13, f32[256,1024]{1,0:T(8,128)} %copy-done.14, f32[256,1024]{1,0:T(8,128)} %all-reduce.4.cloned.1.call-done.refs_4_, ...), custom_call_target="tpu_custom_call" | custom-call | flops 6442450944 | bytes 16777216 | tf_op jit(solution)/shard_map/pallas_call | solution.py:131
  468.1 12.1 %shard_map.57.refs_8_ = f32[1024,2048]{1,0:T(8,128)} custom-call(s32[1]{0:T(128)} %bitcast.core_ref, f32[1,4,768,1024]{3,2,1,0:T(8,128)} %refs_0_.7, f32[256,1024]{1,0:T(8,128)} %copy-done.6, f32[256,1024]{1,0:T(8,128)} %copy-done.7, f32[256,1024]{1,0:T(8,128)} %collective-permute-done.10.refs_2_.refs_3_, ...), custom_call_target="tpu_custom_call", output_to_operand_aliasing={{}: (9, {})} | custom-call | flops 6442450944 | bytes 16777216 | tf_op jit(solution)/shard_map/pallas_call | solution.py:131
  480.2 12.1 %shard_map.58.before = f32[1024,2048]{1,0:T(8,128)} custom-call(s32[1]{0:T(128)} %bitcast.core_ref, f32[1,4,768,1024]{3,2,1,0:T(8,128)} %refs_0_.7, f32[256,1024]{1,0:T(8,128)} %collective-permute-done.7.refs_0_.refs_1_, f32[256,1024]{1,0:T(8,128)} %copy-done.8, f32[256,1024]{1,0:T(8,128)} %collective-permute-done.16.refs_2_.refs_3_, ...), custom_call_target="tpu_custom_call", output_to_operand_aliasing={{}: (9, {})} | custom-call | flops 6442450944 | bytes 16777216 | tf_op jit(solution)/shard_map/pallas_call | solution.py:131
  492.3 4.7 shard_map.59
  (93 shorter events, 29.9 us)
Async XLA Ops:
  6.5 222.4 %all-reduce.4.cloned.1.call-start = ((), (), s32[]{:S(2)}) async-start(), calls=%async_computation | async-start | bytes 2097152 | tf_op jit(solution)/shard_map/psum | solution.py:266
  10.5 10.2 %slice-start = ((s8[12582912]{0:T(1024)(128)(4,1)}), s8[4194304]{0:T(1024)(128)(4,1)S(1)}, s32[]{:S(2)}) async-start(s8[12582912]{0:T(1024)(128)(4,1)} %bitcast.27), calls=%async_computation.3 | async-start | bytes 8388608
  10.5 10.2 %slice-start.1 = ((s8[12582912]{0:T(1024)(128)(4,1)}), s8[4194304]{0:T(1024)(128)(4,1)S(1)}, s32[]{:S(2)}) async-start(s8[12582912]{0:T(1024)(128)(4,1)} %bitcast.27), calls=%async_computation.4 | async-start | bytes 8388608
  13.1 7.5 %slice-start.2 = ((s8[12582912]{0:T(1024)(128)(4,1)}), s8[4194304]{0:T(1024)(128)(4,1)S(1)}, s32[]{:S(2)}) async-start(s8[12582912]{0:T(1024)(128)(4,1)} %bitcast.27), calls=%async_computation.5 | async-start | bytes 8388608
  20.0 12.3 %collective-permute-start = (f32[1792,1024]{1,0:T(8,128)}, f32[1792,1024]{1,0:T(8,128)}, u32[]{:S(2)}, u32[]{:S(2)}) collective-permute-start(f32[1792,1024]{1,0:T(8,128)} %pad_maximum_fusion), channel_id=1, source_target_pairs={{0,1},{1,0},{2,3},{3,2},{4,5},{5,4},{6,7},{7,6},{8,9},{9,8},{10,11... | collective-permute-start | bytes 22020104 | tf_op jit(solution)/shard_map/ppermute | solution.py:22
  24.5 27.8 %collective-permute-start.1 = (f32[256,1024]{1,0:T(8,128)}, f32[256,1024]{1,0:T(8,128)S(1)}, u32[]{:S(2)}, u32[]{:S(2)}) collective-permute-start(f32[256,1024]{1,0:T(8,128)} %get-tuple-element.130), channel_id=1, source_target_pairs={{8,0},{16,8},{24,16},{9,1},{17,9},{25,17},{10,2},{18,10},{26,18},{... | collective-permute-start | bytes 3145736 | tf_op jit(solution)/shard_map/ppermute | solution.py:18
  26.4 48.7 %collective-permute-start.3 = (f32[256,1024]{1,0:T(8,128)}, f32[256,1024]{1,0:T(8,128)S(1)}, u32[]{:S(2)}, u32[]{:S(2)}) collective-permute-start(f32[256,1024]{1,0:T(8,128)} %get-tuple-element.129), channel_id=1, source_target_pairs={{16,0},{24,8},{17,1},{25,9},{18,2},{26,10},{19,3},{27,11},{20,4},{... | collective-permute-start | bytes 3145736 | tf_op jit(solution)/shard_map/ppermute | solution.py:18
  27.7 47.4 %collective-permute-start.4 = (f32[256,1024]{1,0:T(8,128)}, f32[256,1024]{1,0:T(8,128)S(1)}, u32[]{:S(2)}, u32[]{:S(2)}) collective-permute-start(f32[256,1024]{1,0:T(8,128)} %get-tuple-element.128), channel_id=1, source_target_pairs={{24,0},{25,1},{26,2},{27,3},{28,4},{29,5},{30,6},{31,7}} | collective-permute-start | bytes 3145736 | tf_op jit(solution)/shard_map/ppermute | solution.py:18
  52.3 22.8 %copy-start.12 = (f32[256,1024]{1,0:T(8,128)}, f32[256,1024]{1,0:T(8,128)S(1)}, u32[]{:S(2)}) copy-start(f32[256,1024]{1,0:T(8,128)S(1)} %collective-permute-done.1.refs_0_.refs_1_) | copy-start | bytes 3145732
  77.5 5.8 %collective-permute-start.5 = (f32[768,1024]{1,0:T(8,128)S(1)}, f32[768,1024]{1,0:T(8,128)S(1)}, u32[]{:S(2)}, u32[]{:S(2)}) collective-permute-start(f32[768,1024]{1,0:T(8,128)S(1)} %pad_maximum_fusion.1), channel_id=1, source_target_pairs={{0,1},{1,0},{2,3},{3,2},{4,5},{5,4},{6,7},{7,6},{8,9},{9,8},{10,11... | collective-permute-start | bytes 9437192 | tf_op jit(solution)/shard_map/ppermute | solution.py:22
  78.0 36.6 %copy-start.18 = (f32[1,768]{1,0:T(1,128)S(1)}, f32[1,768]{1,0:T(1,128)}, u32[]{:S(2)}) copy-start(f32[1,768]{1,0:T(1,128)} %param.6) | copy-start | bytes 9220
  78.0 31.5 %collective-permute-start.10 = (f32[256,1024]{1,0:T(8,128)}, f32[256,1024]{1,0:T(8,128)}, u32[]{:S(2)}, u32[]{:S(2)}) collective-permute-start(f32[256,1024]{1,0:T(8,128)} %get-tuple-element.78), channel_id=1, source_target_pairs={{24,0},{25,1},{26,2},{27,3},{28,4},{29,5},{30,6},{31,7}} | collective-permute-start | bytes 3145736 | tf_op jit(solution)/shard_map/ppermute | solution.py:18
  100.6 15.6 %collective-permute-start.11 = (f32[256,1024]{1,0:T(8,128)}, f32[256,1024]{1,0:T(8,128)S(1)}, u32[]{:S(2)}, u32[]{:S(2)}) collective-permute-start(f32[256,1024]{1,0:T(8,128)} %get-tuple-element.79), channel_id=1, source_target_pairs={{0,24},{1,25},{2,26},{3,27},{4,28},{5,29},{6,30},{7,31}} | collective-permute-start | bytes 3145736 | tf_op jit(solution)/shard_map/ppermute | solution.py:18
  101.4 27.4 %collective-permute-start.2 = (f32[256,1024]{1,0:T(8,128)}, f32[256,1024]{1,0:T(8,128)S(1)}, u32[]{:S(2)}, u32[]{:S(2)}) collective-permute-start(f32[256,1024]{1,0:T(8,128)} %get-tuple-element.66), channel_id=1, source_target_pairs={{8,0},{16,8},{24,16},{9,1},{17,9},{25,17},{10,2},{18,10},{26,18},{... | collective-permute-start | bytes 3145736 | tf_op jit(solution)/shard_map/ppermute | solution.py:18
  106.2 44.9 %collective-permute-start.6 = (f32[256,1024]{1,0:T(8,128)}, f32[256,1024]{1,0:T(8,128)}, u32[]{:S(2)}, u32[]{:S(2)}) collective-permute-start(f32[256,1024]{1,0:T(8,128)} %get-tuple-element.68), channel_id=1, source_target_pairs={{0,8},{8,16},{16,24},{1,9},{9,17},{17,25},{2,10},{10,18},{18,26},{... | collective-permute-start | bytes 3145736 | tf_op jit(solution)/shard_map/ppermute | solution.py:18
  108.1 43.8 %collective-permute-start.8 = (f32[256,1024]{1,0:T(8,128)}, f32[256,1024]{1,0:T(8,128)S(1)}, u32[]{:S(2)}, u32[]{:S(2)}) collective-permute-start(f32[256,1024]{1,0:T(8,128)} %get-tuple-element.75), channel_id=1, source_target_pairs={{16,0},{24,8},{17,1},{25,9},{18,2},{26,10},{19,3},{27,11},{20,4},{... | collective-permute-start | bytes 3145736 | tf_op jit(solution)/shard_map/ppermute | solution.py:18
  109.5 42.5 %collective-permute-start.9 = (f32[256,1024]{1,0:T(8,128)}, f32[256,1024]{1,0:T(8,128)}, u32[]{:S(2)}, u32[]{:S(2)}) collective-permute-start(f32[256,1024]{1,0:T(8,128)} %get-tuple-element.76), channel_id=1, source_target_pairs={{0,16},{8,24},{1,17},{9,25},{2,18},{10,26},{3,19},{11,27},{4,20},{... | collective-permute-start | bytes 3145736 | tf_op jit(solution)/shard_map/ppermute | solution.py:18
  116.2 35.7 %copy-start.15 = (f32[256,1024]{1,0:T(8,128)}, f32[256,1024]{1,0:T(8,128)S(1)}, u32[]{:S(2)}) copy-start(f32[256,1024]{1,0:T(8,128)S(1)} %collective-permute-done.11.refs_2_) | copy-start | bytes 3145732
  128.8 27.8 %copy-start.6 = (f32[256,1024]{1,0:T(8,128)}, f32[256,1024]{1,0:T(8,128)S(1)}, u32[]{:S(2)}) copy-start(f32[256,1024]{1,0:T(8,128)S(1)} %collective-permute-done.2.refs_0_.refs_1_) | copy-start | bytes 3145732
  151.9 4.7 copy-start.7
  159.8 13.8 %collective-permute-start.12 = (f32[768,1024]{1,0:T(8,128)}, f32[768,1024]{1,0:T(8,128)S(1)}, u32[]{:S(2)}, u32[]{:S(2)}) collective-permute-start(f32[768,1024]{1,0:T(8,128)} %pad_maximum_fusion.2), channel_id=1, source_target_pairs={{0,1},{1,0},{2,3},{3,2},{4,5},{5,4},{6,7},{7,6},{8,9},{9,8},{10,11... | collective-permute-start | bytes 9437192 | tf_op jit(solution)/shard_map/ppermute | solution.py:22
  160.3 39.0 %collective-permute-start.7 = (f32[256,1024]{1,0:T(8,128)}, f32[256,1024]{1,0:T(8,128)}, u32[]{:S(2)}, u32[]{:S(2)}) collective-permute-start(f32[256,1024]{1,0:T(8,128)} %get-tuple-element.70), channel_id=1, source_target_pairs={{8,0},{16,8},{24,16},{9,1},{17,9},{25,17},{10,2},{18,10},{26,18},{... | collective-permute-start | bytes 3145736 | tf_op jit(solution)/shard_map/ppermute | solution.py:18
  171.6 57.4 %collective-permute-start.16 = (f32[256,1024]{1,0:T(8,128)}, f32[256,1024]{1,0:T(8,128)}, u32[]{:S(2)}, u32[]{:S(2)}) collective-permute-start(f32[256,1024]{1,0:T(8,128)} %get-tuple-element.93), channel_id=1, source_target_pairs={{24,0},{25,1},{26,2},{27,3},{28,4},{29,5},{30,6},{31,7}} | collective-permute-start | bytes 3145736 | tf_op jit(solution)/shard_map/ppermute | solution.py:18
  173.3 166.3 %all-reduce.6.cloned.1.call-start = ((), (), s32[]{:S(2)}) async-start(), calls=%async_computation.1 | async-start | bytes 2097152 | tf_op jit(solution)/shard_map/psum | solution.py:266
  190.9 38.0 %collective-permute-start.17 = (f32[256,1024]{1,0:T(8,128)}, f32[256,1024]{1,0:T(8,128)S(1)}, u32[]{:S(2)}, u32[]{:S(2)}) collective-permute-start(f32[256,1024]{1,0:T(8,128)} %get-tuple-element.94), channel_id=1, source_target_pairs={{0,24},{1,25},{2,26},{3,27},{4,28},{5,29},{6,30},{7,31}} | collective-permute-start | bytes 3145736 | tf_op jit(solution)/shard_map/ppermute | solution.py:18
  191.6 37.3 %collective-permute-start.14 = (f32[256,1024]{1,0:T(8,128)}, f32[256,1024]{1,0:T(8,128)S(1)}, u32[]{:S(2)}, u32[]{:S(2)}) collective-permute-start(f32[256,1024]{1,0:T(8,128)} %get-tuple-element.90), channel_id=1, source_target_pairs={{16,0},{24,8},{17,1},{25,9},{18,2},{26,10},{19,3},{27,11},{20,4},{... | collective-permute-start | bytes 3145736 | tf_op jit(solution)/shard_map/ppermute | solution.py:18
  192.9 50.2 %collective-permute-start.15 = (f32[256,1024]{1,0:T(8,128)}, f32[256,1024]{1,0:T(8,128)S(1)}, u32[]{:S(2)}, u32[]{:S(2)}) collective-permute-start(f32[256,1024]{1,0:T(8,128)} %get-tuple-element.91), channel_id=1, source_target_pairs={{0,16},{8,24},{1,17},{9,25},{2,18},{10,26},{3,19},{11,27},{4,20},{... | collective-permute-start | bytes 3145736 | tf_op jit(solution)/shard_map/ppermute | solution.py:18
  199.3 44.3 %collective-permute-start.13 = (f32[256,1024]{1,0:T(8,128)}, f32[256,1024]{1,0:T(8,128)}, u32[]{:S(2)}, u32[]{:S(2)}) collective-permute-start(f32[256,1024]{1,0:T(8,128)} %get-tuple-element.86), channel_id=1, source_target_pairs={{0,8},{8,16},{16,24},{1,9},{9,17},{17,25},{2,10},{10,18},{18,26},{... | collective-permute-start | bytes 3145736 | tf_op jit(solution)/shard_map/ppermute | solution.py:18
  228.9 14.7 %copy-start.16 = (f32[256,1024]{1,0:T(8,128)}, f32[256,1024]{1,0:T(8,128)S(1)}, u32[]{:S(2)}) copy-start(f32[256,1024]{1,0:T(8,128)S(1)} %collective-permute-done.17.refs_2_) | copy-start | bytes 3145732
  228.9 19.4 %copy-start.8 = (f32[256,1024]{1,0:T(8,128)}, f32[256,1024]{1,0:T(8,128)S(1)}, u32[]{:S(2)}) copy-start(f32[256,1024]{1,0:T(8,128)S(1)} %collective-permute-done.14.refs_1_.refs_2_) | copy-start | bytes 3145732
  250.3 5.9 %collective-permute-start.18 = (f32[768,1024]{1,0:T(8,128)S(1)}, f32[768,1024]{1,0:T(8,128)S(1)}, u32[]{:S(2)}, u32[]{:S(2)}) collective-permute-start(f32[768,1024]{1,0:T(8,128)S(1)} %pad_maximum_fusion.3), channel_id=1, source_target_pairs={{0,1},{1,0},{2,3},{3,2},{4,5},{5,4},{6,7},{7,6},{8,9},{9,8},{10,11... | collective-permute-start | bytes 9437192 | tf_op jit(solution)/shard_map/ppermute | solution.py:22
  273.7 31.9 %collective-permute-start.19 = (f32[256,1024]{1,0:T(8,128)}, f32[256,1024]{1,0:T(8,128)}, u32[]{:S(2)}, u32[]{:S(2)}) collective-permute-start(f32[256,1024]{1,0:T(8,128)} %get-tuple-element.100), channel_id=1, source_target_pairs={{0,8},{8,16},{16,24},{1,9},{9,17},{17,25},{2,10},{10,18},{18,26},{... | collective-permute-start | bytes 3145736 | tf_op jit(solution)/shard_map/ppermute | solution.py:18
  283.0 46.3 %collective-permute-start.20 = (f32[256,1024]{1,0:T(8,128)}, f32[256,1024]{1,0:T(8,128)}, u32[]{:S(2)}, u32[]{:S(2)}) collective-permute-start(f32[256,1024]{1,0:T(8,128)} %get-tuple-element.101), channel_id=1, source_target_pairs={{0,16},{8,24},{1,17},{9,25},{2,18},{10,26},{3,19},{11,27},{4,20},{... | collective-permute-start | bytes 3145736 | tf_op jit(solution)/shard_map/ppermute | solution.py:18
  285.3 44.0 %collective-permute-start.21 = (f32[256,1024]{1,0:T(8,128)}, f32[256,1024]{1,0:T(8,128)}, u32[]{:S(2)}, u32[]{:S(2)}) collective-permute-start(f32[256,1024]{1,0:T(8,128)} %get-tuple-element.102), channel_id=1, source_target_pairs={{0,24},{1,25},{2,26},{3,27},{4,28},{5,29},{6,30},{7,31}} | collective-permute-start | bytes 3145736 | tf_op jit(solution)/shard_map/ppermute | solution.py:18
  287.0 106.3 %all-reduce.8.cloned.1.call-start = ((), (), s32[]{:S(2)}) async-start(), calls=%async_computation.2 | async-start | bytes 2097152 | tf_op jit(solution)/shard_map/psum | solution.py:277
  287.0 52.7 %collective-permute-start.22 = (f32[256,1024]{1,0:T(8,128)}, f32[256,1024]{1,0:T(8,128)S(1)}, u32[]{:S(2)}, u32[]{:S(2)}) collective-permute-start(f32[256,1024]{1,0:T(8,128)} %all-reduce.4.cloned.1.call-done.refs_4_), channel_id=1, source_target_pairs={{8,0},{16,8},{24,16},{9,1},{17,9},{25,17},{10,2},{18,10},{26,18},{... | collective-permute-start | bytes 3145736 | tf_op jit(solution)/shard_map/ppermute | solution.py:18
  290.5 49.3 %collective-permute-start.23 = (f32[256,1024]{1,0:T(8,128)}, f32[256,1024]{1,0:T(8,128)S(1)}, u32[]{:S(2)}, u32[]{:S(2)}) collective-permute-start(f32[256,1024]{1,0:T(8,128)} %all-reduce.4.cloned.1.call-done.refs_4_), channel_id=1, source_target_pairs={{16,0},{24,8},{17,1},{25,9},{18,2},{26,10},{19,3},{27,11},{20,4},{... | collective-permute-start | bytes 3145736 | tf_op jit(solution)/shard_map/ppermute | solution.py:18
  305.6 35.1 %collective-permute-start.24 = (f32[256,1024]{1,0:T(8,128)}, f32[256,1024]{1,0:T(8,128)S(1)}, u32[]{:S(2)}, u32[]{:S(2)}) collective-permute-start(f32[256,1024]{1,0:T(8,128)} %all-reduce.4.cloned.1.call-done.refs_4_), channel_id=1, source_target_pairs={{24,0},{25,1},{26,2},{27,3},{28,4},{29,5},{30,6},{31,7}} | collective-permute-start | bytes 3145736 | tf_op jit(solution)/shard_map/ppermute | solution.py:18
  341.7 51.6 %collective-permute-start.25 = (f32[256,1024]{1,0:T(8,128)}, f32[256,1024]{1,0:T(8,128)S(1)}, u32[]{:S(2)}, u32[]{:S(2)}) collective-permute-start(f32[256,1024]{1,0:T(8,128)} %all-reduce.6.cloned.1.call-done.refs_4_), channel_id=1, source_target_pairs={{8,0},{16,8},{24,16},{9,1},{17,9},{25,17},{10,2},{18,10},{26,18},{... | collective-permute-start | bytes 3145736 | tf_op jit(solution)/shard_map/ppermute | solution.py:18
  343.8 49.5 %collective-permute-start.26 = (f32[256,1024]{1,0:T(8,128)}, f32[256,1024]{1,0:T(8,128)S(1)}, u32[]{:S(2)}, u32[]{:S(2)}) collective-permute-start(f32[256,1024]{1,0:T(8,128)} %all-reduce.6.cloned.1.call-done.refs_4_), channel_id=1, source_target_pairs={{16,0},{24,8},{17,1},{25,9},{18,2},{26,10},{19,3},{27,11},{20,4},{... | collective-permute-start | bytes 3145736 | tf_op jit(solution)/shard_map/ppermute | solution.py:18
  345.1 48.2 %collective-permute-start.27 = (f32[256,1024]{1,0:T(8,128)}, f32[256,1024]{1,0:T(8,128)S(1)}, u32[]{:S(2)}, u32[]{:S(2)}) collective-permute-start(f32[256,1024]{1,0:T(8,128)} %all-reduce.6.cloned.1.call-done.refs_4_), channel_id=1, source_target_pairs={{24,0},{25,1},{26,2},{27,3},{28,4},{29,5},{30,6},{31,7}} | collective-permute-start | bytes 3145736 | tf_op jit(solution)/shard_map/ppermute | solution.py:18
  393.3 16.8 %copy-start.3 = (f32[256,1024]{1,0:T(8,128)}, f32[256,1024]{1,0:T(8,128)S(1)}, u32[]{:S(2)}) copy-start(f32[256,1024]{1,0:T(8,128)S(1)} %collective-permute-done.25.refs_5_) | copy-start | bytes 3145732
  393.3 16.8 %copy-start.4 = (f32[256,1024]{1,0:T(8,128)}, f32[256,1024]{1,0:T(8,128)S(1)}, u32[]{:S(2)}) copy-start(f32[256,1024]{1,0:T(8,128)S(1)} %collective-permute-done.26.refs_6_) | copy-start | bytes 3145732
  393.3 16.8 %copy-start.5 = (f32[256,1024]{1,0:T(8,128)}, f32[256,1024]{1,0:T(8,128)S(1)}, u32[]{:S(2)}) copy-start(f32[256,1024]{1,0:T(8,128)S(1)} %collective-permute-done.27.refs_7_) | copy-start | bytes 3145732
  393.3 28.8 %collective-permute-start.28 = (f32[256,1024]{1,0:T(8,128)}, f32[256,1024]{1,0:T(8,128)}, u32[]{:S(2)}, u32[]{:S(2)}) collective-permute-start(f32[256,1024]{1,0:T(8,128)} %all-reduce.8.cloned.1.call-done.refs_4_), channel_id=1, source_target_pairs={{8,0},{16,8},{24,16},{9,1},{17,9},{25,17},{10,2},{18,10},{26,18},{... | collective-permute-start | bytes 3145736 | tf_op jit(solution)/shard_map/ppermute | solution.py:18
  395.5 48.5 %collective-permute-start.29 = (f32[256,1024]{1,0:T(8,128)}, f32[256,1024]{1,0:T(8,128)}, u32[]{:S(2)}, u32[]{:S(2)}) collective-permute-start(f32[256,1024]{1,0:T(8,128)} %all-reduce.8.cloned.1.call-done.refs_4_), channel_id=1, source_target_pairs={{16,0},{24,8},{17,1},{25,9},{18,2},{26,10},{19,3},{27,11},{20,4},{... | collective-permute-start | bytes 3145736 | tf_op jit(solution)/shard_map/ppermute | solution.py:18
  396.8 47.2 %collective-permute-start.30 = (f32[256,1024]{1,0:T(8,128)}, f32[256,1024]{1,0:T(8,128)}, u32[]{:S(2)}, u32[]{:S(2)}) collective-permute-start(f32[256,1024]{1,0:T(8,128)} %all-reduce.8.cloned.1.call-done.refs_4_), channel_id=1, source_target_pairs={{24,0},{25,1},{26,2},{27,3},{28,4},{29,5},{30,6},{31,7}} | collective-permute-start | bytes 3145736 | tf_op jit(solution)/shard_map/ppermute | solution.py:18
  456.0 36.2 %collective-permute-start.31 = (f32[1024,1024]{1,0:T(8,128)}, f32[1024,1024]{1,0:T(8,128)}, u32[]{:S(2)}, u32[]{:S(2)}) collective-permute-start(f32[1024,1024]{1,0:T(8,128)} %shard_map.55), channel_id=1, source_target_pairs={{0,1},{1,0},{2,3},{3,2},{4,5},{5,4},{6,7},{7,6},{8,9},{9,8},{10,11... | collective-permute-start | bytes 12582920 | tf_op jit(solution)/shard_map/ppermute | solution.py:22
  (9 other events, 12.1 us)
Sparse Core Ops, SparseCore 0:
  173.5 55.4 all-reduce.3
  287.1 52.5 all-reduce.5
  342.1 51.1 all-reduce.7

commit v3 on v2

v3 whole, which is shorter than its diff:
```python
import functools

import jax
import jax.numpy as jnp
from jax import lax
from jax.experimental import pallas as pl
from jax.experimental.pallas import tpu as pltpu
from jax.sharding import Mesh, PartitionSpec as P

CHUNKS = 4
TILE = 256
WIDE = 512
LIGHT = pl.CostEstimate(flops=1, bytes_accessed=1, transcendentals=0)
VMEM_LIMIT = 60 * 1024 * 1024


def shifted(value, by):
    devices = lax.axis_size("tm")
    pairs = [(i, i + by) for i in range(devices) if 0 <= i + by < devices]
    return lax.ppermute(value, "tm", pairs)


def swapped(value):
    return lax.ppermute(value, "core", [(0, 1), (1, 0)])


def together(first, second):
    return lax.optimization_barrier((first, second))


def halves(value):
    high = value.astype(jnp.bfloat16)
    low = (value - high.astype(jnp.float32)).astype(jnp.bfloat16)
    return high, low


def times(left, right, dims):
    return lax.dot_general(left, right, (dims, ((), ())), preferred_element_type=jnp.float32)


def forward_kernel(count, core_ref, *refs):
    foot_own, foot_other = refs[:count], refs[count:2 * count]
    flux_own, flux_other = refs[2 * count:2 * count + 2]
    outs = refs[2 * count + 2:3 * count + 2]
    high_ref, low_ref = refs[3 * count + 2:]
    rows, cells = foot_own[0].shape[-2:]

    @pl.when(pl.program_id(0) == 0)
    def _():
        for i in range(count):
            for side, source in ((0, foot_own[i]), (1, foot_other[i])):
                high, low = halves(source[...].reshape(rows, cells))
                at = (pl.ds(i * rows, rows), pl.ds(side * cells, cells))
                high_ref[at] = high
                low_ref[at] = low

    total = None
    for side, source in ((0, flux_own), (1, flux_other)):
        high, low = halves(source[...].reshape(cells, -1))
        at = pl.ds(side * cells, cells)
        dims = ((1,), (0,))
        term = times(high_ref[:, at], high, dims)
        term = term + times(low_ref[:, at], high, dims)
        term = term + times(high_ref[:, at], low, dims)
        total = term if total is None else total + term
    for i in range(count):
        outs[i][...] = total[i * rows:(i + 1) * rows]


def forward(
    foot_own, own_specs, foot_other, other_specs, rows, flux, flux_other, cells, half, core
):
    count = len(foot_own)
    tile = min(WIDE, half)
    steps = half // tile
    outs = pl.pallas_call(
        functools.partial(forward_kernel, count),
        grid_spec=pltpu.PrefetchScalarGridSpec(
            num_scalar_prefetch=1,
            grid=(steps,),
            in_specs=[
                *own_specs,
                *other_specs,
                pl.BlockSpec((1, cells, tile), lambda j, c: (0, 0, c[0] * steps + j)),
                pl.BlockSpec((cells, tile), lambda j, c: (0, j)),
            ],
            out_specs=[pl.BlockSpec((rows, tile), lambda j, c: (0, j))] * count,
            scratch_shapes=[pltpu.VMEM((count * rows, 2 * cells), jnp.bfloat16)] * 2,
        ),
        out_shape=[jax.ShapeDtypeStruct((rows, half), jnp.float32)] * count,
        compiler_params=pltpu.CompilerParams(vmem_limit_bytes=VMEM_LIMIT),
        cost_estimate=LIGHT,
    )(core, *foot_own, *foot_other, flux, flux_other)
    return list(outs)


def adjoint_kernel(count, sides, first, core_ref, *refs):
    weighted, refs = refs[:count], refs[count:]
    foot, refs = refs[:sides * count], refs[sides * count:]
    before, refs = (None, refs) if first else (refs[:sides], refs[sides:])
    outs, (high_ref, low_ref) = refs[:sides], refs[sides:]
    rows, tile = foot[0].shape[-2:]

    @pl.when(pl.program_id(0) == 0)
    def _():
        for i in range(count):
            high, low = halves(weighted[i][...])
            high_ref[pl.ds(i * rows, rows), :] = high
            low_ref[pl.ds(i * rows, rows), :] = low

    for side in range(sides):
        mine = foot[side * count:(side + 1) * count]
        slab = jnp.concatenate([ref[...].reshape(rows, tile) for ref in mine], axis=0)
        high, low = halves(slab)
        dims = ((0,), (0,))
        total = times(high, high_ref[...], dims)
        total = total + times(low, high_ref[...], dims)
        total = total + times(high, low_ref[...], dims)
        if not first:
            total = total + before[side][...]
        outs[side][...] = total


def adjoint(weighted, sides, core, cells):
    count = len(weighted)
    rows, half = weighted[0].shape
    tile = min(TILE, cells)
    first = sides[0][2] is None
    out_specs = []
    for side in sides:
        if side[4]:
            out_specs.append(pl.BlockSpec((tile, half), lambda j, c: (j, c[0])))
        else:
            out_specs.append(pl.BlockSpec((tile, half), lambda j, c: (j, 0)))
    foot = [array for side in sides for array in side[0]]
    earlier = [] if first else [side[2] for side in sides]
    at = 1 + count + len(foot)
    return pl.pallas_call(
        functools.partial(adjoint_kernel, count, len(sides), first),
        grid_spec=pltpu.PrefetchScalarGridSpec(
            num_scalar_prefetch=1,
            grid=(cells // tile,),
            in_specs=[
                *[pl.BlockSpec((rows, half), lambda j, c: (0, 0))] * count,
                *[spec(tile) for side in sides for spec in side[1]],
                *([] if first else out_specs),
            ],
            out_specs=out_specs,
            scratch_shapes=[pltpu.VMEM((count * rows, half), jnp.bfloat16)] * 2,
        ),
        out_shape=[jax.ShapeDtypeStruct((cells, side[3]), jnp.float32) for side in sides],
        input_output_aliases={} if first else {at + i: i for i in range(len(sides))},
        compiler_params=pltpu.CompilerParams(vmem_limit_bytes=VMEM_LIMIT),
        cost_estimate=LIGHT,
    )(core, *weighted, *foot, *earlier)


def cut_kernel(*refs):
    count = len(refs) // 2
    for source, out in zip(refs[:count], refs[count:]):
        out[...] = source[0, 0]


def cut(footprint, later, rows, r):
    cells = footprint.shape[3]
    tile = min(TILE, cells)
    return list(pl.pallas_call(
        cut_kernel,
        grid=(cells // tile,),
        in_specs=[pl.BlockSpec((1, 1, rows, tile), lambda j, lag=lag: (0, lag, r, j)) for lag in later],
        out_specs=[pl.BlockSpec((rows, tile), lambda j: (0, j))] * len(later),
        out_shape=[jax.ShapeDtypeStruct((rows, cells), jnp.float32)] * len(later),
        cost_estimate=LIGHT,
    )(*[footprint] * len(later)))


def pair_kernel(core_ref, flux, foot, out):
    cells = flux.shape[1]
    slots = foot.shape[2]
    out[pl.ds(0, cells), :] = flux[0]
    out[pl.ds(out.shape[0] - slots, slots), :] = foot[0, 0]


def pair(flux, footprint, half, foot_at, core):
    _, _, slots, cells = footprint.shape
    tile = min(TILE, half)
    steps = half // tile
    return pl.pallas_call(
        pair_kernel,
        grid_spec=pltpu.PrefetchScalarGridSpec(
            num_scalar_prefetch=1,
            grid=(steps,),
            in_specs=[
                pl.BlockSpec((1, cells, tile), lambda j, c: (0, 0, (1 - c[0]) * steps + j)),
                pl.BlockSpec((1, 1, slots, tile), lambda j, c: (0, 0, 0, j)),
            ],
            out_specs=pl.BlockSpec((foot_at + slots, tile), lambda j, c: (0, j)),
        ),
        out_shape=jax.ShapeDtypeStruct((foot_at + slots, half), jnp.float32),
        cost_estimate=LIGHT,
    )(core, flux, footprint)


def combine_kernel(scale, same, *refs):
    total = same[...]
    for ref in refs[:-1]:
        total = total + ref[...]
    refs[-1][...] = scale[...] * total


def combine(scale, same, gathered, r):
    rows, half = gathered[0].shape
    tile = min(WIDE, half)
    block = pl.BlockSpec((rows, tile), lambda j: (0, j))
    return pl.pallas_call(
        combine_kernel,
        grid=(half // tile,),
        in_specs=[
            pl.BlockSpec((rows, 1), lambda j: (r, 0)),
            block,
            *[block] * len(gathered),
        ],
        out_specs=block,
        out_shape=jax.ShapeDtypeStruct((rows, half), jnp.float32),
        cost_estimate=LIGHT,
    )(scale, same, *gathered)


def paste_kernel(core_ref, arrived, before, out_ref):
    out_ref[...] = arrived[...]


def paste(arrived, whole, core):
    cells, half = arrived.shape
    tile = min(TILE, cells)
    return pl.pallas_call(
        paste_kernel,
        grid_spec=pltpu.PrefetchScalarGridSpec(
            num_scalar_prefetch=1,
            grid=(cells // tile,),
            in_specs=[
                pl.BlockSpec((tile, half), lambda j, c: (j, 0)),
                pl.BlockSpec(memory_space=pl.ANY),
            ],
            out_specs=pl.BlockSpec((tile, half), lambda j, c: (j, 1 - c[0])),
        ),
        out_shape=jax.ShapeDtypeStruct(whole.shape, jnp.float32),
        input_output_aliases={2: 0},
        cost_estimate=LIGHT,
    )(core, arrived, whole)


def on_device(footprint, flux, obs_weight, obs_count):
    _, lags, slots, cells = footprint.shape
    half = flux.shape[2] // 2
    rows = slots // CHUNKS
    core_at = lax.axis_index("core")
    core = core_at.astype(jnp.int32)[None]
    valid = (jnp.arange(slots, dtype=jnp.int32) < obs_count[0]).astype(jnp.float32)
    row_scale = (valid * obs_weight[0])[:, None]
    later = range(1, lags)

    def whole(block):
        return pl.BlockSpec((rows, cells), lambda j, c: (block, 0))

    def column(block):
        return lambda tile: pl.BlockSpec((rows, tile), lambda j, c: (block, j))

    pieces = cut(footprint, later, rows, 0)
    own = [[shifted(piece, -lag) for piece, lag in zip(pieces, later)]]
    if half == cells:
        foot_at = pl.cdiv(cells, rows)
        after, _ = together(flux, pieces[0])
        flux_other = foot_other = swapped(pair(after, footprint, half, foot_at * rows, core))
    else:
        flux_other = swapped(lax.dynamic_slice_in_dim(flux[0], (1 - core_at) * half, half, 1))
        foot_other = swapped(footprint[0, 0])
        foot_at = 0
    chunks = range(CHUNKS)
    same = forward(
        [footprint] * CHUNKS,
        [pl.BlockSpec((1, 1, rows, cells), lambda j, c, r=r: (0, 0, r, 0)) for r in chunks],
        [foot_other] * CHUNKS,
        [whole(foot_at + r) for r in chunks],
        rows, flux, flux_other, cells, half, core,
    )
    chunk_specs = [whole(0)] * len(later)

    other, terms, weighted = [], [], []

    def gather_up(r):
        arrived = [shifted(terms[r][lag - 1], lag) for lag in later]
        if r > 0:
            same[r], weighted[r - 1] = together(same[r], weighted[r - 1])
        total = combine(row_scale, same[r], arrived, r)
        if r > 0:
            total, weighted[r - 1] = together(total, weighted[r - 1])
        return total

    for r in chunks:
        if r > 0:
            pieces = cut(footprint, later, rows, r)
            for i in range(len(later)):
                pieces[i], own[r - 1][i] = together(pieces[i], own[r - 1][i])
            own.append([shifted(piece, -lag) for piece, lag in zip(pieces, later)])
            for i in range(len(later)):
                own[r][i], terms[r - 1][i] = together(own[r][i], terms[r - 1][i])
        other.append([swapped(value) for value in own[r]])
        if r > 0:
            total = gather_up(r - 1)
            for i in range(len(later)):
                other[r][i], total = together(other[r][i], total)
            weighted.append(lax.psum(total, "z"))
        terms.append(forward(
            own[r], chunk_specs, other[r], chunk_specs,
            rows, flux, flux_other, cells, half, core,
        ))

    def my_side(r, before):
        first = pl.BlockSpec((1, 1, rows, min(TILE, cells)), lambda j, c: (0, 0, r, j))
        specs = [lambda tile: first] + [column(0)] * len(later)
        return [footprint, *own[r]], specs, before, 2 * half, True

    def their_side(r, before):
        specs = [column(foot_at + r)] + [column(0)] * len(later)
        return [foot_other, *other[r]], specs, before, half, False

    def spread(value):
        return [value] + [shifted(value, -lag) for lag in later]

    weighted.append(lax.psum(gather_up(CHUNKS - 1), "z"))
    mine, theirs = None, None
    for r in chunks:
        if r > 1:
            weighted[r], mine = together(weighted[r], mine)
        if r > 0:
            here = spread(weighted[r - 1])
            mine, theirs = adjoint(here, [my_side(r - 1, mine), their_side(r - 1, theirs)], core, cells)
    here = spread(weighted[r])
    (theirs,) = adjoint(here, [their_side(r, theirs)], core, cells)
    (mine,) = adjoint(here, [my_side(r, mine)], core, cells)
    return paste(swapped(theirs), mine, core)[None]


def solution(mesh):
    devices = mesh.devices
    split = Mesh(devices.reshape(devices.shape[0], devices.shape[1] // 2, 2), ("tm", "z", "core"))
    cells = ("z", "core")
    placed = (P("tm", None, None, cells), P("tm", cells, None), P("tm", None), P("tm"))
    return jax.shard_map(
        on_device, mesh=split, in_specs=placed, out_specs=P("tm", cells, None), check_vma=False
    )
```

time: 507 us -> 493 us (0.972)
  waiting for transfers between devices: 227 us -> 201 us
  Pallas kernels: 152 us -> 173 us
  starting transfers between devices: 77 us -> 96.2 us
  local copies, waits for them, and re-layouts: 20.1 us -> 6.06 us
  other arithmetic: 13.1 us -> 0.79 us
    psum x3 -> x4, waiting for transfers between devices: 78.2 us -> 58.2 us  [the longest x3 58.1 us: on_device(): weighted.append(lax.psum(total, 'z'))]
    pallas_call x6 -> x10, Pallas kernels: 71.4 us -> 90 us  [the longest x5 67.3 us: adjoint(): pl.pallas_call(functools.partial(adjoint_kernel, count, len(sides), first...]
    ppermute x5 -> x14, starting transfers between devices: 2.81 us -> 16.8 us  [swapped(): return lax.ppermute(value, 'core', [(0, 1), (1, 0)])]
    ppermute x5 -> x14, waiting for transfers between devices: 12.6 us -> 0.04 us  [swapped(): return lax.ppermute(value, 'core', [(0, 1), (1, 0)])]
    concatenate x4 -> x0, other arithmetic: 12.4 us -> none  [the longest x1 6.82 us: on_device(): jnp.concatenate([flux_sent, footprint[0, 0]], axis=0)]
    squeeze x2 -> x0, local copies, waits for them, and re-layouts: 7.74 us -> none  [the longest x1 3.92 us: on_device(): footprint[0, 0]]
    ppermute x27 -> x36, waiting for transfers between devices: 136 us -> 143 us  [shifted(): return lax.ppermute(value, 'tm', pairs)]
    ppermute x27 -> x36, starting transfers between devices: 73.9 us -> 79.3 us  [shifted(): return lax.ppermute(value, 'tm', pairs)]
  transfers between devices with their start and end apart: 35 -> 54, of which waited for: 16 -> 12; matrix products, arithmetic and copies ran while one was open for 1% -> 0% of each run, Pallas kernels for 22% -> 27%
where the time goes in v3:
time: 493 us; the launch traced here: 492 us
  waiting for transfers between devices  201 us (41%)
  Pallas kernels  173 us (35%)
  starting transfers between devices  96.2 us (20%)
  between operations  14.4 us (3%)
  local copies, waits for them, and re-layouts  6.06 us (1%)
    ppermute x36, waiting for transfers between devices, shifted(): return lax.ppermute(value, 'tm', pairs)  143 us
    ppermute x36, starting transfers between devices, shifted(): return lax.ppermute(value, 'tm', pairs)  79.3 us
    pallas_call x5, Pallas kernels, forward(): pl.pallas_call(functools.partial(forward_kernel, count), grid_spec=pltpu....  67.5 us
    pallas_call x5, Pallas kernels, adjoint(): pl.pallas_call(functools.partial(adjoint_kernel, count, len(sides), first...  67.3 us
    psum x3, waiting for transfers between devices, on_device(): weighted.append(lax.psum(total, 'z'))  58.1 us
    ppermute x14, starting transfers between devices, swapped(): return lax.ppermute(value, 'core', [(0, 1), (1, 0)])  16.8 us
    pallas_call x4, Pallas kernels, cut(): pl.pallas_call(cut_kernel, grid=(cells // tile,), in_specs=[pl.BlockSpec(...  16.1 us
    pallas_call x4, Pallas kernels, combine(): pl.pallas_call(combine_kernel, grid=(half // tile,), in_specs=[pl.BlockSp...  11 us
  transfers between devices with their start and end apart: 54, of which 12 were waited for; matrix products, arithmetic and copies ran while one was open for 0% of the time, Pallas kernels for 27%

profile of v3, /device:TPU:3, one launch (start us, length us, event | category | flops | bytes accessed | tf_op | source)
XLA Modules:
  0.0 491.7 jit_solution(16243852712003806719)
XLA Ops:
  6.5 4.0 shard_map.46
  10.5 6.7 %shard_map.47 = f32[1920,1024]{1,0:T(8,128)} custom-call(s32[1]{0:T(128)} %bitcast.core_ref, f32[1,1024,2048]{2,1,0:T(8,128)} %refs_6_.7, f32[1,4,768,1024]{3,2,1,0:T(8,128)} %refs_4_.7), custom_call_target="tpu_custom_call" | custom-call | flops 1 | bytes 1 | tf_op jit(solution)/shard_map/pallas_call | solution.py:188
  19.9 1.9 collective-permute-start.3
  22.0 34.7 %collective-permute-done.4.refs_1_.refs_6_ = f32[192,1024]{1,0:T(8,128)S(1)} collective-permute-done((f32[192,1024]{1,0:T(8,128)}, f32[192,1024]{1,0:T(8,128)S(1)}, u32[]{:S(2)}, u32[]{:S(2)}) %collective-permute-start.4) | collective-permute-done | bytes 786464 | tf_op jit(solution)/shard_map/ppermute | solution.py:20
  57.5 4.1 shard_map.51
  63.2 1.9 collective-permute-start.9
  66.8 12.8 %shard_map.52 = (f32[192,1024]{1,0:T(8,128)}, f32[192,1024]{1,0:T(8,128)}, f32[192,1024]{1,0:T(8,128)}) custom-call(s32[1]{0:T(128)} %bitcast.core_ref, f32[192,1024]{1,0:T(8,128)} %copy-done.6, f32[192,1024]{1,0:T(8,128)} %copy-done.4, f32[192,1024]{1,0:T(8,128)} %copy-done.3, f32[192,1024]{1,0:T(8,128)} %copy-done.9, ...), custom_call_target="tpu_custom_call" | custom-call | flops 1 | bytes 1 | tf_op jit(solution)/shard_map/pallas_call | solution.py:76
  79.6 20.2 %collective-permute-done.10.refs_1_.refs_6_ = f32[192,1024]{1,0:T(8,128)S(1)} collective-permute-done((f32[192,1024]{1,0:T(8,128)}, f32[192,1024]{1,0:T(8,128)S(1)}, u32[]{:S(2)}, u32[]{:S(2)}) %collective-permute-start.10) | collective-permute-done | bytes 786464 | tf_op jit(solution)/shard_map/ppermute | solution.py:20
  101.2 1.9 collective-permute-start.12
  106.2 11.0 %collective-permute-done.13.refs_1_ = f32[192,1024]{1,0:T(8,128)S(1)} collective-permute-done((f32[192,1024]{1,0:T(8,128)}, f32[192,1024]{1,0:T(8,128)S(1)}, u32[]{:S(2)}, u32[]{:S(2)}) %collective-permute-start.13) | collective-permute-done | bytes 786464 | tf_op jit(solution)/shard_map/ppermute | solution.py:20
  117.2 1.9 collective-permute-start.16
  119.2 4.1 shard_map.50
  124.6 1.9 collective-permute-start.18
  128.1 16.0 %shard_map.48 = (f32[192,1024]{1,0:T(8,128)}, f32[192,1024]{1,0:T(8,128)}, f32[192,1024]{1,0:T(8,128)}, f32[192,1024]{1,0:T(8,128)}) custom-call(s32[1]{0:T(128)} %bitcast.core_ref, f32[1,4,768,1024]{3,2,1,0:T(8,128)} %refs_4_.7, f32[1,4,768,1024]{3,2,1,0:T(8,128)} %refs_4_.7, f32[1,4,768,1024]{3,2,1,0:T(8,128)} %refs_4_.7, f32[1,4,768,1024]{3,2,1,0:T(8,128)} %refs_4_.7, ...), custom_call_target="tpu_custom_call" | custom-call | flops 1 | bytes 1 | tf_op jit(solution)/shard_map/pallas_call | solution.py:76
  145.8 2.7 shard_map.53
  148.5 12.9 %shard_map.54 = (f32[192,1024]{1,0:T(8,128)}, f32[192,1024]{1,0:T(8,128)}, f32[192,1024]{1,0:T(8,128)}) custom-call(s32[1]{0:T(128)} %bitcast.core_ref, f32[192,1024]{1,0:T(8,128)} %copy-done.7, f32[192,1024]{1,0:T(8,128)} %copy-done.5, f32[192,1024]{1,0:T(8,128)} %copy-done.8, f32[192,1024]{1,0:T(8,128)} %collective-permute-done.11.refs_3_.refs_9_, ...), custom_call_target="tpu_custom_call" | custom-call | flops 1 | bytes 1 | tf_op jit(solution)/shard_map/pallas_call | solution.py:76
  161.4 5.0 %collective-permute-start.22 = (f32[192,1024]{1,0:T(8,128)}, f32[192,1024]{1,0:T(8,128)}, u32[]{:S(2)}, u32[]{:S(2)}) collective-permute-start(f32[192,1024]{1,0:T(8,128)} %get-tuple-element.154), channel_id=1, source_target_pairs={{0,16},{8,24},{1,17},{9,25},{2,18},{10,26},{3,19},{11,27},{4,20},{... | collective-permute-start | bytes 2359304 | tf_op jit(solution)/shard_map/ppermute | solution.py:20
  170.0 2.7 collective-permute-start.20
  172.6 7.6 %collective-permute-done.22.refs_1_ = f32[192,1024]{1,0:T(8,128)} collective-permute-done((f32[192,1024]{1,0:T(8,128)}, f32[192,1024]{1,0:T(8,128)}, u32[]{:S(2)}, u32[]{:S(2)}) %collective-permute-start.22) | collective-permute-done | bytes 786464 | tf_op jit(solution)/shard_map/ppermute | solution.py:20
  180.2 3.3 collective-permute-start.25
  183.6 4.0 shard_map.49
  187.6 19.2 %collective-permute-start.29 = (f32[192,1024]{1,0:T(8,128)}, f32[192,1024]{1,0:T(8,128)}, u32[]{:S(2)}, u32[]{:S(2)}) collective-permute-start(f32[192,1024]{1,0:T(8,128)} %get-tuple-element.170), channel_id=1, source_target_pairs={{8,0},{16,8},{24,16},{9,1},{17,9},{25,17},{10,2},{18,10},{26,18},{... | collective-permute-start | bytes 2359304 | tf_op jit(solution)/shard_map/ppermute | solution.py:20
  206.8 9.6 %all-reduce.5.cloned.1.call-done.refs_0_ = f32[192,1024]{1,0:T(8,128)} async-done(((f32[192,1024]{1,0:T(8,128)}), f32[192,1024]{1,0:T(8,128)}) %all-reduce.5.cloned.1.call-update) | async-done | bytes 786448 | tf_op jit(solution)/shard_map/psum | solution.py:313
  217.9 2.7 shard_map.55
  222.9 12.9 %shard_map.56 = (f32[192,1024]{1,0:T(8,128)}, f32[192,1024]{1,0:T(8,128)}, f32[192,1024]{1,0:T(8,128)}) custom-call(s32[1]{0:T(128)} %bitcast.core_ref, f32[192,1024]{1,0:T(8,128)} %copy-done.11, f32[192,1024]{1,0:T(8,128)} %copy-done.10, f32[192,1024]{1,0:T(8,128)} %collective-permute-done.8.refs_2_.refs_7_, f32[192,1024]{1,0:T(8,128)} %copy-done.12, ...), custom_call_target="tpu_custom_call" | custom-call | flops 1 | bytes 1 | tf_op jit(solution)/shard_map/pallas_call | solution.py:76
  235.8 3.8 collective-permute-start.31
  239.7 3.9 collective-permute-done.27.refs_1_.refs_6_
  243.6 2.3 collective-permute-start.32
  248.6 7.8 %collective-permute-done.31.refs_0_ = f32[192,1024]{1,0:T(8,128)} collective-permute-done((f32[192,1024]{1,0:T(8,128)}, f32[192,1024]{1,0:T(8,128)}, u32[]{:S(2)}, u32[]{:S(2)}) %collective-permute-start.31) | collective-permute-done | bytes 786464 | tf_op jit(solution)/shard_map/ppermute | solution.py:20
  258.0 25.3 %all-reduce.7.cloned.1.call-done.refs_0_ = f32[192,1024]{1,0:T(8,128)} async-done(((f32[192,1024]{1,0:T(8,128)}), f32[192,1024]{1,0:T(8,128)}) %all-reduce.7.cloned.1.call-update) | async-done | bytes 786448 | tf_op jit(solution)/shard_map/psum | solution.py:313
  283.3 2.7 shard_map.57
  288.1 12.8 %shard_map.58 = (f32[192,1024]{1,0:T(8,128)}, f32[192,1024]{1,0:T(8,128)}, f32[192,1024]{1,0:T(8,128)}) custom-call(s32[1]{0:T(128)} %bitcast.core_ref, f32[192,1024]{1,0:T(8,128)} %collective-permute-done.29.refs_0_.refs_5_, f32[192,1024]{1,0:T(8,128)} %copy-done.14, f32[192,1024]{1,0:T(8,128)} %collective-permute-done.17.refs_2_.refs_7_, ...), custom_call_target="tpu_custom_call" | custom-call | flops 1 | bytes 1 | tf_op jit(solution)/shard_map/pallas_call | solution.py:76
  300.9 3.1 collective-permute-start.34
  309.0 12.4 %collective-permute-done.34.refs_0_ = f32[192,1024]{1,0:T(8,128)S(1)} collective-permute-done((f32[192,1024]{1,0:T(8,128)}, f32[192,1024]{1,0:T(8,128)S(1)}, u32[]{:S(2)}, u32[]{:S(2)}) %collective-permute-start.34) | collective-permute-done | bytes 786464 | tf_op jit(solution)/shard_map/ppermute | solution.py:20
  323.3 23.3 %all-reduce.9.cloned.1.call-done.refs_0_ = f32[192,1024]{1,0:T(8,128)} async-done(((f32[192,1024]{1,0:T(8,128)}), f32[192,1024]{1,0:T(8,128)}) %all-reduce.9.cloned.1.call-update) | async-done | bytes 786448 | tf_op jit(solution)/shard_map/psum | solution.py:313
  348.6 2.8 shard_map.59
  351.4 2.8 collective-permute-start.37
  354.2 15.0 %shard_map.60 = (f32[1024,2048]{1,0:T(8,128)}, f32[1024,1024]{1,0:T(8,128)}) custom-call(s32[1]{0:T(128)} %bitcast.core_ref, f32[192,1024]{1,0:T(8,128)} %all-reduce.5.cloned.1.call-done.refs_0_, f32[192,1024]{1,0:T(8,128)} %collective-permute-done.40.refs_1_, f32[192,1024]{1,0:T(8,128)} %collective-permute-done.41.refs_2_, ...), custom_call_target="tpu_custom_call" | custom-call | flops 1 | bytes 1 | tf_op jit(solution)/shard_map/pallas_call | solution.py:138
  372.1 1.9 collective-permute-start.46
  374.0 28.1 %collective-permute-done.38.refs_2_ = f32[192,1024]{1,0:T(8,128)} collective-permute-done((f32[192,1024]{1,0:T(8,128)}, f32[192,1024]{1,0:T(8,128)}, u32[]{:S(2)}, u32[]{:S(2)}) %collective-permute-start.38) | collective-permute-done | bytes 786464 | tf_op jit(solution)/shard_map/ppermute | solution.py:20
  403.0 15.7 %shard_map.61 = (f32[1024,2048]{1,0:T(8,128)}, f32[1024,1024]{1,0:T(8,128)}) custom-call(s32[1]{0:T(128)} %bitcast.core_ref, f32[192,1024]{1,0:T(8,128)} %all-reduce.7.cloned.1.call-done.refs_0_, f32[192,1024]{1,0:T(8,128)} %copy-done.24, f32[192,1024]{1,0:T(8,128)} %collective-permute-done.38.refs_2_, ...), custom_call_target="tpu_custom_call", output_to_operand_aliasing={{0}: (13, {}), {1}: (14, {})} | custom-call | flops 1 | bytes 1 | tf_op jit(solution)/shard_map/pallas_call | solution.py:138
  420.8 2.2 collective-permute-start.43
  423.0 15.7 %shard_map.62 = (f32[1024,2048]{1,0:T(8,128)}, f32[1024,1024]{1,0:T(8,128)}) custom-call(s32[1]{0:T(128)} %bitcast.core_ref, f32[192,1024]{1,0:T(8,128)} %all-reduce.9.cloned.1.call-done.refs_0_, f32[192,1024]{1,0:T(8,128)} %collective-permute-done.46.refs_1_, ...), custom_call_target="tpu_custom_call", output_to_operand_aliasing={{0}: (13, {}), {1}: (14, {})} | custom-call | flops 1 | bytes 1 | tf_op jit(solution)/shard_map/pallas_call | solution.py:138
  438.8 16.9 %collective-permute-done.44.refs_2_ = f32[192,1024]{1,0:T(8,128)S(1)} collective-permute-done((f32[192,1024]{1,0:T(8,128)}, f32[192,1024]{1,0:T(8,128)S(1)}, u32[]{:S(2)}, u32[]{:S(2)}) %collective-permute-start.44) | collective-permute-done | bytes 786464 | tf_op jit(solution)/shard_map/ppermute | solution.py:20
  456.8 10.4 %shard_map.63 = f32[1024,1024]{1,0:T(8,128)} custom-call(s32[1]{0:T(128)} %bitcast.core_ref, f32[192,1024]{1,0:T(8,128)} %all-reduce.11.cloned.1.call-done.refs_0_, f32[192,1024]{1,0:T(8,128)} %copy-done.17, f32[192,1024]{1,0:T(8,128)} %copy-done.16, f32[192,1024]{1,0:T(8,128)} %copy-done.15, ...), custom_call_target="tpu_custom_call", output_to_operand_aliasing={{}: (9, {})} | custom-call | flops 1 | bytes 1 | tf_op jit(solution)/shard_map/pallas_call | solution.py:138
  467.3 2.8 collective-permute-start.49
  470.1 10.4 %shard_map.64.before = f32[1024,2048]{1,0:T(8,128)} custom-call(s32[1]{0:T(128)} %bitcast.core_ref, f32[192,1024]{1,0:T(8,128)} %all-reduce.11.cloned.1.call-done.refs_0_, f32[192,1024]{1,0:T(8,128)} %copy-done.17, f32[192,1024]{1,0:T(8,128)} %copy-done.16, f32[192,1024]{1,0:T(8,128)} %copy-done.15, ...), custom_call_target="tpu_custom_call", output_to_operand_aliasing={{}: (9, {})} | custom-call | flops 1 | bytes 1 | tf_op jit(solution)/shard_map/pallas_call | solution.py:138
  480.4 4.7 shard_map.65
  (140 shorter events, 44.7 us)
Async XLA Ops:
  6.5 209.8 %all-reduce.5.cloned.1.call-start = ((), (), s32[]{:S(2)}) async-start(), calls=%async_computation | async-start | bytes 1572864 | tf_op jit(solution)/shard_map/psum | solution.py:313
  17.2 49.6 %collective-permute-start = (f32[1920,1024]{1,0:T(8,128)}, f32[1920,1024]{1,0:T(8,128)}, u32[]{:S(2)}, u32[]{:S(2)}) collective-permute-start(f32[1920,1024]{1,0:T(8,128)} %shard_map.47), channel_id=1, source_target_pairs={{0,1},{1,0},{2,3},{3,2},{4,5},{5,4},{6,7},{7,6},{8,9},{9,8},{10,11... | collective-permute-start | bytes 23592968 | tf_op jit(solution)/shard_map/ppermute | solution.py:24
  18.6 38.1 %collective-permute-start.4 = (f32[192,1024]{1,0:T(8,128)}, f32[192,1024]{1,0:T(8,128)S(1)}, u32[]{:S(2)}, u32[]{:S(2)}) collective-permute-start(f32[192,1024]{1,0:T(8,128)} %get-tuple-element.118), channel_id=1, source_target_pairs={{16,0},{24,8},{17,1},{25,9},{18,2},{26,10},{19,3},{27,11},{20,4},{... | collective-permute-start | bytes 2359304 | tf_op jit(solution)/shard_map/ppermute | solution.py:20
  19.9 41.7 %collective-permute-start.3 = (f32[192,1024]{1,0:T(8,128)S(1)}, f32[192,1024]{1,0:T(8,128)S(1)}, u32[]{:S(2)}, u32[]{:S(2)}) collective-permute-start(f32[192,1024]{1,0:T(8,128)S(1)} %copy-done.26), channel_id=1, source_target_pairs={{8,0},{16,8},{24,16},{9,1},{17,9},{25,17},{10,2},{18,10},{26,18},{... | collective-permute-start | bytes 2359304 | tf_op jit(solution)/shard_map/ppermute | solution.py:20
  21.8 41.4 %collective-permute-start.7 = (f32[192,1024]{1,0:T(8,128)S(1)}, f32[192,1024]{1,0:T(8,128)}, u32[]{:S(2)}, u32[]{:S(2)}) collective-permute-start(f32[192,1024]{1,0:T(8,128)S(1)} %collective-permute-done.1.refs_2_.refs_7_), channel_id=1, source_target_pairs={{0,1},{1,0},{2,3},{3,2},{4,5},{5,4},{6,7},{7,6},{8,9},{9,8},{10,11... | collective-permute-start | bytes 2359304 | tf_op jit(solution)/shard_map/ppermute | solution.py:24
  61.9 37.9 %collective-permute-start.10 = (f32[192,1024]{1,0:T(8,128)}, f32[192,1024]{1,0:T(8,128)S(1)}, u32[]{:S(2)}, u32[]{:S(2)}) collective-permute-start(f32[192,1024]{1,0:T(8,128)} %get-tuple-element.127), channel_id=1, source_target_pairs={{16,0},{24,8},{17,1},{25,9},{18,2},{26,10},{19,3},{27,11},{20,4},{... | collective-permute-start | bytes 2359304 | tf_op jit(solution)/shard_map/ppermute | solution.py:20
  63.2 37.9 %collective-permute-start.9 = (f32[192,1024]{1,0:T(8,128)}, f32[192,1024]{1,0:T(8,128)S(1)}, u32[]{:S(2)}, u32[]{:S(2)}) collective-permute-start(f32[192,1024]{1,0:T(8,128)} %get-tuple-element.123), channel_id=1, source_target_pairs={{8,0},{16,8},{24,16},{9,1},{17,9},{25,17},{10,2},{18,10},{26,18},{... | collective-permute-start | bytes 2359304 | tf_op jit(solution)/shard_map/ppermute | solution.py:20
  65.2 39.3 %collective-permute-start.2 = (f32[192,1024]{1,0:T(8,128)}, f32[192,1024]{1,0:T(8,128)S(1)}, u32[]{:S(2)}, u32[]{:S(2)}) collective-permute-start(f32[192,1024]{1,0:T(8,128)} %get-tuple-element.117), channel_id=1, source_target_pairs={{24,0},{25,1},{26,2},{27,3},{28,4},{29,5},{30,6},{31,7}} | collective-permute-start | bytes 2359304 | tf_op jit(solution)/shard_map/ppermute | solution.py:20
  101.2 22.1 %collective-permute-start.12 = (f32[192,1024]{1,0:T(8,128)}, f32[192,1024]{1,0:T(8,128)}, u32[]{:S(2)}, u32[]{:S(2)}) collective-permute-start(f32[192,1024]{1,0:T(8,128)} %get-tuple-element.131), channel_id=1, source_target_pairs={{0,8},{8,16},{16,24},{1,9},{9,17},{17,25},{2,10},{10,18},{18,26},{... | collective-permute-start | bytes 2359304 | tf_op jit(solution)/shard_map/ppermute | solution.py:20
  103.1 21.5 %collective-permute-start.11 = (f32[192,1024]{1,0:T(8,128)S(1)}, f32[192,1024]{1,0:T(8,128)}, u32[]{:S(2)}, u32[]{:S(2)}) collective-permute-start(f32[192,1024]{1,0:T(8,128)S(1)} %collective-permute-done.9.refs_0_.refs_5_), channel_id=1, source_target_pairs={{0,1},{1,0},{2,3},{3,2},{4,5},{5,4},{6,7},{7,6},{8,9},{9,8},{10,11... | collective-permute-start | bytes 2359304 | tf_op jit(solution)/shard_map/ppermute | solution.py:24
  104.5 39.7 %collective-permute-start.14 = (f32[192,1024]{1,0:T(8,128)}, f32[192,1024]{1,0:T(8,128)}, u32[]{:S(2)}, u32[]{:S(2)}) collective-permute-start(f32[192,1024]{1,0:T(8,128)} %get-tuple-element.133), channel_id=1, source_target_pairs={{0,24},{1,25},{2,26},{3,27},{4,28},{5,29},{6,30},{7,31}} | collective-permute-start | bytes 2359304 | tf_op jit(solution)/shard_map/ppermute | solution.py:20
  106.1 42.3 %collective-permute-start.15 = (f32[192,1024]{1,0:T(8,128)S(1)}, f32[192,1024]{1,0:T(8,128)}, u32[]{:S(2)}, u32[]{:S(2)}) collective-permute-start(f32[192,1024]{1,0:T(8,128)S(1)} %collective-permute-done.10.refs_1_.refs_6_), channel_id=1, source_target_pairs={{0,1},{1,0},{2,3},{3,2},{4,5},{5,4},{6,7},{7,6},{8,9},{9,8},{10,11... | collective-permute-start | bytes 2359304 | tf_op jit(solution)/shard_map/ppermute | solution.py:24
  117.2 31.3 %collective-permute-start.16 = (f32[192,1024]{1,0:T(8,128)S(1)}, f32[192,1024]{1,0:T(8,128)}, u32[]{:S(2)}, u32[]{:S(2)}) collective-permute-start(f32[192,1024]{1,0:T(8,128)S(1)} %collective-permute-done.2.refs_2_.refs_7_), channel_id=1, source_target_pairs={{0,1},{1,0},{2,3},{3,2},{4,5},{5,4},{6,7},{7,6},{8,9},{9,8},{10,11... | collective-permute-start | bytes 2359304 | tf_op jit(solution)/shard_map/ppermute | solution.py:24
  123.3 38.1 %collective-permute-start.19 = (f32[192,1024]{1,0:T(8,128)}, f32[192,1024]{1,0:T(8,128)S(1)}, u32[]{:S(2)}, u32[]{:S(2)}) collective-permute-start(f32[192,1024]{1,0:T(8,128)} %get-tuple-element.147), channel_id=1, source_target_pairs={{16,0},{24,8},{17,1},{25,9},{18,2},{26,10},{19,3},{27,11},{20,4},{... | collective-permute-start | bytes 2359304 | tf_op jit(solution)/shard_map/ppermute | solution.py:20
  124.6 41.8 %collective-permute-start.18 = (f32[192,1024]{1,0:T(8,128)}, f32[192,1024]{1,0:T(8,128)S(1)}, u32[]{:S(2)}, u32[]{:S(2)}) collective-permute-start(f32[192,1024]{1,0:T(8,128)} %get-tuple-element.143), channel_id=1, source_target_pairs={{8,0},{16,8},{24,16},{9,1},{17,9},{25,17},{10,2},{18,10},{26,18},{... | collective-permute-start | bytes 2359304 | tf_op jit(solution)/shard_map/ppermute | solution.py:20
  144.2 24.2 %collective-permute-start.8 = (f32[192,1024]{1,0:T(8,128)}, f32[192,1024]{1,0:T(8,128)}, u32[]{:S(2)}, u32[]{:S(2)}) collective-permute-start(f32[192,1024]{1,0:T(8,128)} %get-tuple-element.121), channel_id=1, source_target_pairs={{24,0},{25,1},{26,2},{27,3},{28,4},{29,5},{30,6},{31,7}} | collective-permute-start | bytes 2359304 | tf_op jit(solution)/shard_map/ppermute | solution.py:20
  166.4 21.2 %collective-permute-start.21 = (f32[192,1024]{1,0:T(8,128)}, f32[192,1024]{1,0:T(8,128)}, u32[]{:S(2)}, u32[]{:S(2)}) collective-permute-start(f32[192,1024]{1,0:T(8,128)} %get-tuple-element.153), channel_id=1, source_target_pairs={{0,8},{8,16},{16,24},{1,9},{9,17},{17,25},{2,10},{10,18},{18,26},{... | collective-permute-start | bytes 2359304 | tf_op jit(solution)/shard_map/ppermute | solution.py:20
  168.3 115.0 %all-reduce.7.cloned.1.call-start = ((), (), s32[]{:S(2)}) async-start(), calls=%async_computation.1 | async-start | bytes 1572864 | tf_op jit(solution)/shard_map/psum | solution.py:313
  168.4 48.0 %collective-permute-start.23 = (f32[192,1024]{1,0:T(8,128)}, f32[192,1024]{1,0:T(8,128)}, u32[]{:S(2)}, u32[]{:S(2)}) collective-permute-start(f32[192,1024]{1,0:T(8,128)} %get-tuple-element.155), channel_id=1, source_target_pairs={{0,24},{1,25},{2,26},{3,27},{4,28},{5,29},{6,30},{7,31}} | collective-permute-start | bytes 2359304 | tf_op jit(solution)/shard_map/ppermute | solution.py:20
  170.0 50.7 %collective-permute-start.20 = (f32[192,1024]{1,0:T(8,128)S(1)}, f32[192,1024]{1,0:T(8,128)S(1)}, u32[]{:S(2)}, u32[]{:S(2)}) collective-permute-start(f32[192,1024]{1,0:T(8,128)S(1)} %collective-permute-done.18.refs_0_.refs_5_), channel_id=1, source_target_pairs={{0,1},{1,0},{2,3},{3,2},{4,5},{5,4},{6,7},{7,6},{8,9},{9,8},{10,11... | collective-permute-start | bytes 2359304 | tf_op jit(solution)/shard_map/ppermute | solution.py:24
  172.6 49.4 %collective-permute-start.24 = (f32[192,1024]{1,0:T(8,128)S(1)}, f32[192,1024]{1,0:T(8,128)S(1)}, u32[]{:S(2)}, u32[]{:S(2)}) collective-permute-start(f32[192,1024]{1,0:T(8,128)S(1)} %collective-permute-done.19.refs_1_.refs_6_), channel_id=1, source_target_pairs={{0,1},{1,0},{2,3},{3,2},{4,5},{5,4},{6,7},{7,6},{8,9},{9,8},{10,11... | collective-permute-start | bytes 2359304 | tf_op jit(solution)/shard_map/ppermute | solution.py:24
  180.2 41.8 %collective-permute-start.25 = (f32[192,1024]{1,0:T(8,128)}, f32[192,1024]{1,0:T(8,128)}, u32[]{:S(2)}, u32[]{:S(2)}) collective-permute-start(f32[192,1024]{1,0:T(8,128)} %collective-permute-done.8.refs_2_.refs_7_), channel_id=1, source_target_pairs={{0,1},{1,0},{2,3},{3,2},{4,5},{5,4},{6,7},{7,6},{8,9},{9,8},{10,11... | collective-permute-start | bytes 2359304 | tf_op jit(solution)/shard_map/ppermute | solution.py:24
  187.6 48.3 %collective-permute-start.29 = (f32[192,1024]{1,0:T(8,128)}, f32[192,1024]{1,0:T(8,128)}, u32[]{:S(2)}, u32[]{:S(2)}) collective-permute-start(f32[192,1024]{1,0:T(8,128)} %get-tuple-element.170), channel_id=1, source_target_pairs={{8,0},{16,8},{24,16},{9,1},{17,9},{25,17},{10,2},{18,10},{26,18},{... | collective-permute-start | bytes 2359304 | tf_op jit(solution)/shard_map/ppermute | solution.py:20
  216.4 23.3 %collective-permute-start.17 = (f32[192,1024]{1,0:T(8,128)}, f32[192,1024]{1,0:T(8,128)}, u32[]{:S(2)}, u32[]{:S(2)}) collective-permute-start(f32[192,1024]{1,0:T(8,128)} %get-tuple-element.141), channel_id=1, source_target_pairs={{24,0},{25,1},{26,2},{27,3},{28,4},{29,5},{30,6},{31,7}} | collective-permute-start | bytes 2359304 | tf_op jit(solution)/shard_map/ppermute | solution.py:20
  220.7 22.9 %collective-permute-start.27 = (f32[192,1024]{1,0:T(8,128)}, f32[192,1024]{1,0:T(8,128)S(1)}, u32[]{:S(2)}, u32[]{:S(2)}) collective-permute-start(f32[192,1024]{1,0:T(8,128)} %get-tuple-element.166), channel_id=1, source_target_pairs={{16,0},{24,8},{17,1},{25,9},{18,2},{26,10},{19,3},{27,11},{20,4},{... | collective-permute-start | bytes 2359304 | tf_op jit(solution)/shard_map/ppermute | solution.py:20
  235.8 20.5 %collective-permute-start.31 = (f32[192,1024]{1,0:T(8,128)}, f32[192,1024]{1,0:T(8,128)}, u32[]{:S(2)}, u32[]{:S(2)}) collective-permute-start(f32[192,1024]{1,0:T(8,128)} %get-tuple-element.176), channel_id=1, source_target_pairs={{0,8},{8,16},{16,24},{1,9},{9,17},{17,25},{2,10},{10,18},{18,26},{... | collective-permute-start | bytes 2359304 | tf_op jit(solution)/shard_map/ppermute | solution.py:20
  239.6 106.9 %all-reduce.9.cloned.1.call-start = ((), (), s32[]{:S(2)}) async-start(), calls=%async_computation.2 | async-start | bytes 1572864 | tf_op jit(solution)/shard_map/psum | solution.py:313
  243.6 39.7 %collective-permute-start.32 = (f32[192,1024]{1,0:T(8,128)}, f32[192,1024]{1,0:T(8,128)}, u32[]{:S(2)}, u32[]{:S(2)}) collective-permute-start(f32[192,1024]{1,0:T(8,128)} %get-tuple-element.177), channel_id=1, source_target_pairs={{0,16},{8,24},{1,17},{9,25},{2,18},{10,26},{3,19},{11,27},{4,20},{... | collective-permute-start | bytes 2359304 | tf_op jit(solution)/shard_map/ppermute | solution.py:20
  245.9 37.4 %collective-permute-start.33 = (f32[192,1024]{1,0:T(8,128)}, f32[192,1024]{1,0:T(8,128)}, u32[]{:S(2)}, u32[]{:S(2)}) collective-permute-start(f32[192,1024]{1,0:T(8,128)} %get-tuple-element.178), channel_id=1, source_target_pairs={{0,24},{1,25},{2,26},{3,27},{4,28},{5,29},{6,30},{7,31}} | collective-permute-start | bytes 2359304 | tf_op jit(solution)/shard_map/ppermute | solution.py:20
  247.5 38.6 %collective-permute-start.30 = (f32[192,1024]{1,0:T(8,128)}, f32[192,1024]{1,0:T(8,128)S(1)}, u32[]{:S(2)}, u32[]{:S(2)}) collective-permute-start(f32[192,1024]{1,0:T(8,128)} %collective-permute-done.29.refs_0_.refs_5_), channel_id=1, source_target_pairs={{0,1},{1,0},{2,3},{3,2},{4,5},{5,4},{6,7},{7,6},{8,9},{9,8},{10,11... | collective-permute-start | bytes 2359304 | tf_op jit(solution)/shard_map/ppermute | solution.py:24
  248.6 37.5 %collective-permute-start.28 = (f32[192,1024]{1,0:T(8,128)S(1)}, f32[192,1024]{1,0:T(8,128)S(1)}, u32[]{:S(2)}, u32[]{:S(2)}) collective-permute-start(f32[192,1024]{1,0:T(8,128)S(1)} %collective-permute-done.27.refs_1_.refs_6_), channel_id=1, source_target_pairs={{0,1},{1,0},{2,3},{3,2},{4,5},{5,4},{6,7},{7,6},{8,9},{9,8},{10,11... | collective-permute-start | bytes 2359304 | tf_op jit(solution)/shard_map/ppermute | solution.py:24
  256.4 29.7 %collective-permute-start.26 = (f32[192,1024]{1,0:T(8,128)}, f32[192,1024]{1,0:T(8,128)S(1)}, u32[]{:S(2)}, u32[]{:S(2)}) collective-permute-start(f32[192,1024]{1,0:T(8,128)} %collective-permute-done.17.refs_2_.refs_7_), channel_id=1, source_target_pairs={{0,1},{1,0},{2,3},{3,2},{4,5},{5,4},{6,7},{7,6},{8,9},{9,8},{10,11... | collective-permute-start | bytes 2359304 | tf_op jit(solution)/shard_map/ppermute | solution.py:24
  300.9 20.5 %collective-permute-start.34 = (f32[192,1024]{1,0:T(8,128)}, f32[192,1024]{1,0:T(8,128)S(1)}, u32[]{:S(2)}, u32[]{:S(2)}) collective-permute-start(f32[192,1024]{1,0:T(8,128)} %get-tuple-element.188), channel_id=1, source_target_pairs={{0,8},{8,16},{16,24},{1,9},{9,17},{17,25},{2,10},{10,18},{18,26},{... | collective-permute-start | bytes 2359304 | tf_op jit(solution)/shard_map/ppermute | solution.py:20
  304.0 114.8 %all-reduce.11.cloned.1.call-start = ((), (), s32[]{:S(2)}) async-start(), calls=%async_computation.3 | async-start | bytes 1572864 | tf_op jit(solution)/shard_map/psum | solution.py:331
  304.1 42.5 %collective-permute-start.35 = (f32[192,1024]{1,0:T(8,128)}, f32[192,1024]{1,0:T(8,128)S(1)}, u32[]{:S(2)}, u32[]{:S(2)}) collective-permute-start(f32[192,1024]{1,0:T(8,128)} %get-tuple-element.189), channel_id=1, source_target_pairs={{0,16},{8,24},{1,17},{9,25},{2,18},{10,26},{3,19},{11,27},{4,20},{... | collective-permute-start | bytes 2359304 | tf_op jit(solution)/shard_map/ppermute | solution.py:20
  305.4 41.9 %collective-permute-start.36 = (f32[192,1024]{1,0:T(8,128)}, f32[192,1024]{1,0:T(8,128)S(1)}, u32[]{:S(2)}, u32[]{:S(2)}) collective-permute-start(f32[192,1024]{1,0:T(8,128)} %get-tuple-element.190), channel_id=1, source_target_pairs={{0,24},{1,25},{2,26},{3,27},{4,28},{5,29},{6,30},{7,31}} | collective-permute-start | bytes 2359304 | tf_op jit(solution)/shard_map/ppermute | solution.py:20
  306.1 45.3 %collective-permute-start.42 = (f32[192,1024]{1,0:T(8,128)}, f32[192,1024]{1,0:T(8,128)}, u32[]{:S(2)}, u32[]{:S(2)}) collective-permute-start(f32[192,1024]{1,0:T(8,128)} %all-reduce.5.cloned.1.call-done.refs_0_), channel_id=1, source_target_pairs={{24,0},{25,1},{26,2},{27,3},{28,4},{29,5},{30,6},{31,7}} | collective-permute-start | bytes 2359304 | tf_op jit(solution)/shard_map/ppermute | solution.py:20
  307.7 46.5 %collective-permute-start.41 = (f32[192,1024]{1,0:T(8,128)}, f32[192,1024]{1,0:T(8,128)}, u32[]{:S(2)}, u32[]{:S(2)}) collective-permute-start(f32[192,1024]{1,0:T(8,128)} %all-reduce.5.cloned.1.call-done.refs_0_), channel_id=1, source_target_pairs={{16,0},{24,8},{17,1},{25,9},{18,2},{26,10},{19,3},{27,11},{20,4},{... | collective-permute-start | bytes 2359304 | tf_op jit(solution)/shard_map/ppermute | solution.py:20
  321.4 32.8 %collective-permute-start.40 = (f32[192,1024]{1,0:T(8,128)}, f32[192,1024]{1,0:T(8,128)}, u32[]{:S(2)}, u32[]{:S(2)}) collective-permute-start(f32[192,1024]{1,0:T(8,128)} %all-reduce.5.cloned.1.call-done.refs_0_), channel_id=1, source_target_pairs={{8,0},{16,8},{24,16},{9,1},{17,9},{25,17},{10,2},{18,10},{26,18},{... | collective-permute-start | bytes 2359304 | tf_op jit(solution)/shard_map/ppermute | solution.py:20
  346.6 25.5 %collective-permute-start.39 = (f32[192,1024]{1,0:T(8,128)}, f32[192,1024]{1,0:T(8,128)S(1)}, u32[]{:S(2)}, u32[]{:S(2)}) collective-permute-start(f32[192,1024]{1,0:T(8,128)} %all-reduce.7.cloned.1.call-done.refs_0_), channel_id=1, source_target_pairs={{24,0},{25,1},{26,2},{27,3},{28,4},{29,5},{30,6},{31,7}} | collective-permute-start | bytes 2359304 | tf_op jit(solution)/shard_map/ppermute | solution.py:20
  347.3 54.9 %collective-permute-start.38 = (f32[192,1024]{1,0:T(8,128)}, f32[192,1024]{1,0:T(8,128)}, u32[]{:S(2)}, u32[]{:S(2)}) collective-permute-start(f32[192,1024]{1,0:T(8,128)} %all-reduce.7.cloned.1.call-done.refs_0_), channel_id=1, source_target_pairs={{16,0},{24,8},{17,1},{25,9},{18,2},{26,10},{19,3},{27,11},{20,4},{... | collective-permute-start | bytes 2359304 | tf_op jit(solution)/shard_map/ppermute | solution.py:20
  351.4 50.7 %collective-permute-start.37 = (f32[192,1024]{1,0:T(8,128)}, f32[192,1024]{1,0:T(8,128)S(1)}, u32[]{:S(2)}, u32[]{:S(2)}) collective-permute-start(f32[192,1024]{1,0:T(8,128)} %all-reduce.7.cloned.1.call-done.refs_0_), channel_id=1, source_target_pairs={{8,0},{16,8},{24,16},{9,1},{17,9},{25,17},{10,2},{18,10},{26,18},{... | collective-permute-start | bytes 2359304 | tf_op jit(solution)/shard_map/ppermute | solution.py:20
  369.2 51.6 %collective-permute-start.48 = (f32[192,1024]{1,0:T(8,128)S(1)}, f32[192,1024]{1,0:T(8,128)}, u32[]{:S(2)}, u32[]{:S(2)}) collective-permute-start(f32[192,1024]{1,0:T(8,128)S(1)} %copy-done.22), channel_id=1, source_target_pairs={{24,0},{25,1},{26,2},{27,3},{28,4},{29,5},{30,6},{31,7}} | collective-permute-start | bytes 2359304 | tf_op jit(solution)/shard_map/ppermute | solution.py:20
  370.8 52.2 %collective-permute-start.47 = (f32[192,1024]{1,0:T(8,128)S(1)}, f32[192,1024]{1,0:T(8,128)}, u32[]{:S(2)}, u32[]{:S(2)}) collective-permute-start(f32[192,1024]{1,0:T(8,128)S(1)} %copy-done.22), channel_id=1, source_target_pairs={{16,0},{24,8},{17,1},{25,9},{18,2},{26,10},{19,3},{27,11},{20,4},{... | collective-permute-start | bytes 2359304 | tf_op jit(solution)/shard_map/ppermute | solution.py:20
  372.1 50.9 %collective-permute-start.46 = (f32[192,1024]{1,0:T(8,128)S(1)}, f32[192,1024]{1,0:T(8,128)}, u32[]{:S(2)}, u32[]{:S(2)}) collective-permute-start(f32[192,1024]{1,0:T(8,128)S(1)} %copy-done.22), channel_id=1, source_target_pairs={{8,0},{16,8},{24,16},{9,1},{17,9},{25,17},{10,2},{18,10},{26,18},{... | collective-permute-start | bytes 2359304 | tf_op jit(solution)/shard_map/ppermute | solution.py:20
  418.8 20.0 %collective-permute-start.45 = (f32[192,1024]{1,0:T(8,128)}, f32[192,1024]{1,0:T(8,128)S(1)}, u32[]{:S(2)}, u32[]{:S(2)}) collective-permute-start(f32[192,1024]{1,0:T(8,128)} %all-reduce.11.cloned.1.call-done.refs_0_), channel_id=1, source_target_pairs={{24,0},{25,1},{26,2},{27,3},{28,4},{29,5},{30,6},{31,7}} | collective-permute-start | bytes 2359304 | tf_op jit(solution)/shard_map/ppermute | solution.py:20
  419.5 36.1 %collective-permute-start.44 = (f32[192,1024]{1,0:T(8,128)}, f32[192,1024]{1,0:T(8,128)S(1)}, u32[]{:S(2)}, u32[]{:S(2)}) collective-permute-start(f32[192,1024]{1,0:T(8,128)} %all-reduce.11.cloned.1.call-done.refs_0_), channel_id=1, source_target_pairs={{16,0},{24,8},{17,1},{25,9},{18,2},{26,10},{19,3},{27,11},{20,4},{... | collective-permute-start | bytes 2359304 | tf_op jit(solution)/shard_map/ppermute | solution.py:20
  420.8 34.8 %collective-permute-start.43 = (f32[192,1024]{1,0:T(8,128)}, f32[192,1024]{1,0:T(8,128)S(1)}, u32[]{:S(2)}, u32[]{:S(2)}) collective-permute-start(f32[192,1024]{1,0:T(8,128)} %all-reduce.11.cloned.1.call-done.refs_0_), channel_id=1, source_target_pairs={{8,0},{16,8},{24,16},{9,1},{17,9},{25,17},{10,2},{18,10},{26,18},{... | collective-permute-start | bytes 2359304 | tf_op jit(solution)/shard_map/ppermute | solution.py:20
  (33 other events, 409.7 us)
Sparse Core Ops, SparseCore 0:
  168.4 47.8 all-reduce.4
  239.7 43.5 all-reduce.6
  304.1 42.3 all-reduce.8
  354.3 45.3 all-reduce.10

commit v4 on v3

v4 whole, which is shorter than its diff:
```python
import functools

import jax
import jax.numpy as jnp
from jax import lax
from jax.experimental import pallas as pl
from jax.experimental.pallas import tpu as pltpu
from jax.sharding import Mesh, PartitionSpec as P

CHUNKS = 4
TILE = 256
WIDE = 512
LIGHT = pl.CostEstimate(flops=1, bytes_accessed=1, transcendentals=0)
VMEM_LIMIT = 60 * 1024 * 1024


def shifted(value, by):
    devices = lax.axis_size("tm")
    pairs = [(i, i + by) for i in range(devices) if 0 <= i + by < devices]
    return lax.ppermute(value, "tm", pairs)


def swapped(value):
    return lax.ppermute(value, "core", [(0, 1), (1, 0)])


def together(first, second):
    return lax.optimization_barrier((first, second))


def halves(value):
    high = value.astype(jnp.bfloat16)
    low = (value - high.astype(jnp.float32)).astype(jnp.bfloat16)
    return high, low


def times(left, right, dims):
    return lax.dot_general(left, right, (dims, ((), ())), preferred_element_type=jnp.float32)


def split_kernel(core_ref, own, other, high_ref, low_ref):
    cells = other.shape[0]
    for at, value in ((0, own[0]), (cells, other[...])):
        high, low = halves(value)
        high_ref[pl.ds(at, cells), :] = high
        low_ref[pl.ds(at, cells), :] = low


def split(flux, flux_other, core):
    cells, half = flux_other.shape
    tile = min(TILE, half)
    steps = half // tile
    block = pl.BlockSpec((2 * cells, tile), lambda j, c: (0, j))
    return pl.pallas_call(
        split_kernel,
        grid_spec=pltpu.PrefetchScalarGridSpec(
            num_scalar_prefetch=1,
            grid=(steps,),
            in_specs=[
                pl.BlockSpec((1, cells, tile), lambda j, c: (0, 0, c[0] * steps + j)),
                pl.BlockSpec((cells, tile), lambda j, c: (0, j)),
            ],
            out_specs=[block, block],
        ),
        out_shape=[jax.ShapeDtypeStruct((2 * cells, half), jnp.bfloat16)] * 2,
        cost_estimate=LIGHT,
    )(core, flux, flux_other)


def forward_kernel(count, *refs):
    foot_own, foot_other = refs[:count], refs[count:2 * count]
    flux_high, flux_low = refs[2 * count:2 * count + 2]
    outs = refs[2 * count + 2:3 * count + 2]
    high_ref, low_ref = refs[3 * count + 2:]
    rows, cells = foot_own[0].shape[-2:]

    @pl.when(pl.program_id(0) == 0)
    def _():
        for i in range(count):
            for side, source in ((0, foot_own[i]), (1, foot_other[i])):
                high, low = halves(source[...].reshape(rows, cells))
                at = (pl.ds(i * rows, rows), pl.ds(side * cells, cells))
                high_ref[at] = high
                low_ref[at] = low

    dims = ((1,), (0,))
    total = times(high_ref[...], flux_high[...], dims)
    total = total + times(low_ref[...], flux_high[...], dims)
    total = total + times(high_ref[...], flux_low[...], dims)
    for i in range(count):
        outs[i][...] = total[i * rows:(i + 1) * rows]


def forward(foot_own, own_specs, foot_other, other_specs, rows, flux_parts):
    count = len(foot_own)
    depth, half = flux_parts[0].shape
    tile = min(WIDE, half)
    outs = pl.pallas_call(
        functools.partial(forward_kernel, count),
        grid=(half // tile,),
        in_specs=[
            *own_specs,
            *other_specs,
            *[pl.BlockSpec((depth, tile), lambda j: (0, j))] * 2,
        ],
        out_specs=[pl.BlockSpec((rows, tile), lambda j: (0, j))] * count,
        scratch_shapes=[pltpu.VMEM((count * rows, depth), jnp.bfloat16)] * 2,
        out_shape=[jax.ShapeDtypeStruct((rows, half), jnp.float32)] * count,
        compiler_params=pltpu.CompilerParams(vmem_limit_bytes=VMEM_LIMIT),
        cost_estimate=LIGHT,
    )(*foot_own, *foot_other, *flux_parts)
    return list(outs)


def adjoint_kernel(count, sides, first, core_ref, *refs):
    weighted, refs = refs[:count], refs[count:]
    foot, refs = refs[:sides * count], refs[sides * count:]
    before, refs = (None, refs) if first else (refs[:sides], refs[sides:])
    outs, (high_ref, low_ref) = refs[:sides], refs[sides:]
    rows, tile = foot[0].shape[-2:]

    @pl.when(pl.program_id(0) == 0)
    def _():
        for i in range(count):
            high, low = halves(weighted[i][...])
            high_ref[pl.ds(i * rows, rows), :] = high
            low_ref[pl.ds(i * rows, rows), :] = low

    for side in range(sides):
        mine = foot[side * count:(side + 1) * count]
        slab = jnp.concatenate([ref[...].reshape(rows, tile) for ref in mine], axis=0)
        high, low = halves(slab.T)
        dims = ((1,), (0,))
        total = times(high, high_ref[...], dims)
        total = total + times(low, high_ref[...], dims)
        total = total + times(high, low_ref[...], dims)
        if not first:
            total = total + before[side][...]
        outs[side][...] = total


def adjoint(weighted, sides, core, cells):
    count = len(weighted)
    rows, half = weighted[0].shape
    tile = min(WIDE, cells)
    first = sides[0][2] is None
    out_specs = []
    for side in sides:
        if side[4]:
            out_specs.append(pl.BlockSpec((tile, half), lambda j, c: (j, c[0])))
        else:
            out_specs.append(pl.BlockSpec((tile, half), lambda j, c: (j, 0)))
    foot = [array for side in sides for array in side[0]]
    earlier = [] if first else [side[2] for side in sides]
    at = 1 + count + len(foot)
    return pl.pallas_call(
        functools.partial(adjoint_kernel, count, len(sides), first),
        grid_spec=pltpu.PrefetchScalarGridSpec(
            num_scalar_prefetch=1,
            grid=(cells // tile,),
            in_specs=[
                *[pl.BlockSpec((rows, half), lambda j, c: (0, 0))] * count,
                *[spec(tile) for side in sides for spec in side[1]],
                *([] if first else out_specs),
            ],
            out_specs=out_specs,
            scratch_shapes=[pltpu.VMEM((count * rows, half), jnp.bfloat16)] * 2,
        ),
        out_shape=[jax.ShapeDtypeStruct((cells, side[3]), jnp.float32) for side in sides],
        input_output_aliases={} if first else {at + i: i for i in range(len(sides))},
        compiler_params=pltpu.CompilerParams(vmem_limit_bytes=VMEM_LIMIT),
        cost_estimate=LIGHT,
    )(core, *weighted, *foot, *earlier)


def cut_kernel(*refs):
    count = len(refs) // 2
    for source, out in zip(refs[:count], refs[count:]):
        out[...] = source[0, 0]


def cut(footprint, lags, rows, r):
    cells = footprint.shape[3]
    tile = min(WIDE, cells)
    return list(pl.pallas_call(
        cut_kernel,
        grid=(cells // tile,),
        in_specs=[pl.BlockSpec((1, 1, rows, tile), lambda j, lag=lag: (0, lag, r, j)) for lag in lags],
        out_specs=[pl.BlockSpec((rows, tile), lambda j: (0, j))] * len(lags),
        out_shape=[jax.ShapeDtypeStruct((rows, cells), jnp.float32)] * len(lags),
        cost_estimate=LIGHT,
    )(*[footprint] * len(lags)))


def stack_kernel(*refs):
    for i, ref in enumerate(refs[:-1]):
        rows = ref.shape[0]
        refs[-1][pl.ds(i * rows, rows), :] = ref[...]


def stack(pieces):
    rows, cells = pieces[0].shape
    tile = min(WIDE, cells)
    return pl.pallas_call(
        stack_kernel,
        grid=(cells // tile,),
        in_specs=[pl.BlockSpec((rows, tile), lambda j: (0, j))] * len(pieces),
        out_specs=pl.BlockSpec((rows * len(pieces), tile), lambda j: (0, j)),
        out_shape=jax.ShapeDtypeStruct((rows * len(pieces), cells), jnp.float32),
        cost_estimate=LIGHT,
    )(*pieces)


def side_kernel(core_ref, flux, out):
    out[...] = flux[0]


def side_of(flux, core):
    _, cells, width = flux.shape
    tile = min(WIDE, width // 2)
    steps = width // 2 // tile
    return pl.pallas_call(
        side_kernel,
        grid_spec=pltpu.PrefetchScalarGridSpec(
            num_scalar_prefetch=1,
            grid=(steps,),
            in_specs=[pl.BlockSpec((1, cells, tile), lambda j, c: (0, 0, (1 - c[0]) * steps + j))],
            out_specs=pl.BlockSpec((cells, tile), lambda j, c: (0, j)),
        ),
        out_shape=jax.ShapeDtypeStruct((cells, width // 2), jnp.float32),
        cost_estimate=LIGHT,
    )(core, flux)


def combine_kernel(scale, same, *refs):
    total = same[...]
    for ref in refs[:-1]:
        total = total + ref[...]
    refs[-1][...] = scale[...] * total


def combine(scale, same, gathered, r):
    rows, half = gathered[0].shape
    tile = min(WIDE, half)
    block = pl.BlockSpec((rows, tile), lambda j: (0, j))
    return pl.pallas_call(
        combine_kernel,
        grid=(half // tile,),
        in_specs=[
            pl.BlockSpec((rows, 1), lambda j: (r, 0)),
            block,
            *[block] * len(gathered),
        ],
        out_specs=block,
        out_shape=jax.ShapeDtypeStruct((rows, half), jnp.float32),
        cost_estimate=LIGHT,
    )(scale, same, *gathered)


def paste_kernel(core_ref, arrived, before, out_ref):
    out_ref[...] = arrived[...]


def paste(arrived, whole, core):
    cells, half = arrived.shape
    tile = min(TILE, cells)
    return pl.pallas_call(
        paste_kernel,
        grid_spec=pltpu.PrefetchScalarGridSpec(
            num_scalar_prefetch=1,
            grid=(cells // tile,),
            in_specs=[
                pl.BlockSpec((tile, half), lambda j, c: (j, 0)),
                pl.BlockSpec(memory_space=pl.ANY),
            ],
            out_specs=pl.BlockSpec((tile, half), lambda j, c: (j, 1 - c[0])),
        ),
        out_shape=jax.ShapeDtypeStruct(whole.shape, jnp.float32),
        input_output_aliases={2: 0},
        cost_estimate=LIGHT,
    )(core, arrived, whole)


def on_device(footprint, flux, obs_weight, obs_count):
    _, lags, slots, cells = footprint.shape
    half = flux.shape[2] // 2
    rows = slots // CHUNKS
    chunks = range(CHUNKS)
    core = lax.axis_index("core").astype(jnp.int32)[None]
    valid = (jnp.arange(slots, dtype=jnp.int32) < obs_count[0]).astype(jnp.float32)
    row_scale = (valid * obs_weight[0])[:, None]
    later = range(1, lags)

    pieces = cut(footprint, later, rows, 0)
    own = [[shifted(piece, -lag) for piece, lag in zip(pieces, later)]]
    after, _ = together(flux, pieces[0])
    flux_parts = split(flux, swapped(side_of(after, core)), core)
    foot_other = swapped(cut(footprint, [0], slots, 0)[0])
    same = forward(
        [footprint] * CHUNKS,
        [pl.BlockSpec((1, 1, rows, cells), lambda j, r=r: (0, 0, r, 0)) for r in chunks],
        [foot_other] * CHUNKS,
        [pl.BlockSpec((rows, cells), lambda j, r=r: (r, 0)) for r in chunks],
        rows, flux_parts,
    )
    specs = [pl.BlockSpec((rows, cells), lambda j: (0, 0))] * len(later)

    other_specs = [pl.BlockSpec((rows, cells), lambda j, i=i: (i, 0)) for i in range(len(later))]

    other, terms, weighted, sent = [], [], [], []

    def gather_up(r):
        arrived = [shifted(terms[r][lag - 1], lag) for lag in later]
        if r + 1 < CHUNKS:
            arrived[0], terms[r + 1][0] = together(arrived[0], terms[r + 1][0])
        total = combine(row_scale, same[r], arrived, r)
        if r > 0:
            total, weighted[r - 1] = together(total, weighted[r - 1])
        return total

    def column(r):
        return lambda tile: pl.BlockSpec((rows, tile), lambda j, c: (r, j))

    def my_side(r, before):
        def first(tile):
            return pl.BlockSpec((1, 1, rows, tile), lambda j, c: (0, 0, r, j))

        return [footprint, *own[r]], [first] + [column(0)] * len(later), before, 2 * half, True

    def their_side(r, before):
        foot = [foot_other] + [other[r]] * len(later)
        return foot, [column(r)] + [column(i) for i in range(len(later))], before, half, False

    done = [None, None]

    def advance(r):
        total = gather_up(r)
        arrived = lax.psum(total, "z")
        if r > 0:
            for i in range(len(later)):
                arrived, sent[r - 1][i] = together(arrived, sent[r - 1][i])
        if r > 1:
            arrived, done[0] = together(arrived, done[0])
        weighted.append(arrived)
        sent.append([shifted(arrived, -lag) for lag in later])
        if r > 0:
            first, weighted[r] = together(weighted[r - 1], weighted[r])
            both = [my_side(r - 1, done[0]), their_side(r - 1, done[1])]
            done[:] = adjoint([first, *sent[r - 1]], both, core, cells)
        return total

    for r in chunks:
        if r > 0:
            pieces = cut(footprint, later, rows, r)
            for i in range(len(later)):
                pieces[i], own[r - 1][i] = together(pieces[i], own[r - 1][i])
            own.append([shifted(piece, -lag) for piece, lag in zip(pieces, later)])
            for i in range(len(later)):
                own[r][i], terms[r - 1][i] = together(own[r][i], terms[r - 1][i])
        if r > 1:
            total = advance(r - 2)
            for i in range(len(later)):
                own[r][i], _ = together(own[r][i], total)
        other.append(swapped(stack(own[r])))
        terms.append(forward(own[r], specs, [other[r]] * len(later), other_specs, rows, flux_parts))
    for r in range(max(CHUNKS - 2, 0), CHUNKS):
        advance(r)
    mine, theirs = done
    here = [weighted[r], *sent[r]]
    (theirs,) = adjoint(here, [their_side(r, theirs)], core, cells)
    (mine,) = adjoint(here, [my_side(r, mine)], core, cells)
    return paste(swapped(theirs), mine, core)[None]


def solution(mesh):
    devices = mesh.devices
    split = Mesh(devices.reshape(devices.shape[0], devices.shape[1] // 2, 2), ("tm", "z", "core"))
    cells = ("z", "core")
    placed = (P("tm", None, None, cells), P("tm", cells, None), P("tm", None), P("tm"))
    return jax.shard_map(
        on_device, mesh=split, in_specs=placed, out_specs=P("tm", cells, None), check_vma=False
    )
```

time: 493 us -> 484 us (0.982)
  waiting for transfers between devices: 201 us -> 185 us
  starting transfers between devices: 96.2 us -> 81.1 us
  Pallas kernels: 173 us -> 188 us
    ppermute x36, waiting for transfers between devices: 143 us -> 121 us  [shifted(): return lax.ppermute(value, 'tm', pairs)]
    pallas_call x6 -> x11, Pallas kernels: 74.2 us -> 89.5 us  [the longest x5 67.5 us: forward(): pl.pallas_call(functools.partial(forward_kernel, count), grid=(half // ti...]
    ppermute x14 -> x7, starting transfers between devices: 16.8 us -> 4.8 us  [swapped(): return lax.ppermute(value, 'core', [(0, 1), (1, 0)])]
    psum x4, waiting for transfers between devices: 58.2 us -> 64.2 us  [advance(): arrived = lax.psum(total, 'z')]
    pallas_call x4 -> x5, Pallas kernels: 16.1 us -> 14.2 us  [cut(): pl.pallas_call(cut_kernel, grid=(cells // tile,), in_specs=[pl.BlockSpec(...]
  transfers between devices with their start and end apart: 54 -> 47, of which waited for: 12 -> 13; matrix products, arithmetic and copies ran while one was open for 0% -> 0% of each run, Pallas kernels for 27% -> 33%
where the time goes in v4:
time: 484 us; the launch traced here: 478 us
  Pallas kernels  188 us (39%)
  waiting for transfers between devices  185 us (38%)
  starting transfers between devices  81.1 us (17%)
  between operations  14.7 us (3%)
  local copies, waits for them, and re-layouts  7.39 us (2%)
    ppermute x36, waiting for transfers between devices, shifted(): return lax.ppermute(value, 'tm', pairs)  121 us
    ppermute x36, starting transfers between devices, shifted(): return lax.ppermute(value, 'tm', pairs)  76.2 us
    pallas_call x5, Pallas kernels, adjoint(): pl.pallas_call(functools.partial(adjoint_kernel, count, len(sides), first...  69.1 us
    pallas_call x5, Pallas kernels, forward(): pl.pallas_call(functools.partial(forward_kernel, count), grid=(half // ti...  67.5 us
    psum x4, waiting for transfers between devices, advance(): arrived = lax.psum(total, 'z')  64.2 us
    pallas_call x5, Pallas kernels, cut(): pl.pallas_call(cut_kernel, grid=(cells // tile,), in_specs=[pl.BlockSpec(...  14.2 us
    pallas_call x4, Pallas kernels, stack(): pl.pallas_call(stack_kernel, grid=(cells // tile,), in_specs=[pl.BlockSpe...  11 us
    pallas_call x4, Pallas kernels, combine(): pl.pallas_call(combine_kernel, grid=(half // tile,), in_specs=[pl.BlockSp...  10.9 us
  transfers between devices with their start and end apart: 47, of which 13 were waited for; matrix products, arithmetic and copies ran while one was open for 0% of the time, Pallas kernels for 33%

profile of v4, /device:TPU:3, one launch (start us, length us, event | category | flops | bytes accessed | tf_op | source)
XLA Modules:
  0.0 478.0 jit_solution(8913140035694794827)
XLA Ops:
  6.5 2.7 shard_map.47
  9.3 3.8 shard_map.48
  17.7 34.2 %collective-permute-done.4.refs_1_.refs_6_ = f32[192,1024]{1,0:T(8,128)S(1)} collective-permute-done((f32[192,1024]{1,0:T(8,128)}, f32[192,1024]{1,0:T(8,128)S(1)}, u32[]{:S(2)}, u32[]{:S(2)}) %collective-permute-start.4) | collective-permute-done | bytes 786464 | tf_op jit(solution)/shard_map/ppermute | solution.py:20
  54.0 2.7 shard_map.52
  57.6 2.8 shard_map.51
  60.3 3.2 shard_map.46
  68.3 7.2 %shard_map.49 = (bf16[2048,1024]{1,0:T(8,128)(2,1)}, bf16[2048,1024]{1,0:T(8,128)(2,1)}) custom-call(s32[1]{0:T(128)} %bitcast.core_ref, f32[1,1024,2048]{2,1,0:T(8,128)} %own.1, f32[1024,1024]{1,0:T(8,128)} %collective-permute-done.1.other), custom_call_target="tpu_custom_call" | custom-call | flops 1 | bytes 1 | tf_op jit(solution)/shard_map/pallas_call | solution.py:54
  75.5 12.8 %shard_map.53 = (f32[192,1024]{1,0:T(8,128)}, f32[192,1024]{1,0:T(8,128)}, f32[192,1024]{1,0:T(8,128)}) custom-call(f32[192,1024]{1,0:T(8,128)} %copy-done.5, f32[192,1024]{1,0:T(8,128)} %copy-done.3, f32[192,1024]{1,0:T(8,128)} %copy-done.4, f32[576,1024]{1,0:T(8,128)} %collective-permute-done.6.refs_3_.refs_4_.refs_5_.refs_9_.refs_10_.refs_11_, ...), custom_call_target="tpu_custom_call" | custom-call | flops 1 | bytes 1 | tf_op jit(solution)/shard_map/pallas_call | solution.py:98
  88.4 14.6 %collective-permute-done.9.refs_1_.refs_6_ = f32[192,1024]{1,0:T(8,128)} collective-permute-done((f32[192,1024]{1,0:T(8,128)}, f32[192,1024]{1,0:T(8,128)}, u32[]{:S(2)}, u32[]{:S(2)}) %collective-permute-start.9) | collective-permute-done | bytes 786464 | tf_op jit(solution)/shard_map/ppermute | solution.py:20
  103.0 2.8 shard_map.55
  106.2 2.8 shard_map.54
  109.0 3.5 collective-permute-start.8
  112.5 2.7 collective-permute-start.7
  118.5 12.8 %collective-permute-done.8.refs_0_.refs_5_ = f32[192,1024]{1,0:T(8,128)} collective-permute-done((f32[192,1024]{1,0:T(8,128)}, f32[192,1024]{1,0:T(8,128)}, u32[]{:S(2)}, u32[]{:S(2)}) %collective-permute-start.8) | collective-permute-done | bytes 786464 | tf_op jit(solution)/shard_map/ppermute | solution.py:20
  132.8 2.4 collective-permute-start.13
  136.9 16.0 %shard_map.50 = (f32[192,1024]{1,0:T(8,128)}, f32[192,1024]{1,0:T(8,128)}, f32[192,1024]{1,0:T(8,128)}, f32[192,1024]{1,0:T(8,128)}) custom-call(f32[1,4,768,1024]{3,2,1,0:T(8,128)} %refs_4_.7, f32[1,4,768,1024]{3,2,1,0:T(8,128)} %refs_4_.7, f32[1,4,768,1024]{3,2,1,0:T(8,128)} %refs_4_.7, f32[1,4,768,1024]{3,2,1,0:T(8,128)} %refs_4_.7, f32[768,1024]{1,0:T(8,128)} %copy-done, ...), custom_call_target="tpu_custom_call" | custom-call | flops 1 | bytes 1 | tf_op jit(solution)/shard_map/pallas_call | solution.py:98
  152.9 12.9 %shard_map.56 = (f32[192,1024]{1,0:T(8,128)}, f32[192,1024]{1,0:T(8,128)}, f32[192,1024]{1,0:T(8,128)}) custom-call(f32[192,1024]{1,0:T(8,128)} %collective-permute-done.3.refs_0_.refs_5_, f32[192,1024]{1,0:T(8,128)} %collective-permute-done.9.refs_1_.refs_6_, f32[192,1024]{1,0:T(8,128)} %collective-permute-done.10.refs_2_.refs_7_, ...), custom_call_target="tpu_custom_call" | custom-call | flops 1 | bytes 1 | tf_op jit(solution)/shard_map/pallas_call | solution.py:98
  167.4 2.7 shard_map.58
  170.1 2.7 shard_map.59
  173.3 2.7 shard_map.57
  176.1 2.3 collective-permute-start.15
  178.4 3.8 collective-permute-start.12
  186.1 12.3 %collective-permute-done.15.refs_0_.refs_5_ = f32[192,1024]{1,0:T(8,128)S(1)} collective-permute-done((f32[192,1024]{1,0:T(8,128)}, f32[192,1024]{1,0:T(8,128)S(1)}, u32[]{:S(2)}, u32[]{:S(2)}) %collective-permute-start.15) | collective-permute-done | bytes 786464 | tf_op jit(solution)/shard_map/ppermute | solution.py:20
  201.3 12.9 %shard_map.60 = (f32[192,1024]{1,0:T(8,128)}, f32[192,1024]{1,0:T(8,128)}, f32[192,1024]{1,0:T(8,128)}) custom-call(f32[192,1024]{1,0:T(8,128)} %collective-permute-done.8.refs_0_.refs_5_, f32[192,1024]{1,0:T(8,128)} %collective-permute-done.16.refs_1_.refs_6_, f32[192,1024]{1,0:T(8,128)} %collective-permute-done.17.refs_2_.refs_7_, f32[576,1024]{1,0:T(8,128)} %copy-done.2, ...), custom_call_target="tpu_custom_call" | custom-call | flops 1 | bytes 1 | tf_op jit(solution)/shard_map/pallas_call | solution.py:98
  214.3 4.6 collective-permute-done.20.refs_1_
  218.9 2.7 shard_map.61
  221.6 8.5 %all-reduce.5.cloned.1.call-done.refs_0_ = f32[192,1024]{1,0:T(8,128)} async-done(((f32[192,1024]{1,0:T(8,128)}), f32[192,1024]{1,0:T(8,128)}) %all-reduce.5.cloned.1.call-update) | async-done | bytes 786448 | tf_op jit(solution)/shard_map/psum | solution.py:338
  230.1 2.8 shard_map.62
  234.9 8.0 %collective-permute-start.30 = (f32[192,1024]{1,0:T(8,128)}, f32[192,1024]{1,0:T(8,128)}, u32[]{:S(2)}, u32[]{:S(2)}) collective-permute-start(f32[192,1024]{1,0:T(8,128)} %all-reduce.5.cloned.1.call-done.refs_0_), channel_id=1, source_target_pairs={{8,0},{16,8},{24,16},{9,1},{17,9},{25,17},{10,2},{18,10},{26,18},{... | collective-permute-start | bytes 2359304 | tf_op jit(solution)/shard_map/ppermute | solution.py:20
  244.5 4.6 collective-permute-start.19
  249.1 22.7 %collective-permute-done.31.refs_2_ = f32[192,1024]{1,0:T(8,128)} collective-permute-done((f32[192,1024]{1,0:T(8,128)}, f32[192,1024]{1,0:T(8,128)}, u32[]{:S(2)}, u32[]{:S(2)}) %collective-permute-start.31) | collective-permute-done | bytes 786464 | tf_op jit(solution)/shard_map/ppermute | solution.py:20
  275.6 14.8 %all-reduce.7.cloned.1.call-done.refs_0_ = f32[192,1024]{1,0:T(8,128)} async-done(((f32[192,1024]{1,0:T(8,128)}), f32[192,1024]{1,0:T(8,128)}) %all-reduce.7.cloned.1.call-update) | async-done | bytes 786448 | tf_op jit(solution)/shard_map/psum | solution.py:338
  290.4 2.4 collective-permute-start.33
  294.2 12.8 %shard_map.63 = (f32[192,1024]{1,0:T(8,128)}, f32[192,1024]{1,0:T(8,128)}, f32[192,1024]{1,0:T(8,128)}) custom-call(f32[192,1024]{1,0:T(8,128)} %copy-done.6, f32[192,1024]{1,0:T(8,128)} %collective-permute-done.22.refs_1_.refs_6_, f32[192,1024]{1,0:T(8,128)} %collective-permute-done.23.refs_2_.refs_7_, f32[576,1024]{1,0:T(8,128)} %copy-done.1, ...), custom_call_target="tpu_custom_call" | custom-call | flops 1 | bytes 1 | tf_op jit(solution)/shard_map/pallas_call | solution.py:98
  308.3 2.7 shard_map.65
  314.0 4.5 collective-permute-start.25
  318.5 2.5 collective-permute-start.26
  321.7 15.3 %shard_map.66 = (f32[1024,2048]{1,0:T(8,128)}, f32[1024,1024]{1,0:T(8,128)}) custom-call(s32[1]{0:T(128)} %bitcast.core_ref, f32[192,1024]{1,0:T(8,128)} %all-reduce.5.cloned.1.call-done.refs_0_, f32[192,1024]{1,0:T(8,128)} %collective-permute-done.30.refs_1_, f32[192,1024]{1,0:T(8,128)} %collective-permute-done.31.refs_2_, ...), custom_call_target="tpu_custom_call" | custom-call | flops 1 | bytes 1 | tf_op jit(solution)/shard_map/pallas_call | solution.py:156
  337.0 18.0 %all-reduce.9.cloned.1.call-done.refs_0_ = f32[192,1024]{1,0:T(8,128)} async-done(((f32[192,1024]{1,0:T(8,128)}), f32[192,1024]{1,0:T(8,128)}) %all-reduce.9.cloned.1.call-update) | async-done | bytes 786448 | tf_op jit(solution)/shard_map/psum | solution.py:338
  356.4 2.8 shard_map.64
  363.4 16.7 %shard_map.67 = (f32[1024,2048]{1,0:T(8,128)}, f32[1024,1024]{1,0:T(8,128)}) custom-call(s32[1]{0:T(128)} %bitcast.core_ref, f32[192,1024]{1,0:T(8,128)} %all-reduce.7.cloned.1.call-done.refs_0_, f32[192,1024]{1,0:T(8,128)} %collective-permute-done.33.refs_1_, ...), custom_call_target="tpu_custom_call", output_to_operand_aliasing={{0}: (13, {}), {1}: (14, {})} | custom-call | flops 1 | bytes 1 | tf_op jit(solution)/shard_map/pallas_call | solution.py:156
  380.1 22.9 %all-reduce.11.cloned.1.call-done.refs_0_ = f32[192,1024]{1,0:T(8,128)} async-done(((f32[192,1024]{1,0:T(8,128)}), f32[192,1024]{1,0:T(8,128)}) %all-reduce.11.cloned.1.call-update) | async-done | bytes 786448 | tf_op jit(solution)/shard_map/psum | solution.py:338
  406.2 3.0 collective-permute-start.39
  409.3 16.5 %shard_map.68 = (f32[1024,2048]{1,0:T(8,128)}, f32[1024,1024]{1,0:T(8,128)}) custom-call(s32[1]{0:T(128)} %bitcast.core_ref, f32[192,1024]{1,0:T(8,128)} %all-reduce.9.cloned.1.call-done.refs_0_, f32[192,1024]{1,0:T(8,128)} %copy-done.15, f32[192,1024]{1,0:T(8,128)} %copy-done.16, ...), custom_call_target="tpu_custom_call", output_to_operand_aliasing={{0}: (13, {}), {1}: (14, {})} | custom-call | flops 1 | bytes 1 | tf_op jit(solution)/shard_map/pallas_call | solution.py:156
  425.8 17.0 %collective-permute-done.40.refs_2_ = f32[192,1024]{1,0:T(8,128)S(1)} collective-permute-done((f32[192,1024]{1,0:T(8,128)}, f32[192,1024]{1,0:T(8,128)S(1)}, u32[]{:S(2)}, u32[]{:S(2)}) %collective-permute-start.40) | collective-permute-done | bytes 786464 | tf_op jit(solution)/shard_map/ppermute | solution.py:20
  444.0 10.3 %shard_map.69 = f32[1024,1024]{1,0:T(8,128)} custom-call(s32[1]{0:T(128)} %bitcast.core_ref, f32[192,1024]{1,0:T(8,128)} %all-reduce.11.cloned.1.call-done.refs_0_, f32[192,1024]{1,0:T(8,128)} %copy-done.9, f32[192,1024]{1,0:T(8,128)} %copy-done.8, f32[192,1024]{1,0:T(8,128)} %copy-done.7, f32[768,1024]{1,0:T(8,128)} %copy-done, ...), custom_call_target="tpu_custom_call", output_to_operand_aliasing={{}: (9, {})} | custom-call | flops 1 | bytes 1 | tf_op jit(solution)/shard_map/pallas_call | solution.py:156
  455.9 10.3 %shard_map.70.before = f32[1024,2048]{1,0:T(8,128)} custom-call(s32[1]{0:T(128)} %bitcast.core_ref, f32[192,1024]{1,0:T(8,128)} %all-reduce.11.cloned.1.call-done.refs_0_, f32[192,1024]{1,0:T(8,128)} %copy-done.9, f32[192,1024]{1,0:T(8,128)} %copy-done.8, f32[192,1024]{1,0:T(8,128)} %copy-done.7, ...), custom_call_target="tpu_custom_call", output_to_operand_aliasing={{}: (9, {})} | custom-call | flops 1 | bytes 1 | tf_op jit(solution)/shard_map/pallas_call | solution.py:156
  466.3 4.7 shard_map.71
  (118 shorter events, 52.7 us)
Async XLA Ops:
  6.5 223.6 %all-reduce.5.cloned.1.call-start = ((), (), s32[]{:S(2)}) async-start(), calls=%async_computation | async-start | bytes 1572864 | tf_op jit(solution)/shard_map/psum | solution.py:338
  13.1 55.2 %collective-permute-start.1 = (f32[1024,1024]{1,0:T(8,128)}, f32[1024,1024]{1,0:T(8,128)}, u32[]{:S(2)}, u32[]{:S(2)}) collective-permute-start(f32[1024,1024]{1,0:T(8,128)} %shard_map.48), channel_id=1, source_target_pairs={{0,1},{1,0},{2,3},{3,2},{4,5},{5,4},{6,7},{7,6},{8,9},{9,8},{10,11... | collective-permute-start | bytes 12582920 | tf_op jit(solution)/shard_map/ppermute | solution.py:24
  13.8 38.1 %collective-permute-start.4 = (f32[192,1024]{1,0:T(8,128)}, f32[192,1024]{1,0:T(8,128)S(1)}, u32[]{:S(2)}, u32[]{:S(2)}) collective-permute-start(f32[192,1024]{1,0:T(8,128)} %get-tuple-element.131), channel_id=1, source_target_pairs={{16,0},{24,8},{17,1},{25,9},{18,2},{26,10},{19,3},{27,11},{20,4},{... | collective-permute-start | bytes 2359304 | tf_op jit(solution)/shard_map/ppermute | solution.py:20
  15.0 36.8 %collective-permute-start.5 = (f32[192,1024]{1,0:T(8,128)}, f32[192,1024]{1,0:T(8,128)S(1)}, u32[]{:S(2)}, u32[]{:S(2)}) collective-permute-start(f32[192,1024]{1,0:T(8,128)} %get-tuple-element.132), channel_id=1, source_target_pairs={{24,0},{25,1},{26,2},{27,3},{28,4},{29,5},{30,6},{31,7}} | collective-permute-start | bytes 2359304 | tf_op jit(solution)/shard_map/ppermute | solution.py:20
  15.8 36.1 %collective-permute-start.2 = (f32[192,1024]{1,0:T(8,128)S(1)}, f32[192,1024]{1,0:T(8,128)S(1)}, u32[]{:S(2)}, u32[]{:S(2)}) collective-permute-start(f32[192,1024]{1,0:T(8,128)S(1)} %copy-done.19), channel_id=1, source_target_pairs={{8,0},{16,8},{24,16},{9,1},{17,9},{25,17},{10,2},{18,10},{26,18},{... | collective-permute-start | bytes 2359304 | tf_op jit(solution)/shard_map/ppermute | solution.py:20
  56.8 18.7 %collective-permute-start.6 = (f32[576,1024]{1,0:T(8,128)}, f32[576,1024]{1,0:T(8,128)}, u32[]{:S(2)}, u32[]{:S(2)}) collective-permute-start(f32[576,1024]{1,0:T(8,128)} %shard_map.52), channel_id=1, source_target_pairs={{0,1},{1,0},{2,3},{3,2},{4,5},{5,4},{6,7},{7,6},{8,9},{9,8},{10,11... | collective-permute-start | bytes 7077896 | tf_op jit(solution)/shard_map/ppermute | solution.py:24
  63.5 24.8 %collective-permute-start.3 = (f32[192,1024]{1,0:T(8,128)}, f32[192,1024]{1,0:T(8,128)}, u32[]{:S(2)}, u32[]{:S(2)}) collective-permute-start(f32[192,1024]{1,0:T(8,128)} %get-tuple-element.130), channel_id=1, source_target_pairs={{8,0},{16,8},{24,16},{9,1},{17,9},{25,17},{10,2},{18,10},{26,18},{... | collective-permute-start | bytes 2359304 | tf_op jit(solution)/shard_map/ppermute | solution.py:20
  65.4 37.6 %collective-permute-start.9 = (f32[192,1024]{1,0:T(8,128)}, f32[192,1024]{1,0:T(8,128)}, u32[]{:S(2)}, u32[]{:S(2)}) collective-permute-start(f32[192,1024]{1,0:T(8,128)} %get-tuple-element.139), channel_id=1, source_target_pairs={{16,0},{24,8},{17,1},{25,9},{18,2},{26,10},{19,3},{27,11},{20,4},{... | collective-permute-start | bytes 2359304 | tf_op jit(solution)/shard_map/ppermute | solution.py:20
  66.7 36.3 %collective-permute-start.10 = (f32[192,1024]{1,0:T(8,128)}, f32[192,1024]{1,0:T(8,128)}, u32[]{:S(2)}, u32[]{:S(2)}) collective-permute-start(f32[192,1024]{1,0:T(8,128)} %get-tuple-element.143), channel_id=1, source_target_pairs={{24,0},{25,1},{26,2},{27,3},{28,4},{29,5},{30,6},{31,7}} | collective-permute-start | bytes 2359304 | tf_op jit(solution)/shard_map/ppermute | solution.py:20
  68.3 48.2 %collective-permute-start = (f32[768,1024]{1,0:T(8,128)}, f32[768,1024]{1,0:T(8,128)S(1)}, u32[]{:S(2)}, u32[]{:S(2)}) collective-permute-start(f32[768,1024]{1,0:T(8,128)} %shard_map.46), channel_id=1, source_target_pairs={{0,1},{1,0},{2,3},{3,2},{4,5},{5,4},{6,7},{7,6},{8,9},{9,8},{10,11... | collective-permute-start | bytes 9437192 | tf_op jit(solution)/shard_map/ppermute | solution.py:24
  105.8 27.0 %collective-permute-start.11 = (f32[576,1024]{1,0:T(8,128)}, f32[576,1024]{1,0:T(8,128)}, u32[]{:S(2)}, u32[]{:S(2)}) collective-permute-start(f32[576,1024]{1,0:T(8,128)} %shard_map.55), channel_id=1, source_target_pairs={{0,1},{1,0},{2,3},{3,2},{4,5},{5,4},{6,7},{7,6},{8,9},{9,8},{10,11... | collective-permute-start | bytes 7077896 | tf_op jit(solution)/shard_map/ppermute | solution.py:24
  109.0 22.2 %collective-permute-start.8 = (f32[192,1024]{1,0:T(8,128)}, f32[192,1024]{1,0:T(8,128)}, u32[]{:S(2)}, u32[]{:S(2)}) collective-permute-start(f32[192,1024]{1,0:T(8,128)} %get-tuple-element.137), channel_id=1, source_target_pairs={{8,0},{16,8},{24,16},{9,1},{17,9},{25,17},{10,2},{18,10},{26,18},{... | collective-permute-start | bytes 2359304 | tf_op jit(solution)/shard_map/ppermute | solution.py:20
  112.5 53.2 %collective-permute-start.7 = (f32[192,1024]{1,0:T(8,128)}, f32[192,1024]{1,0:T(8,128)}, u32[]{:S(2)}, u32[]{:S(2)}) collective-permute-start(f32[192,1024]{1,0:T(8,128)} %get-tuple-element.134), channel_id=1, source_target_pairs={{0,8},{8,16},{16,24},{1,9},{9,17},{17,25},{2,10},{10,18},{18,26},{... | collective-permute-start | bytes 2359304 | tf_op jit(solution)/shard_map/ppermute | solution.py:20
  115.2 50.5 %collective-permute-start.16 = (f32[192,1024]{1,0:T(8,128)}, f32[192,1024]{1,0:T(8,128)}, u32[]{:S(2)}, u32[]{:S(2)}) collective-permute-start(f32[192,1024]{1,0:T(8,128)} %get-tuple-element.158), channel_id=1, source_target_pairs={{16,0},{24,8},{17,1},{25,9},{18,2},{26,10},{19,3},{27,11},{20,4},{... | collective-permute-start | bytes 2359304 | tf_op jit(solution)/shard_map/ppermute | solution.py:20
  116.5 49.2 %collective-permute-start.17 = (f32[192,1024]{1,0:T(8,128)}, f32[192,1024]{1,0:T(8,128)}, u32[]{:S(2)}, u32[]{:S(2)}) collective-permute-start(f32[192,1024]{1,0:T(8,128)} %get-tuple-element.163), channel_id=1, source_target_pairs={{24,0},{25,1},{26,2},{27,3},{28,4},{29,5},{30,6},{31,7}} | collective-permute-start | bytes 2359304 | tf_op jit(solution)/shard_map/ppermute | solution.py:20
  131.3 34.5 %collective-permute-start.14 = (f32[192,1024]{1,0:T(8,128)}, f32[192,1024]{1,0:T(8,128)}, u32[]{:S(2)}, u32[]{:S(2)}) collective-permute-start(f32[192,1024]{1,0:T(8,128)} %get-tuple-element.154), channel_id=1, source_target_pairs={{0,24},{1,25},{2,26},{3,27},{4,28},{5,29},{6,30},{7,31}} | collective-permute-start | bytes 2359304 | tf_op jit(solution)/shard_map/ppermute | solution.py:20
  132.8 34.6 %collective-permute-start.13 = (f32[192,1024]{1,0:T(8,128)}, f32[192,1024]{1,0:T(8,128)}, u32[]{:S(2)}, u32[]{:S(2)}) collective-permute-start(f32[192,1024]{1,0:T(8,128)} %get-tuple-element.153), channel_id=1, source_target_pairs={{0,16},{8,24},{1,17},{9,25},{2,18},{10,26},{3,19},{11,27},{4,20},{... | collective-permute-start | bytes 2359304 | tf_op jit(solution)/shard_map/ppermute | solution.py:20
  172.8 26.8 %collective-permute-start.18 = (f32[576,1024]{1,0:T(8,128)}, f32[576,1024]{1,0:T(8,128)S(1)}, u32[]{:S(2)}, u32[]{:S(2)}) collective-permute-start(f32[576,1024]{1,0:T(8,128)} %shard_map.59), channel_id=1, source_target_pairs={{0,1},{1,0},{2,3},{3,2},{4,5},{5,4},{6,7},{7,6},{8,9},{9,8},{10,11... | collective-permute-start | bytes 7077896 | tf_op jit(solution)/shard_map/ppermute | solution.py:24
  176.1 22.3 %collective-permute-start.15 = (f32[192,1024]{1,0:T(8,128)}, f32[192,1024]{1,0:T(8,128)S(1)}, u32[]{:S(2)}, u32[]{:S(2)}) collective-permute-start(f32[192,1024]{1,0:T(8,128)} %get-tuple-element.156), channel_id=1, source_target_pairs={{8,0},{16,8},{24,16},{9,1},{17,9},{25,17},{10,2},{18,10},{26,18},{... | collective-permute-start | bytes 2359304 | tf_op jit(solution)/shard_map/ppermute | solution.py:20
  178.4 35.8 %collective-permute-start.12 = (f32[192,1024]{1,0:T(8,128)}, f32[192,1024]{1,0:T(8,128)}, u32[]{:S(2)}, u32[]{:S(2)}) collective-permute-start(f32[192,1024]{1,0:T(8,128)} %get-tuple-element.148), channel_id=1, source_target_pairs={{0,8},{8,16},{16,24},{1,9},{9,17},{17,25},{2,10},{10,18},{18,26},{... | collective-permute-start | bytes 2359304 | tf_op jit(solution)/shard_map/ppermute | solution.py:20
  182.3 32.0 %collective-permute-start.21 = (f32[192,1024]{1,0:T(8,128)}, f32[192,1024]{1,0:T(8,128)}, u32[]{:S(2)}, u32[]{:S(2)}) collective-permute-start(f32[192,1024]{1,0:T(8,128)} %get-tuple-element.174), channel_id=1, source_target_pairs={{0,24},{1,25},{2,26},{3,27},{4,28},{5,29},{6,30},{7,31}} | collective-permute-start | bytes 2359304 | tf_op jit(solution)/shard_map/ppermute | solution.py:20
  183.8 35.1 %collective-permute-start.20 = (f32[192,1024]{1,0:T(8,128)}, f32[192,1024]{1,0:T(8,128)}, u32[]{:S(2)}, u32[]{:S(2)}) collective-permute-start(f32[192,1024]{1,0:T(8,128)} %get-tuple-element.173), channel_id=1, source_target_pairs={{0,16},{8,24},{1,17},{9,25},{2,18},{10,26},{3,19},{11,27},{4,20},{... | collective-permute-start | bytes 2359304 | tf_op jit(solution)/shard_map/ppermute | solution.py:20
  186.0 104.4 %all-reduce.7.cloned.1.call-start = ((), (), s32[]{:S(2)}) async-start(), calls=%async_computation.1 | async-start | bytes 1572864 | tf_op jit(solution)/shard_map/psum | solution.py:338
  198.3 31.8 %copy-start.6 = (f32[192,1024]{1,0:T(8,128)}, f32[192,1024]{1,0:T(8,128)S(1)}, u32[]{:S(2)}) copy-start(f32[192,1024]{1,0:T(8,128)S(1)} %collective-permute-done.15.refs_0_.refs_5_) | copy-start | bytes 2359300
  198.3 31.8 %collective-permute-start.22 = (f32[192,1024]{1,0:T(8,128)}, f32[192,1024]{1,0:T(8,128)}, u32[]{:S(2)}, u32[]{:S(2)}) collective-permute-start(f32[192,1024]{1,0:T(8,128)} %get-tuple-element.178), channel_id=1, source_target_pairs={{16,0},{24,8},{17,1},{25,9},{18,2},{26,10},{19,3},{27,11},{20,4},{... | collective-permute-start | bytes 2359304 | tf_op jit(solution)/shard_map/ppermute | solution.py:20
  199.6 30.4 %collective-permute-start.23 = (f32[192,1024]{1,0:T(8,128)}, f32[192,1024]{1,0:T(8,128)}, u32[]{:S(2)}, u32[]{:S(2)}) collective-permute-start(f32[192,1024]{1,0:T(8,128)} %get-tuple-element.183), channel_id=1, source_target_pairs={{24,0},{25,1},{26,2},{27,3},{28,4},{29,5},{30,6},{31,7}} | collective-permute-start | bytes 2359304 | tf_op jit(solution)/shard_map/ppermute | solution.py:20
  232.9 60.0 %collective-permute-start.24 = (f32[576,1024]{1,0:T(8,128)}, f32[576,1024]{1,0:T(8,128)S(1)}, u32[]{:S(2)}, u32[]{:S(2)}) collective-permute-start(f32[576,1024]{1,0:T(8,128)} %shard_map.62), channel_id=1, source_target_pairs={{0,1},{1,0},{2,3},{3,2},{4,5},{5,4},{6,7},{7,6},{8,9},{9,8},{10,11... | collective-permute-start | bytes 7077896 | tf_op jit(solution)/shard_map/ppermute | solution.py:24
  233.6 38.2 %collective-permute-start.31 = (f32[192,1024]{1,0:T(8,128)}, f32[192,1024]{1,0:T(8,128)}, u32[]{:S(2)}, u32[]{:S(2)}) collective-permute-start(f32[192,1024]{1,0:T(8,128)} %all-reduce.5.cloned.1.call-done.refs_0_), channel_id=1, source_target_pairs={{16,0},{24,8},{17,1},{25,9},{18,2},{26,10},{19,3},{27,11},{20,4},{... | collective-permute-start | bytes 2359304 | tf_op jit(solution)/shard_map/ppermute | solution.py:20
  234.9 38.5 %collective-permute-start.30 = (f32[192,1024]{1,0:T(8,128)}, f32[192,1024]{1,0:T(8,128)}, u32[]{:S(2)}, u32[]{:S(2)}) collective-permute-start(f32[192,1024]{1,0:T(8,128)} %all-reduce.5.cloned.1.call-done.refs_0_), channel_id=1, source_target_pairs={{8,0},{16,8},{24,16},{9,1},{17,9},{25,17},{10,2},{18,10},{26,18},{... | collective-permute-start | bytes 2359304 | tf_op jit(solution)/shard_map/ppermute | solution.py:20
  242.9 112.1 %all-reduce.9.cloned.1.call-start = ((), (), s32[]{:S(2)}) async-start(), calls=%async_computation.2 | async-start | bytes 1572864 | tf_op jit(solution)/shard_map/psum | solution.py:338
  242.9 47.5 %collective-permute-start.32 = (f32[192,1024]{1,0:T(8,128)}, f32[192,1024]{1,0:T(8,128)}, u32[]{:S(2)}, u32[]{:S(2)}) collective-permute-start(f32[192,1024]{1,0:T(8,128)} %all-reduce.5.cloned.1.call-done.refs_0_), channel_id=1, source_target_pairs={{24,0},{25,1},{26,2},{27,3},{28,4},{29,5},{30,6},{31,7}} | collective-permute-start | bytes 2359304 | tf_op jit(solution)/shard_map/ppermute | solution.py:20
  244.5 62.6 %collective-permute-start.19 = (f32[192,1024]{1,0:T(8,128)}, f32[192,1024]{1,0:T(8,128)S(1)}, u32[]{:S(2)}, u32[]{:S(2)}) collective-permute-start(f32[192,1024]{1,0:T(8,128)} %get-tuple-element.169), channel_id=1, source_target_pairs={{0,8},{8,16},{16,24},{1,9},{9,17},{17,25},{2,10},{10,18},{18,26},{... | collective-permute-start | bytes 2359304 | tf_op jit(solution)/shard_map/ppermute | solution.py:20
  271.8 35.2 %collective-permute-start.29 = (f32[192,1024]{1,0:T(8,128)}, f32[192,1024]{1,0:T(8,128)}, u32[]{:S(2)}, u32[]{:S(2)}) collective-permute-start(f32[192,1024]{1,0:T(8,128)} %get-tuple-element.194), channel_id=1, source_target_pairs={{0,24},{1,25},{2,26},{3,27},{4,28},{5,29},{6,30},{7,31}} | collective-permute-start | bytes 2359304 | tf_op jit(solution)/shard_map/ppermute | solution.py:20
  273.4 34.9 %collective-permute-start.28 = (f32[192,1024]{1,0:T(8,128)}, f32[192,1024]{1,0:T(8,128)}, u32[]{:S(2)}, u32[]{:S(2)}) collective-permute-start(f32[192,1024]{1,0:T(8,128)} %get-tuple-element.193), channel_id=1, source_target_pairs={{0,16},{8,24},{1,17},{9,25},{2,18},{10,26},{3,19},{11,27},{4,20},{... | collective-permute-start | bytes 2359304 | tf_op jit(solution)/shard_map/ppermute | solution.py:20
  290.4 30.6 %collective-permute-start.33 = (f32[192,1024]{1,0:T(8,128)}, f32[192,1024]{1,0:T(8,128)}, u32[]{:S(2)}, u32[]{:S(2)}) collective-permute-start(f32[192,1024]{1,0:T(8,128)} %all-reduce.7.cloned.1.call-done.refs_0_), channel_id=1, source_target_pairs={{8,0},{16,8},{24,16},{9,1},{17,9},{25,17},{10,2},{18,10},{26,18},{... | collective-permute-start | bytes 2359304 | tf_op jit(solution)/shard_map/ppermute | solution.py:20
  311.1 92.0 %all-reduce.11.cloned.1.call-start = ((), (), s32[]{:S(2)}) async-start(), calls=%async_computation.3 | async-start | bytes 1572864 | tf_op jit(solution)/shard_map/psum | solution.py:338
  311.1 43.9 %collective-permute-start.34 = (f32[192,1024]{1,0:T(8,128)}, f32[192,1024]{1,0:T(8,128)}, u32[]{:S(2)}, u32[]{:S(2)}) collective-permute-start(f32[192,1024]{1,0:T(8,128)} %all-reduce.7.cloned.1.call-done.refs_0_), channel_id=1, source_target_pairs={{16,0},{24,8},{17,1},{25,9},{18,2},{26,10},{19,3},{27,11},{20,4},{... | collective-permute-start | bytes 2359304 | tf_op jit(solution)/shard_map/ppermute | solution.py:20
  312.4 42.6 %collective-permute-start.35 = (f32[192,1024]{1,0:T(8,128)}, f32[192,1024]{1,0:T(8,128)}, u32[]{:S(2)}, u32[]{:S(2)}) collective-permute-start(f32[192,1024]{1,0:T(8,128)} %all-reduce.7.cloned.1.call-done.refs_0_), channel_id=1, source_target_pairs={{24,0},{25,1},{26,2},{27,3},{28,4},{29,5},{30,6},{31,7}} | collective-permute-start | bytes 2359304 | tf_op jit(solution)/shard_map/ppermute | solution.py:20
  314.0 41.0 %collective-permute-start.25 = (f32[192,1024]{1,0:T(8,128)}, f32[192,1024]{1,0:T(8,128)S(1)}, u32[]{:S(2)}, u32[]{:S(2)}) collective-permute-start(f32[192,1024]{1,0:T(8,128)} %get-tuple-element.188), channel_id=1, source_target_pairs={{0,8},{8,16},{16,24},{1,9},{9,17},{17,25},{2,10},{10,18},{18,26},{... | collective-permute-start | bytes 2359304 | tf_op jit(solution)/shard_map/ppermute | solution.py:20
  318.5 36.5 %collective-permute-start.26 = (f32[192,1024]{1,0:T(8,128)}, f32[192,1024]{1,0:T(8,128)S(1)}, u32[]{:S(2)}, u32[]{:S(2)}) collective-permute-start(f32[192,1024]{1,0:T(8,128)} %get-tuple-element.189), channel_id=1, source_target_pairs={{0,16},{8,24},{1,17},{9,25},{2,18},{10,26},{3,19},{11,27},{4,20},{... | collective-permute-start | bytes 2359304 | tf_op jit(solution)/shard_map/ppermute | solution.py:20
  321.0 34.0 %collective-permute-start.27 = (f32[192,1024]{1,0:T(8,128)}, f32[192,1024]{1,0:T(8,128)S(1)}, u32[]{:S(2)}, u32[]{:S(2)}) collective-permute-start(f32[192,1024]{1,0:T(8,128)} %get-tuple-element.190), channel_id=1, source_target_pairs={{0,24},{1,25},{2,26},{3,27},{4,28},{5,29},{6,30},{7,31}} | collective-permute-start | bytes 2359304 | tf_op jit(solution)/shard_map/ppermute | solution.py:20
  359.2 43.9 %collective-permute-start.36 = (f32[192,1024]{1,0:T(8,128)S(1)}, f32[192,1024]{1,0:T(8,128)S(1)}, u32[]{:S(2)}, u32[]{:S(2)}) collective-permute-start(f32[192,1024]{1,0:T(8,128)S(1)} %copy-done.14), channel_id=1, source_target_pairs={{8,0},{16,8},{24,16},{9,1},{17,9},{25,17},{10,2},{18,10},{26,18},{... | collective-permute-start | bytes 2359304 | tf_op jit(solution)/shard_map/ppermute | solution.py:20
  361.4 41.7 %collective-permute-start.37 = (f32[192,1024]{1,0:T(8,128)S(1)}, f32[192,1024]{1,0:T(8,128)S(1)}, u32[]{:S(2)}, u32[]{:S(2)}) collective-permute-start(f32[192,1024]{1,0:T(8,128)S(1)} %copy-done.14), channel_id=1, source_target_pairs={{16,0},{24,8},{17,1},{25,9},{18,2},{26,10},{19,3},{27,11},{20,4},{... | collective-permute-start | bytes 2359304 | tf_op jit(solution)/shard_map/ppermute | solution.py:20
  362.7 40.4 %collective-permute-start.38 = (f32[192,1024]{1,0:T(8,128)S(1)}, f32[192,1024]{1,0:T(8,128)S(1)}, u32[]{:S(2)}, u32[]{:S(2)}) collective-permute-start(f32[192,1024]{1,0:T(8,128)S(1)} %copy-done.14), channel_id=1, source_target_pairs={{24,0},{25,1},{26,2},{27,3},{28,4},{29,5},{30,6},{31,7}} | collective-permute-start | bytes 2359304 | tf_op jit(solution)/shard_map/ppermute | solution.py:20
  404.2 21.6 %collective-permute-start.41 = (f32[192,1024]{1,0:T(8,128)}, f32[192,1024]{1,0:T(8,128)S(1)}, u32[]{:S(2)}, u32[]{:S(2)}) collective-permute-start(f32[192,1024]{1,0:T(8,128)} %all-reduce.11.cloned.1.call-done.refs_0_), channel_id=1, source_target_pairs={{24,0},{25,1},{26,2},{27,3},{28,4},{29,5},{30,6},{31,7}} | collective-permute-start | bytes 2359304 | tf_op jit(solution)/shard_map/ppermute | solution.py:20
  404.9 37.9 %collective-permute-start.40 = (f32[192,1024]{1,0:T(8,128)}, f32[192,1024]{1,0:T(8,128)S(1)}, u32[]{:S(2)}, u32[]{:S(2)}) collective-permute-start(f32[192,1024]{1,0:T(8,128)} %all-reduce.11.cloned.1.call-done.refs_0_), channel_id=1, source_target_pairs={{16,0},{24,8},{17,1},{25,9},{18,2},{26,10},{19,3},{27,11},{20,4},{... | collective-permute-start | bytes 2359304 | tf_op jit(solution)/shard_map/ppermute | solution.py:20
  406.2 36.6 %collective-permute-start.39 = (f32[192,1024]{1,0:T(8,128)}, f32[192,1024]{1,0:T(8,128)S(1)}, u32[]{:S(2)}, u32[]{:S(2)}) collective-permute-start(f32[192,1024]{1,0:T(8,128)} %all-reduce.11.cloned.1.call-done.refs_0_), channel_id=1, source_target_pairs={{8,0},{16,8},{24,16},{9,1},{17,9},{25,17},{10,2},{18,10},{26,18},{... | collective-permute-start | bytes 2359304 | tf_op jit(solution)/shard_map/ppermute | solution.py:20
  454.3 12.0 %collective-permute-start.42 = (f32[1024,1024]{1,0:T(8,128)}, f32[1024,1024]{1,0:T(8,128)}, u32[]{:S(2)}, u32[]{:S(2)}) collective-permute-start(f32[1024,1024]{1,0:T(8,128)} %shard_map.69), channel_id=1, source_target_pairs={{0,1},{1,0},{2,3},{3,2},{4,5},{5,4},{6,7},{7,6},{8,9},{9,8},{10,11... | collective-permute-start | bytes 12582920 | tf_op jit(solution)/shard_map/ppermute | solution.py:24
  (19 other events, 94.1 us)
Sparse Core Ops, SparseCore 0:
  186.2 43.8 all-reduce.4
  243.0 47.3 all-reduce.6
  311.2 43.7 all-reduce.8
  359.3 43.6 all-reduce.10
